TPU v7x, 32 devices: a whole 2x2x4 slice. The times are simulated.
32 devices in a mesh: rep: 2 (over core), sq: 16 (over z, y, x).
Axes of the slice: x: 2, y: 2, z: 4, core: 2. Of those that a mesh axis runs over, the one named last changes fastest.
Arguments:
- inputs: bfloat16 [4, 1024, 768], P('rep', 'sq'), may hold values from -6 to 6
- w_query: bfloat16 [768, 768], P('sq'), may hold values from -0.21875 to 0.21875
- w_key: bfloat16 [768, 768], P('sq'), may hold values from -0.21875 to 0.21875
- w_value: bfloat16 [768, 768], P('sq'), may hold values from -0.21875 to 0.21875
- w_out: bfloat16 [768, 768], P('sq'), may hold values from -1.75 to 1.75
- table: bfloat16 [32, 12], P('sq'), may hold values from -4 to 4
- gain_one: bfloat16 [768], P('sq'), may hold values from 0.5 to 1.5
- gain_two: bfloat16 [768], P('sq'), may hold values from 0.5 to 1.5
- w_router: bfloat16 [768, 8], P('sq'), may hold values from -0.109375 to 0.109375
- w_up: bfloat16 [768, 24576], P(None, 'sq'), may hold values from -0.21875 to 0.21875
- w_down: bfloat16 [24576, 768], P('sq'), may hold values from -1.25 to 1.25
- routes: int32 [4, 1024, 1], P('rep', 'sq'), may hold values from 0 to 7; in each aligned block of 64 rows (0 to 63, 64 to 127, ..., all dimensions but the last counted through in order) at most 16 rows name the same one
- segments: int32 [4, 1024], P('rep', 'sq'), may hold values from 0 to 1, as said below
- cotangent: bfloat16 [4, 1024, 768], P('rep', 'sq'), may hold values from -6 to 6
Outputs:
- output: bfloat16 [4, 1024, 768], P('rep', 'sq')
- input_grad: float32 [4, 1024, 768], P('rep', 'sq')
- query_grad: float32 [768, 768], P('sq')
- key_grad: float32 [768, 768], P('sq')
- value_grad: float32 [768, 768], P('sq')
- out_grad: float32 [768, 768], P('sq')
- table_grad: float32 [32, 12], P('sq')
- gain_one_grad: float32 [768], P('sq')
- gain_two_grad: float32 [768], P('sq')
- router_grad: float32 [768, 8], P('sq')
- up_grad: float32 [768, 24576], P(None, 'sq')
- down_grad: float32 [24576, 768], P('sq')
Inputs may be any that keep to these rules, and one draw needn't show every extreme that they name: `routes`: in each aligned block of 64 rows (one sequence's positions on one device), at most 16 tokens name the same expert. `segments`: segment numbers count a sequence's documents from 0 and never fall along it. Of sequences 2 k and 2 k + 1, one is a single document and the other holds 2 documents.
All inputs are finite; a program needn't handle non-finite values.
Results may differ from a plain program's by a relative error of at most 0.03.
Values may be sent and summed in bfloat16 or wider, within the bound.
No kernel may reach another device: no remote copies, remote signals or barrier semaphores. Data moves between devices by JAX's collectives and lax.ppermute only.
A program may use at most 192 MiB of HBM per device.

v0:
```python
from functools import partial

import jax
import jax.numpy as jnp
from jax import lax
from jax.experimental import pallas as pl
from jax.experimental.pallas import tpu as pltpu
from jax.sharding import PartitionSpec as P

EXPERTS = 8
CAP = 32
HEAD_GROUPS = 4
EPS = 1e-06
NEGATIVE = -1e30
LIMITS = (1, 2, 3, 4, 5, 6, 7, 8, 12, 16, 23, 32, 46, 64, 91)
LANES = 128
f32 = jnp.float32
bf16 = jnp.bfloat16


def dot(a, b, dims=((1,), (0,))):
    return lax.dot_general(a, b, (dims, ((), ())), preferred_element_type=f32)


def relative_tile(offset, shape, rows, sub):
    row = lax.broadcasted_iota(jnp.int32, shape, 0)
    col = lax.broadcasted_iota(jnp.int32, shape, 1)
    return col - LANES - (rows * (row // sub) + offset + row % sub)


def forward_kernel(
    place_ref,
    own_ref,
    other_ref,
    attended_ref,
    probs_ref,
    query_ref,
    pair_ref,
    normed_all,
    weight_ref,
    gain_one_ref,
    gain_two_ref,
    router_ref,
    weights,
    project,
    scores,
    strip,
    seg_key_ref,
    seg_query_ref,
    table_ref,
    *,
    groups,
    half,
    rows,
    sub,
    head_dim,
    shard,
    all_heads,
):
    core_at = pl.multiple_of(place_ref[0], half)
    other_at = pl.multiple_of(half - place_ref[0], half)
    query_at = pl.multiple_of(place_ref[1], sub)
    width = gain_one_ref.shape[1]
    length = groups * rows
    heads = attended_ref.shape[1] // head_dim
    head_width = heads * head_dim
    per = LANES // rows
    tile = per * sub
    steps = length // LANES
    base = 3 * head_width
    table_rows = 32 // groups
    seg_row = lax.broadcasted_iota(jnp.int32, (sub, rows), 0)
    seg_col = lax.broadcasted_iota(jnp.int32, (sub, rows), 1)
    seg_pick = seg_col == seg_row + place_ref[1]
    for p in range(groups):
        at = slice(p * shard, (p + 1) * shard)
        small = own_ref[p, half:, base:].astype(f32)
        gain_one_ref[:, at] = small[0:1, 0:shard]
        gain_two_ref[:, at] = small[1:2, 0:shard]
        router_ref[:, at] = small[2 : 2 + EXPERTS, 0:shard]
        for k in range(table_rows):
            table_ref[p * table_rows + k : p * table_rows + k + 1, :] = small[
                2 + EXPERTS : 3 + EXPERTS, k * all_heads : (k + 1) * all_heads
            ]
        seg = small[3 + EXPERTS : 4 + EXPERTS, 0:rows]
        seg_key_ref[:, p * rows : (p + 1) * rows] = seg
        seg_query_ref[p * sub : (p + 1) * sub, :] = jnp.sum(
            jnp.where(seg_pick, jnp.broadcast_to(seg, (sub, rows)), 0.0), axis=1, keepdims=True
        )
    part = shard // 2
    for c in range(2):

        @pl.when(place_ref[4] == c)
        def _():
            at = slice(c * part, (c + 1) * part)
            weights[:, at, :] = own_ref[:, half:, 0:base].astype(f32)
            at = slice((1 - c) * part, (2 - c) * part)
            weights[:, at, :] = other_ref[:, half:, 0:base].astype(f32)

    weight_ref[...] = weights[...].reshape(width, base).astype(bf16)
    gain = gain_one_ref[...]
    head_col = lax.broadcasted_iota(jnp.int32, (32, all_heads), 1)

    def norm(x):
        x = x.astype(f32)
        scale = lax.rsqrt(jnp.mean(x * x, axis=-1, keepdims=True) + EPS)
        return ((x * scale) * gain).astype(bf16)

    def norm_step(p, carry):
        normed_all[p, pl.ds(core_at, half), :] = norm(own_ref[p, 0:half, :])
        normed_all[p, pl.ds(other_at, half), :] = norm(other_ref[p, 0:half, :])
        return carry

    lax.fori_loop(0, groups, norm_step, 0)
    chunk = 4

    def project_step(c, carry):
        block = normed_all[pl.ds(c * chunk, chunk)].reshape(chunk * rows, width)
        result = dot(block, weight_ref[...]).astype(bf16)
        project[pl.ds(c * chunk, chunk)] = result.reshape(chunk, rows, 3 * head_width)
        pair_ref[pl.ds(c * chunk * rows, chunk * rows), :] = result[:, head_width:]
        return carry

    lax.fori_loop(0, groups // chunk, project_step, 0)

    def query_step(p, carry):
        query_ref[pl.ds(p * sub, sub), :] = project[p, pl.ds(query_at, sub), 0:head_width]
        return carry

    lax.fori_loop(0, groups, query_step, 0)
    factor = head_dim ** (-0.5)
    left = length - 2 * LANES
    right = length + LANES
    relative = relative_tile(place_ref[1], (tile, 3 * LANES), rows, sub)
    magnitude = jnp.abs(relative)
    for h in range(heads):
        at = h * head_dim
        mine = head_col == place_ref[2] + h
        column = jnp.sum(jnp.where(mine, table_ref[...], 0.0), axis=1, keepdims=True)
        entry = [column[b : b + 1, :] for b in range(32)]
        bias = jnp.where(relative > 0, entry[16], entry[0])
        for k, threshold in enumerate(LIMITS):
            value = jnp.where(relative > 0, entry[17 + k], entry[1 + k])
            bias = jnp.where(magnitude >= threshold, value, bias)
        strip[:, 0:left] = jnp.broadcast_to(entry[15], (tile, left))
        strip[:, left:right] = bias
        strip[:, right:] = jnp.broadcast_to(entry[31], (tile, strip.shape[1] - right))
        scores[...] = (
            dot(query_ref[:, at : at + head_dim], pair_ref[:, at : at + head_dim], ((1,), (1,)))
            * factor
        )

        def soft_step(qb, carry):
            start = pl.multiple_of(length - LANES - qb * LANES, LANES)
            for par in range(per):
                here = pl.ds(qb * tile + par * sub, sub)
                value = scores[here, :] + strip[par * sub : (par + 1) * sub, pl.ds(start, length)]
                same = seg_query_ref[here, :] == seg_key_ref[...]
                value = jnp.where(same, value, NEGATIVE)
                top = jnp.max(value, axis=-1, keepdims=True)
                value = jnp.exp(value - top)
                total = jnp.sum(value, axis=-1, keepdims=True)
                probs_ref[h, here, :] = (value * (1.0 / total)).astype(bf16)
            return carry

        lax.fori_loop(0, steps, soft_step, 0)
        attended_ref[:, at : at + head_dim] = dot(
            probs_ref[h], pair_ref[:, head_width + at : head_width + at + head_dim]
        ).astype(bf16)


def backward_kernel(
    place_ref,
    probs_ref,
    query_ref,
    pair_ref,
    grad_ref,
    d_all_ref,
    table_ref,
    scores,
    low,
    strip,
    flipped,
    d_query,
    *,
    groups,
    half,
    rows,
    sub,
    head_dim,
):
    query_at = pl.multiple_of(place_ref[1], sub)
    length = groups * rows
    head_width = query_ref.shape[1]
    heads = head_width // head_dim
    per = LANES // rows
    tile = per * sub
    steps = length // LANES
    factor = head_dim ** (-0.5)
    left = length - 2 * LANES
    right = length + LANES
    relative = relative_tile(place_ref[1], (tile, 3 * LANES), rows, sub)
    magnitude = jnp.abs(relative)
    count = jnp.zeros_like(relative)
    for threshold in LIMITS:
        count = count + (magnitude >= threshold).astype(jnp.int32)
    bucket = count + jnp.where(relative > 0, 16, 0)

    def lanes_sum(value):
        value = jnp.sum(value, axis=0, keepdims=True)
        total = value[:, 0:LANES]
        for k in range(1, value.shape[1] // LANES):
            total = total + value[:, k * LANES : (k + 1) * LANES]
        return total

    for h in range(heads):
        at = h * head_dim
        grad = grad_ref[:, at : at + head_dim]
        scores[...] = dot(
            grad, pair_ref[:, head_width + at : head_width + at + head_dim], ((1,), (1,))
        )
        strip[...] = jnp.zeros_like(strip)

        def score_step(qb, carry):
            start = pl.multiple_of(length - LANES - qb * LANES, LANES)
            for par in range(per):
                here = pl.ds(qb * tile + par * sub, sub)
                probs = probs_ref[h, here, :].astype(f32)
                value = scores[here, :]
                delta = jnp.sum(probs * value, axis=-1, keepdims=True)
                value = probs * (value - delta)
                low[here, :] = value.astype(bf16)
                strip[par * sub : (par + 1) * sub, pl.ds(start, length)] += value
            return carry

        lax.fori_loop(0, steps, score_step, 0)
        d_query[:, at : at + head_dim] = dot(low[...], pair_ref[:, at : at + head_dim]) * factor
        flipped[at : at + head_dim, :] = (
            dot(query_ref[:, at : at + head_dim], low[...], ((0,), (0,))) * factor
        )
        flipped[head_width + at : head_width + at + head_dim, :] = dot(
            grad, probs_ref[h], ((0,), (0,))
        )
        near = strip[:, left:right]
        for b in range(32):
            table_ref[h, b : b + 1, :] = lanes_sum(jnp.where(bucket == b, near, 0.0))
        table_ref[h, 15:16, :] += lanes_sum(strip[:, 0:left])
        table_ref[h, 31:32, :] += lanes_sum(strip[:, right:])
    d_all_ref[:, :, 0:head_width] = jnp.zeros((groups, rows, head_width), bf16)
    for c in range(length // LANES):
        block = flipped[:, c * LANES : (c + 1) * LANES].T.astype(bf16)
        d_all_ref[c * per : (c + 1) * per, :, head_width:] = block.reshape(
            per, rows, 2 * head_width
        )

    def place_step(p, carry):
        d_all_ref[p, pl.ds(query_at, sub), 0:head_width] = d_query[
            pl.ds(p * sub, sub), :
        ].astype(bf16)
        return carry

    lax.fori_loop(0, groups, place_step, 0)


def last_kernel(
    place_ref,
    d_own_ref,
    d_other_ref,
    weight_ref,
    normed_ref,
    own_ref,
    gain_two_ref,
    router_ref,
    table_ref,
    last_ref,
    d_sum,
    w_grad,
    gain_sum,
    small,
    *,
    groups,
    half,
    rows,
    shard,
    all_heads,
):
    core_at = pl.multiple_of(place_ref[0], half)
    width = weight_ref.shape[0]
    base = weight_ref.shape[1]
    part = shard // 2
    length = groups * rows
    d_sum[...] = (d_own_ref[...].astype(f32) + d_other_ref[...].astype(f32)).astype(bf16)
    gain_sum[...] = jnp.zeros_like(gain_sum)
    chunk = 4

    def normed_step(c, carry):
        at = pl.ds(c * chunk, chunk)
        block = d_sum[at, pl.ds(core_at, half), :].reshape(chunk * half, base)
        d_normed = dot(block, weight_ref[...], ((1,), (1,)))
        x = own_ref[at, 0:half, :].astype(f32).reshape(chunk * half, width)
        unit = x * lax.rsqrt(jnp.mean(x * x, axis=-1, keepdims=True) + EPS)
        gain_sum[...] += jnp.sum(d_normed * unit, axis=0, keepdims=True)
        last_ref[at, 0:half, :] = d_normed.reshape(chunk, half, width).astype(bf16)
        return carry

    lax.fori_loop(0, groups // chunk, normed_step, 0)
    w_grad[...] = dot(
        normed_ref[...].reshape(length, width), d_sum[...].reshape(length, base), ((0,), (0,))
    ).reshape(groups, shard, base)
    for c in range(2):

        @pl.when(place_ref[4] == c)
        def _():
            last_ref[:, half:, 0:base] = w_grad[:, c * part : (c + 1) * part, :].astype(bf16)

    heads = table_ref.shape[0]
    head_col = lax.broadcasted_iota(jnp.int32, (32, all_heads), 1)
    table = jnp.zeros((32, all_heads), f32)
    for h in range(heads):
        column = jnp.sum(table_ref[h], axis=1, keepdims=True)
        table = table + jnp.where(head_col == place_ref[2] + h, column, 0.0)
    table_rows = 32 // groups
    small[...] = jnp.zeros_like(small)
    for p in range(groups):
        at = slice(p * shard, (p + 1) * shard)
        small[p, 0:1, 0:shard] = gain_sum[:, at]
        small[p, 1:2, 0:shard] = gain_two_ref[:, at]
        small[p, 2 : 2 + EXPERTS, 0:shard] = router_ref[:, at]
        for k in range(table_rows):
            small[p, 2 + EXPERTS : 3 + EXPERTS, k * all_heads : (k + 1) * all_heads] = table[
                p * table_rows + k : p * table_rows + k + 1, :
            ]
    last_ref[:, half:, base:] = small[...].astype(bf16)


def out_grad_kernel(
    place_ref, attended_ref, other_ref, d_ref, d_other_ref, out_ref, total, *, groups, shard
):
    part = shard // 2
    width = total.shape[2]
    grad = dot(attended_ref[...], d_ref[...], ((0,), (0,)))
    grad = grad + dot(other_ref[...], d_other_ref[...], ((0,), (0,)))
    total[...] = grad.reshape(groups, shard, width)
    for c in range(2):

        @pl.when(place_ref[4] == c)
        def _():
            out_ref[...] = total[:, c * part : (c + 1) * part, :].astype(bf16)


def sum_kernel(
    place_ref, final_ref, keep_ref, give_ref, four_ref, small_ref, *, half, seqs
):
    groups, _, width = final_ref.shape
    part = four_ref.shape[1]
    base = width - small_ref.shape[1]
    head_width = base // 3
    per_seq = groups // (2 * seqs)
    split = per_seq // HEAD_GROUPS
    mine = place_ref[3]
    yours = seqs - mine
    for l in range(seqs):

        def total(first):
            value = final_ref[first, 0:half, :].astype(f32)
            for k in range(1, per_seq):
                value = value + final_ref[first + k, 0:half, :].astype(f32)
            return value

        keep_ref[l] = total((mine + l) * per_seq)
        give_ref[l] = total((yours + l) * per_seq).astype(bf16)
    for g in range(HEAD_GROUPS):
        grad = jnp.zeros((part, base), f32)
        for s in range(2 * seqs):
            for t in range(split):
                grad = grad + final_ref[(s * HEAD_GROUPS + g) * split + t, half:, 0:base].astype(
                    f32
                )
        for i in range(3):
            four_ref[i, :, g * head_width : (g + 1) * head_width] = grad[
                :, i * head_width : (i + 1) * head_width
            ]
    small = final_ref[0, half:, base:].astype(f32)
    for p in range(1, groups):
        small = small + final_ref[p, half:, base:].astype(f32)
    small_ref[...] = small


def input_kernel(
    place_ref,
    keep_ref,
    given_ref,
    four_ref,
    other_ref,
    out_mine_ref,
    out_other_ref,
    x_ref,
    d_hidden_ref,
    gain_ref,
    input_ref,
    query_ref,
    key_ref,
    value_ref,
    out_ref,
    d_normed_ref,
    *,
    half,
):
    core_at = pl.multiple_of(place_ref[0], half)
    other_at = pl.multiple_of(half - place_ref[0], half)
    seqs, rows, width = x_ref.shape
    part = four_ref.shape[1]
    d_normed_ref[:, pl.ds(core_at, half), :] = keep_ref[...]
    d_normed_ref[:, pl.ds(other_at, half), :] = given_ref[...].astype(f32)
    d_normed = d_normed_ref[...].reshape(seqs * rows, width)
    x = x_ref[...].reshape(seqs * rows, width).astype(f32)
    scale = lax.rsqrt(jnp.mean(x * x, axis=-1, keepdims=True) + EPS)
    unit = x * scale
    d_unit = d_normed * gain_ref[...]
    grad = scale * (d_unit - unit * jnp.mean(d_unit * unit, axis=-1, keepdims=True))
    input_ref[...] = (d_hidden_ref[...] + grad).reshape(seqs, rows, width)
    for c in range(2):

        @pl.when(place_ref[4] == c)
        def _():
            here = slice(c * part, (c + 1) * part)
            there = slice((1 - c) * part, (2 - c) * part)
            for i, ref in enumerate((query_ref, key_ref, value_ref)):
                ref[here, :] = four_ref[i]
                ref[there, :] = other_ref[i].astype(f32)
            out_ref[here, :] = out_mine_ref[...]
            out_ref[there, :] = out_other_ref[...]


def middle_kernel(
    place_ref,
    back_ref,
    swapped_ref,
    x_ref,
    out_ref,
    out_other_ref,
    gain_ref,
    router_ref,
    routes_ref,
    cotangent_ref,
    send_ref,
    attended_ref,
    hidden_ref,
    normed_ref,
    probs_ref,
    spread_ref,
    attended,
    *,
    half,
    sub,
    split,
    few,
    share,
):
    seqs, rows, width = attended.shape
    tokens = seqs * rows
    head_width = back_ref.shape[2]
    core_at = place_ref[0]
    first = place_ref[3]
    for l in range(seqs):
        for g in range(HEAD_GROUPS):
            lanes = slice(g * head_width, (g + 1) * head_width)
            for t in range(split):
                here = pl.multiple_of(core_at + t * sub, sub)
                there = pl.multiple_of(half - core_at + t * sub, sub)
                at = (l * HEAD_GROUPS + g) * split + t
                kept = first * (HEAD_GROUPS * split) + at
                attended[l, pl.ds(here, sub), lanes] = back_ref[kept]
                attended[l, pl.ds(there, sub), lanes] = swapped_ref[at]
    low = attended[...].reshape(tokens, width)
    attended_ref[...] = low
    out_half = width // 2
    here = pl.multiple_of(place_ref[4] * out_half, LANES)
    there = pl.multiple_of(out_half - place_ref[4] * out_half, LANES)
    hidden_ref[:, pl.ds(here, out_half)] = dot(low, out_ref[...])
    hidden_ref[:, pl.ds(there, out_half)] = dot(low, out_other_ref[...])
    hidden = x_ref[...].reshape(tokens, width).astype(f32) + hidden_ref[...]
    hidden_ref[...] = hidden
    scale = lax.rsqrt(jnp.mean(hidden * hidden, axis=-1, keepdims=True) + EPS)
    normed = ((hidden * scale) * gain_ref[...]).astype(bf16)
    normed_ref[...] = normed
    logits = dot(normed, router_ref[...].astype(bf16), ((1,), (1,)))
    logits = jnp.exp(logits - jnp.max(logits, axis=-1, keepdims=True))
    probs = logits / jnp.sum(logits, axis=-1, keepdims=True)
    probs_ref[...] = probs
    chosen = routes_ref[...]
    picked = (chosen == lax.broadcasted_iota(jnp.int32, (tokens, EXPERTS), 1)).astype(f32)
    gate = jnp.sum(probs * picked, axis=-1, keepdims=True)
    row = lax.broadcasted_iota(jnp.int32, (tokens, tokens), 0)
    col = lax.broadcasted_iota(jnp.int32, (tokens, tokens), 1)
    before = (col < row).astype(bf16)
    earlier = dot(before, picked.astype(bf16))
    slot = jnp.sum(earlier * picked, axis=-1, keepdims=True).astype(jnp.int32)
    spot = chosen * CAP + slot
    spread = (spot == lax.broadcasted_iota(jnp.int32, (tokens, EXPERTS * CAP), 1)).astype(bf16)
    spread_ref[...] = spread
    d_expert = (gate * cotangent_ref[...].reshape(tokens, width).astype(f32)).astype(bf16)
    for i, rows_in in enumerate((normed, d_expert)):
        rows_out = dot(spread, rows_in, ((0,), (0,))).astype(bf16)
        for e in range(EXPERTS):
            for k in range(share):
                send_ref[e * share + k, i * few : (i + 1) * few, :] = rows_out[
                    e * few : (e + 1) * few, :
                ]


def expert_step(received, got, up, down):
    pre = dot(received, up)
    root = 0.7978845608028654
    square = pre * pre
    bend = jnp.tanh(root * (pre + 0.044715 * (square * pre)))
    side = 0.5 * (1.0 + bend)
    act = (pre * side).astype(bf16)
    slope = side + 0.5 * pre * (1.0 - bend * bend) * (root * (1.0 + 3 * 0.044715 * square))
    d_pre = (dot(got, down, ((1,), (1,))) * slope).astype(bf16)
    return act, d_pre, dot(act, down), dot(d_pre, up, ((1,), (1,)))


def expert_kernel(
    arrived_ref,
    up_ref,
    down_ref,
    results_ref,
    received_ref,
    got_ref,
    act_ref,
    d_pre_ref,
    out_sum,
    row_sum,
    *,
    few,
):
    groups, _, width = arrived_ref.shape
    step = pl.program_id(0)

    @pl.when(step == 0)
    def _():
        out_sum[...] = jnp.zeros_like(out_sum)
        row_sum[...] = jnp.zeros_like(row_sum)
        shape = (groups * few, width)
        received_ref[...] = arrived_ref[:, 0:few, :].reshape(shape)
        got_ref[...] = arrived_ref[:, few:, :].reshape(shape)

    act, d_pre, out, rows = expert_step(
        received_ref[...], got_ref[...], up_ref[...], down_ref[...]
    )
    act_ref[...] = act
    d_pre_ref[...] = d_pre
    out_sum[...] += out
    row_sum[...] += rows

    @pl.when(step == pl.num_programs(0) - 1)
    def _():
        shape = (groups, few, width)
        results_ref[:, 0:few, :] = out_sum[...].reshape(shape).astype(bf16)
        results_ref[:, few:, :] = row_sum[...].reshape(shape).astype(bf16)


def turn_kernel(
    place_ref,
    returned_ref,
    spread_ref,
    hidden_ref,
    normed_ref,
    probs_ref,
    routes_ref,
    cotangent_ref,
    gain_ref,
    router_ref,
    out_ref,
    out_other_ref,
    output_ref,
    d_hidden_ref,
    d_branch_ref,
    keep_ref,
    give_ref,
    router_grad_ref,
    gain_grad_ref,
    d_attended,
    *,
    half,
    sub,
    split,
    few,
    share,
):
    seqs, rows, width = output_ref.shape
    tokens = seqs * rows
    head_width = keep_ref.shape[2]
    core_at = place_ref[0]
    spread = spread_ref[...]

    def collect(at):
        pieces = []
        for e in range(EXPERTS):
            piece = returned_ref[e * share, at, :].astype(f32)
            for k in range(1, share):
                piece = piece + returned_ref[e * share + k, at, :].astype(f32)
            pieces.append(piece)
        value = jnp.concatenate(pieces, axis=0)
        high = value.astype(bf16)
        low = (value - high.astype(f32)).astype(bf16)
        return dot(spread, high) + dot(spread, low)

    expert_out = collect(slice(0, few))
    d_rows = collect(slice(few, 2 * few))
    hidden = hidden_ref[...]
    probs = probs_ref[...]
    picked = (
        routes_ref[...] == lax.broadcasted_iota(jnp.int32, (tokens, EXPERTS), 1)
    ).astype(f32)
    gate = jnp.sum(probs * picked, axis=-1, keepdims=True)
    output_ref[...] = (hidden + gate * expert_out).astype(bf16).reshape(seqs, rows, width)
    d_final = cotangent_ref[...].reshape(tokens, width).astype(f32)
    d_gate = jnp.sum(d_final * expert_out, axis=-1, keepdims=True)
    d_logits = gate * (picked - probs) * d_gate
    d_normed = d_rows
    for e in range(EXPERTS):
        d_normed = d_normed + d_logits[:, e : e + 1] * router_ref[e : e + 1, :]
    router_grad_ref[...] = lax.dot_general(
        d_logits,
        normed_ref[...].astype(f32),
        (((0,), (0,)), ((), ())),
        precision=lax.Precision.HIGHEST,
        preferred_element_type=f32,
    )
    scale = lax.rsqrt(jnp.mean(hidden * hidden, axis=-1, keepdims=True) + EPS)
    unit = hidden * scale
    gain_grad_ref[...] = jnp.sum(d_normed * unit, axis=0, keepdims=True)
    d_unit = d_normed * gain_ref[...]
    d_hidden = d_final + scale * (d_unit - unit * jnp.mean(d_unit * unit, axis=-1, keepdims=True))
    d_hidden_ref[...] = d_hidden
    d_branch = d_hidden.astype(bf16)
    d_branch_ref[...] = d_branch
    out_half = width // 2
    here = pl.multiple_of(place_ref[4] * out_half, LANES)
    there = pl.multiple_of(out_half - place_ref[4] * out_half, LANES)
    d_low = dot(d_branch_ref[:, pl.ds(here, out_half)], out_ref[...], ((1,), (1,)))
    d_low = d_low + dot(d_branch_ref[:, pl.ds(there, out_half)], out_other_ref[...], ((1,), (1,)))
    d_attended[...] = d_low.astype(bf16).reshape(seqs, rows, width)
    for l in range(seqs):
        for g in range(HEAD_GROUPS):
            lanes = slice(g * head_width, (g + 1) * head_width)
            for t in range(split):
                here = pl.multiple_of(core_at + t * sub, sub)
                there = pl.multiple_of(half - core_at + t * sub, sub)
                at = (l * HEAD_GROUPS + g) * split + t
                keep_ref[at] = d_attended[l, pl.ds(here, sub), lanes]
                give_ref[at] = d_attended[l, pl.ds(there, sub), lanes]


def exchange(value):
    return lax.all_to_all(value, "sq", split_axis=0, concat_axis=0, tiled=True)


def local(
    inputs,
    w_query,
    w_key,
    w_value,
    w_out,
    table,
    gain_one,
    gain_two,
    w_router,
    w_up,
    w_down,
    routes,
    segments,
    cotangent,
):
    seqs, rows, width = inputs.shape
    heads = table.shape[1]
    head_dim = width // heads
    reps = lax.axis_size("rep")
    groups = lax.axis_size("sq")
    length = rows * groups
    tokens = seqs * rows
    share = groups // EXPERTS
    half = rows // 2
    all_seqs = 2 * seqs
    split = groups // (all_seqs * HEAD_GROUPS)
    sub = half // split
    group_heads = heads // HEAD_GROUPS
    head_width = group_heads * head_dim
    shard = w_query.shape[0]
    part = shard // 2
    bucket_rows = table.shape[0]
    core = lax.axis_index("rep") % 2
    me = lax.axis_index("sq")
    group_at = (me // split) % HEAD_GROUPS
    first = core == 0
    pairs = [(i, i ^ 1) for i in range(reps)]

    def swap(value):
        return lax.ppermute(value, "rep", pairs)

    def by_core(own, other, axis):
        return jnp.where(
            first,
            jnp.concatenate([own, other], axis=axis),
            jnp.concatenate([other, own], axis=axis),
        )

    def mine(value, axis, size):
        return lax.dynamic_slice_in_dim(value, core * size, size, axis)

    def yours(value, axis, size):
        return lax.dynamic_slice_in_dim(value, (1 - core) * size, size, axis)

    def over_pairs(value):
        if reps == 2:
            return value
        sets = [list(range(0, reps, 2)), list(range(1, reps, 2))]
        return lax.psum(value, "rep", axis_index_groups=sets)

    x_pair = by_core(mine(inputs, 1, half), swap(yours(inputs, 1, half)), 0)
    seg_low = segments.astype(bf16)
    seg_pair = by_core(seg_low, swap(seg_low), 0)
    w_three = jnp.stack([mine(w, 0, part) for w in (w_query, w_key, w_value)], axis=1)
    w_three = w_three.reshape(part, 3, HEAD_GROUPS, head_width)
    w_send = jnp.transpose(w_three, (2, 0, 1, 3)).reshape(HEAD_GROUPS, part, 3 * head_width)
    spare = width - 3 * head_width

    def widen(value):
        return jnp.pad(value, ((0, 0), (0, spare - value.shape[1])))

    small = jnp.concatenate(
        [
            widen(gain_one[None]),
            widen(gain_two[None]),
            widen(w_router.T),
            widen(table.reshape(1, -1)),
        ],
        axis=0,
    )
    small = jnp.broadcast_to(small[None], (all_seqs,) + small.shape)
    small = jnp.concatenate(
        [small, jnp.pad(seg_pair, ((0, 0), (0, spare - rows)))[:, None, :]], axis=1
    )
    small = jnp.pad(small, ((0, 0), (0, part - small.shape[1]), (0, 0)))

    shape = (all_seqs, HEAD_GROUPS, split)
    lower = jnp.concatenate(
        [
            jnp.broadcast_to(w_send[None, :, None], shape + w_send.shape[1:]),
            jnp.broadcast_to(small[:, None, None], shape + small.shape[1:]),
        ],
        axis=-1,
    )
    send = jnp.concatenate(
        [jnp.broadcast_to(x_pair[:, None, None], shape + x_pair.shape[1:]), lower], axis=3
    ).reshape(groups, half + part, width)
    own = exchange(send)
    own, out_half = lax.optimization_barrier((own, mine(w_out, 1, width // 2)))
    other, out_half = lax.optimization_barrier((swap(own), out_half))
    out_mine = exchange(jnp.broadcast_to(out_half[None], (groups, shard, width // 2)))
    query_at = core * half + (me % split) * sub
    place = jnp.stack([core * half, query_at, group_at * group_heads, core * seqs, core])
    place = place.astype(jnp.int32)
    shard_table = bucket_rows * heads
    queries_count = groups * sub
    tile = (LANES // rows) * sub
    sizes = dict(groups=groups, half=half, rows=rows, sub=sub, head_dim=head_dim)
    smem = pl.BlockSpec(memory_space=pltpu.SMEM)
    vmem = pl.BlockSpec(memory_space=pltpu.VMEM)

    def cost(microseconds):
        return pl.CostEstimate(
            flops=microseconds * 900_000_000,
            bytes_accessed=microseconds * 1_000_000,
            transcendentals=0,
        )

    limit = pltpu.CompilerParams(vmem_limit_bytes=56 * 1024 * 1024)
    (
        attended_part,
        probs,
        queries,
        pair,
        normed_all,
        w_group,
        gain_one_full,
        gain_two_full,
        router_full,
    ) = pl.pallas_call(
        partial(forward_kernel, shard=shard, all_heads=heads, **sizes),
        name="attention_forward",
        out_shape=(
            jax.ShapeDtypeStruct((queries_count, head_width), bf16),
            jax.ShapeDtypeStruct((group_heads, queries_count, length), bf16),
            jax.ShapeDtypeStruct((queries_count, head_width), bf16),
            jax.ShapeDtypeStruct((length, 2 * head_width), bf16),
            jax.ShapeDtypeStruct((groups, rows, width), bf16),
            jax.ShapeDtypeStruct((width, 3 * head_width), bf16),
            jax.ShapeDtypeStruct((1, width), f32),
            jax.ShapeDtypeStruct((1, width), f32),
            jax.ShapeDtypeStruct((EXPERTS, width), f32),
        ),
        in_specs=[smem] + [vmem] * 2,
        out_specs=[vmem] * 9,
        scratch_shapes=[
            pltpu.VMEM((groups, shard, 3 * head_width), f32),
            pltpu.VMEM((groups, rows, 3 * head_width), bf16),
            pltpu.VMEM((queries_count, length), f32),
            pltpu.VMEM((tile, 2 * length - LANES), f32),
            pltpu.VMEM((1, length), f32),
            pltpu.VMEM((queries_count, 1), f32),
            pltpu.VMEM((32, heads), f32),
        ],
        compiler_params=limit,
        cost_estimate=cost(60),
    )(place, own, other)
    attended_part, out_mine = lax.optimization_barrier((attended_part, out_mine))
    back = exchange(attended_part.reshape(groups, sub, head_width))
    out_mine = out_mine.reshape(width, width // 2)
    out_yours = swap(out_mine)
    back_given = swap(yours(back, 0, groups // 2))
    few = CAP
    routes_flat = routes.reshape(tokens, 1)
    pieces = dict(half=half, sub=sub, split=split, few=few)
    buffer, attended, hidden, normed_two, router_probs, spread = pl.pallas_call(
        partial(middle_kernel, share=share, **pieces),
        name="router_and_dispatch",
        out_shape=(
            jax.ShapeDtypeStruct((groups, 2 * few, width), bf16),
            jax.ShapeDtypeStruct((tokens, width), bf16),
            jax.ShapeDtypeStruct((tokens, width), f32),
            jax.ShapeDtypeStruct((tokens, width), bf16),
            jax.ShapeDtypeStruct((tokens, EXPERTS), f32),
            jax.ShapeDtypeStruct((tokens, EXPERTS * CAP), bf16),
        ),
        in_specs=[smem] + [vmem] * 9,
        out_specs=[vmem] * 6,
        scratch_shapes=[pltpu.VMEM((seqs, rows, width), bf16)],
        compiler_params=limit,
        cost_estimate=cost(5),
    )(
        place,
        back,
        back_given,
        inputs,
        out_mine,
        out_yours,
        gain_two_full,
        router_full,
        routes_flat,
        cotangent,
    )
    arrived = exchange(buffer)
    expert_rows = groups * few
    hidden_units = w_up.shape[1]
    chunk = hidden_units // 3 if hidden_units % (3 * LANES) == 0 else hidden_units
    whole = [
        pl.BlockSpec((groups, 2 * few, width), lambda i: (0, 0, 0)),
        pl.BlockSpec((expert_rows, width), lambda i: (0, 0)),
        pl.BlockSpec((expert_rows, chunk), lambda i: (0, i)),
    ]
    rows_low = jax.ShapeDtypeStruct((expert_rows, width), bf16)
    units_low = jax.ShapeDtypeStruct((expert_rows, hidden_units), bf16)
    results, received, got, act, d_pre = pl.pallas_call(
        partial(expert_kernel, few=few),
        name="experts",
        grid=(hidden_units // chunk,),
        out_shape=(
            jax.ShapeDtypeStruct((groups, 2 * few, width), bf16),
            rows_low,
            rows_low,
            units_low,
            units_low,
        ),
        in_specs=[
            whole[0],
            pl.BlockSpec((width, chunk), lambda i: (0, i)),
            pl.BlockSpec((chunk, width), lambda i: (i, 0)),
        ],
        out_specs=[whole[0]] + [whole[1]] * 2 + [whole[2]] * 2,
        scratch_shapes=[pltpu.VMEM((expert_rows, width), f32)] * 2,
        compiler_params=limit,
        cost_estimate=cost(8),
    )(arrived, w_up, w_down)
    returned = exchange(results)
    up_local = dot(received, d_pre, ((0,), (0,))).astype(bf16)
    down_local = dot(act, got, ((0,), (0,))).astype(bf16)
    returned, up_local, down_local = lax.optimization_barrier((returned, up_local, down_local))

    def both_reps(value):
        if reps == 2:
            return value.astype(f32) + swap(value).astype(f32)
        return lax.psum(value, "rep").astype(f32)

    output, d_hidden, d_branch, keep, give, router_grad, gain_two_grad = pl.pallas_call(
        partial(turn_kernel, share=share, **pieces),
        name="combine_and_turn",
        out_shape=(
            jax.ShapeDtypeStruct((seqs, rows, width), bf16),
            jax.ShapeDtypeStruct((tokens, width), f32),
            jax.ShapeDtypeStruct((tokens, width), bf16),
            jax.ShapeDtypeStruct((groups // 2, sub, head_width), bf16),
            jax.ShapeDtypeStruct((groups // 2, sub, head_width), bf16),
            jax.ShapeDtypeStruct((EXPERTS, width), f32),
            jax.ShapeDtypeStruct((1, width), f32),
        ),
        in_specs=[smem] + [vmem] * 11,
        out_specs=[vmem] * 7,
        scratch_shapes=[pltpu.VMEM((seqs, rows, width), bf16)],
        compiler_params=limit,
        cost_estimate=cost(5),
    )(
        place,
        returned,
        spread,
        hidden,
        normed_two,
        router_probs,
        routes_flat,
        cotangent,
        gain_two_full,
        router_full,
        out_mine,
        out_yours,
    )
    grads = exchange(by_core(keep, swap(give), 0))
    out_send = pl.pallas_call(
        partial(out_grad_kernel, groups=groups, shard=shard),
        name="out_grad",
        out_shape=jax.ShapeDtypeStruct((groups, part, width), bf16),
        in_specs=[smem] + [vmem] * 4,
        out_specs=vmem,
        scratch_shapes=[pltpu.VMEM((groups, shard, width), f32)],
        compiler_params=limit,
        cost_estimate=cost(3),
    )(place, attended, swap(attended), d_branch, swap(d_branch))
    grads, out_send = lax.optimization_barrier((grads, out_send))
    grads = grads.reshape(queries_count, head_width)
    out_back = exchange(out_send)
    d_all, table_part = pl.pallas_call(
        partial(backward_kernel, **sizes),
        name="attention_backward",
        out_shape=(
            jax.ShapeDtypeStruct((groups, rows, 3 * head_width), bf16),
            jax.ShapeDtypeStruct((group_heads, groups * bucket_rows, LANES), f32),
        ),
        in_specs=[smem] + [vmem] * 4,
        out_specs=[vmem] * 2,
        scratch_shapes=[
            pltpu.VMEM((queries_count, length), f32),
            pltpu.VMEM((queries_count, length), bf16),
            pltpu.VMEM((tile, 2 * length - LANES), f32),
            pltpu.VMEM((2 * head_width, length), f32),
            pltpu.VMEM((queries_count, head_width), f32),
        ],
        compiler_params=limit,
        cost_estimate=cost(1),
    )(place, probs, queries, pair, grads)
    out_sum = jnp.sum(out_back.astype(f32), axis=0)
    out_sum = over_pairs(out_sum)
    out_other = swap(out_sum)
    last = pl.pallas_call(
        partial(last_kernel, groups=groups, half=half, rows=rows, shard=shard, all_heads=heads),
        name="input_side",
        out_shape=jax.ShapeDtypeStruct((groups, half + part, width), bf16),
        in_specs=[smem] + [vmem] * 8,
        out_specs=vmem,
        scratch_shapes=[
            pltpu.VMEM((groups, rows, 3 * head_width), bf16),
            pltpu.VMEM((groups, shard, 3 * head_width), f32),
            pltpu.VMEM((1, width), f32),
            pltpu.VMEM((groups, part, spare), f32),
        ],
        compiler_params=limit,
        cost_estimate=cost(1),
    )(
        place,
        d_all,
        swap(d_all),
        w_group,
        normed_all,
        own,
        gain_two_grad,
        router_grad,
        table_part,
    )
    last, out_other = lax.optimization_barrier((last, out_other))
    final = exchange(last)
    up_grad = both_reps(up_local)
    down_grad = both_reps(down_local)
    final, up_grad, down_grad = lax.optimization_barrier((final, up_grad, down_grad))
    keep, give, four, small_sum = pl.pallas_call(
        partial(sum_kernel, half=half, seqs=seqs),
        name="sums",
        out_shape=(
            jax.ShapeDtypeStruct((seqs, half, width), f32),
            jax.ShapeDtypeStruct((seqs, half, width), bf16),
            jax.ShapeDtypeStruct((3, part, width), f32),
            jax.ShapeDtypeStruct((part, spare), f32),
        ),
        in_specs=[smem] + [vmem],
        out_specs=[vmem] * 4,
        compiler_params=limit,
        cost_estimate=cost(2),
    )(place, final)
    four = over_pairs(four)
    small_sum = over_pairs(small_sum)
    small_sum = small_sum + swap(small_sum)
    input_grad, query_grad, key_grad, value_grad, out_grad = pl.pallas_call(
        partial(input_kernel, half=half),
        name="input_grad",
        out_shape=(jax.ShapeDtypeStruct((seqs, rows, width), f32),)
        + (jax.ShapeDtypeStruct((shard, width), f32),) * 4,
        in_specs=[smem] + [vmem] * 9,
        out_specs=[vmem] * 5,
        scratch_shapes=[pltpu.VMEM((seqs, rows, width), f32)],
        compiler_params=limit,
        cost_estimate=cost(2),
    )(
        place,
        keep,
        swap(give),
        four,
        swap(four.astype(bf16)),
        out_sum,
        out_other,
        inputs,
        d_hidden,
        gain_one_full,
    )
    return (
        output,
        input_grad,
        query_grad,
        key_grad,
        value_grad,
        out_grad,
        small_sum[2 + EXPERTS, :shard_table].reshape(bucket_rows, heads),
        small_sum[0, :shard],
        small_sum[1, :shard],
        small_sum[2 : 2 + EXPERTS, :shard].T,
        up_grad,
        down_grad,
    )


def solution(mesh):
    in_specs = (
        P("rep", "sq", None),
        P("sq", None),
        P("sq", None),
        P("sq", None),
        P("sq", None),
        P("sq", None),
        P("sq"),
        P("sq"),
        P("sq", None),
        P(None, "sq"),
        P("sq", None),
        P("rep", "sq", None),
        P("rep", "sq"),
        P("rep", "sq", None),
    )
    out_specs = (
        P("rep", "sq", None),
        P("rep", "sq", None),
        P("sq", None),
        P("sq", None),
        P("sq", None),
        P("sq", None),
        P("sq", None),
        P("sq"),
        P("sq"),
        P("sq", None),
        P(None, "sq"),
        P("sq", None),
    )
    return jax.shard_map(local, mesh=mesh, in_specs=in_specs, out_specs=out_specs, check_vma=False)
```

profile of v0, /device:TPU:0, one launch (start us, length us, event | category | flops | bytes accessed | tf_op | source)
XLA Modules:
  0.0 294.5 jit_solution(7656984241266115119)
XLA Ops:
  0.7 0.7 convert_element_type.38
  1.4 0.5 collective-permute-start.1
  1.8 1.0 constant_dynamic-slice_fusion.6
  2.8 0.1 collective-permute-start
  2.9 0.7 reshape.88
  3.6 0.8 constant_dynamic-slice_fusion.2
  4.4 0.1 stack.35
  4.5 0.1 stack.34
  4.7 0.1 stack.33
  4.8 0.1 maximum_bitcast_fusion
  4.9 0.7 fusion.10
  5.7 0.1 copy.29
  5.8 0.2 broadcast_in_dim.19
  6.3 1.2 maximum_maximum_fusion
  7.5 8.3 %all-to-all-start = ((bf16[16,56,768]{2,1,0:T(8,128)(2,1)}), bf16[16,56,768]{2,1,0:T(8,128)(2,1)S(1)}, u32[]{:S(2)}, u32[]{:S(2)}) async-start(bf16[16,56,768]{2,1,0:T(8,128)(2,1)} %bitcast.9), calls=%async_computation | async-start | bytes 2752512 | tf_op jit(solution)/shard_map/all_to_all | solution.py:658
  15.9 30.7 %all-to-all-done.own_ref = bf16[16,56,768]{2,1,0:T(8,128)(2,1)S(1)} async-done(((bf16[16,56,768]{2,1,0:T(8,128)(2,1)}), bf16[16,56,768]{2,1,0:T(8,128)(2,1)S(1)}, u32[]{:S(2)}, u32[]{:S(2)}) %all-to-all-start) | async-done | bytes 1376288 | tf_op jit(solution)/shard_map/all_to_all | solution.py:658
  46.6 0.7 stack.32.place_ref
  47.3 2.4 collective-permute-done.2.other_ref
  49.7 0.9 broadcast_in_dim.48
  50.7 7.2 %all-to-all-start.1 = ((bf16[16,48,384]{2,1,0:T(8,128)(2,1)}), bf16[16,48,384]{2,1,0:T(8,128)(2,1)S(1)}, u32[]{:S(2)}, u32[]{:S(2)}) async-start(bf16[16,48,384]{2,1,0:T(8,128)(2,1)} %broadcast_in_dim.48), calls=%async_computation.1 | async-start | bytes 1179648 | tf_op jit(solution)/shard_map/all_to_all | solution.py:658
  57.9 19.5 %attention_forward.1 = (bf16[512,192]{1,0:T(8,128)(2,1)}, bf16[3,512,1024]{2,1,0:T(8,128)(2,1)}, bf16[512,192]{1,0:T(8,128)(2,1)}, bf16[1024,384]{1,0:T(8,128)(2...) custom-call(s32[5]{0:T(128)} %stack.32.place_ref, ...), custom_call_target="tpu_custom_call" | custom-call | flops 54000001024 | bytes 60000000 | tf_op jit(solution)/shard_map/attention_forward/pallas_call | solution.py:791
  77.5 6.9 %all-to-all-start.2 = ((bf16[16,32,192]{2,1,0:T(8,128)(2,1)}), bf16[16,32,192]{2,1,0:T(8,128)(2,1)S(1)}, u32[]{:S(2)}, u32[]{:S(2)}) async-start(bf16[16,32,192]{2,1,0:T(8,128)(2,1)} %bitcast.30), calls=%async_computation.2 | async-start | bytes 524288 | tf_op jit(solution)/shard_map/all_to_all | solution.py:658
  84.4 10.5 %all-to-all-done.2.back_ref = bf16[16,32,192]{2,1,0:T(8,128)(2,1)S(1)} async-done(((bf16[16,32,192]{2,1,0:T(8,128)(2,1)}), bf16[16,32,192]{2,1,0:T(8,128)(2,1)S(1)}, u32[]{:S(2)}, u32[]{:S(2)}) %all-to-all-start.2) | async-done | bytes 196640 | tf_op jit(solution)/shard_map/all_to_all | solution.py:658
  95.0 0.5 broadcast.52
  95.5 0.7 reduce.7
  96.2 0.8 reshape.94.routes_ref
  97.0 0.6 copy-done.13
  97.6 0.2 copy-done.9
  97.9 4.1 %router_and_dispatch.1 = (bf16[16,64,768]{2,1,0:T(8,128)(2,1)}, bf16[128,768]{1,0:T(8,128)(2,1)}, f32[128,768]{1,0:T(8,128)}, bf16[128,768]{1,0:T(8,128)(2,1)}, ...) custom-call(s32[5]{0:T(128)} %stack.32.place_ref, bf16[16,32,192]{2,1,0:T(8,128)(2,1)} %copy-done.4, ...), custom_call_target="tpu_custom_call" | custom-call | flops 4499999744 | bytes 5000000 | tf_op jit(solution)/shard_map/router_and_dispatch/pallas_call | solution.py:827
  101.9 42.4 %all_to_all.40.arrived_ref = bf16[16,64,768]{2,1,0:T(8,128)(2,1)} all-to-all(bf16[16,64,768]{2,1,0:T(8,128)(2,1)} %get-tuple-element.75), channel_id=1, replica_groups=mesh['rep'=2,'sq'=16] {'sq'}, dimensions={0} | all-to-all | bytes 3145728 | tf_op jit(solution)/shard_map/all_to_all | solution.py:658
  144.3 10.4 %experts.1 = (bf16[16,64,768]{2,1,0:T(8,128)(2,1)}, bf16[512,768]{1,0:T(8,128)(2,1)}, bf16[512,768]{1,0:T(8,128)(2,1)}, bf16[512,1536]{1,0:T(8,128)(2,1)}, bf16[512,1536]{1,0:T(8,128)(2,1)}) custom-call(bf16[16,64,768]{2,1,0:T(8,128)(2,1)} %all_to_all.40.arrived_ref, bf16[768,1536]{1,0:T(8,128)(2,1)} %up_ref.1, bf16[1536,768]{1,0:T(8,128)(2,1)} %down_ref.1), custom_call_target="tpu_custom_call" | custom-call | flops 7200000000 | bytes 8000000 | tf_op jit(solution)/shard_map/experts/pallas_call | solution.py:866
  154.7 4.8 %all-to-all-start.4 = ((bf16[16,64,768]{2,1,0:T(8,128)(2,1)}), bf16[16,64,768]{2,1,0:T(8,128)(2,1)}, u32[]{:S(2)}, u32[]{:S(2)}) async-start(bf16[16,64,768]{2,1,0:T(8,128)(2,1)} %get-tuple-element.76), calls=%async_computation.4 | async-start | bytes 3145728 | tf_op jit(solution)/shard_map/all_to_all | solution.py:658
  159.6 2.9 convolution_convert_fusion.1
  162.4 1.4 convolution_convert_fusion
  163.9 29.6 %all-to-all-done.4.returned_ref = bf16[16,64,768]{2,1,0:T(8,128)(2,1)} async-done(((bf16[16,64,768]{2,1,0:T(8,128)(2,1)}), bf16[16,64,768]{2,1,0:T(8,128)(2,1)}, u32[]{:S(2)}, u32[]{:S(2)}) %all-to-all-start.4) | async-done | bytes 1572896 | tf_op jit(solution)/shard_map/all_to_all | solution.py:658
  193.5 4.6 %combine_and_turn.1 = (bf16[2,64,768]{2,1,0:T(8,128)(2,1)}, f32[128,768]{1,0:T(8,128)}, bf16[128,768]{1,0:T(8,128)(2,1)}, bf16[8,32,192]{2,1,0:T(8,128)(2,1)}, b...) custom-call(s32[5]{0:T(128)} %stack.32.place_ref, ...), custom_call_target="tpu_custom_call" | custom-call | flops 4499999744 | bytes 5000000 | tf_op jit(solution)/shard_map/combine_and_turn/pallas_call | solution.py:897
  198.0 0.5 collective-permute-start.6
  198.6 1.0 collective-permute-done.5
  199.6 1.8 maximum_select_fusion
  201.4 7.2 %all-to-all-start.5 = ((bf16[16,32,192]{2,1,0:T(8,128)(2,1)}), bf16[16,32,192]{2,1,0:T(8,128)(2,1)S(1)}, u32[]{:S(2)}, u32[]{:S(2)}) async-start(bf16[16,32,192]{2,1,0:T(8,128)(2,1)} %maximum_select_fusion), calls=%async_computation.5 | async-start | bytes 524288 | tf_op jit(solution)/shard_map/all_to_all | solution.py:658
  208.7 0.7 copy-done.11
  209.3 0.7 copy-done.12
  210.0 2.9 out_grad.1
  212.9 5.9 %all-to-all-done.5 = bf16[16,32,192]{2,1,0:T(8,128)(2,1)S(1)} async-done(((bf16[16,32,192]{2,1,0:T(8,128)(2,1)}), bf16[16,32,192]{2,1,0:T(8,128)(2,1)S(1)}, u32[]{:S(2)}, u32[]{:S(2)}) %all-to-all-start.5) | async-done | bytes 196640 | tf_op jit(solution)/shard_map/all_to_all | solution.py:658
  218.8 3.6 %all-to-all-start.6 = ((bf16[16,24,768]{2,1,0:T(8,128)(2,1)}), bf16[16,24,768]{2,1,0:T(8,128)(2,1)S(1)}, u32[]{:S(2)}, u32[]{:S(2)}) async-start(bf16[16,24,768]{2,1,0:T(8,128)(2,1)} %out_grad.1), calls=%async_computation.6 | async-start | bytes 1179648 | tf_op jit(solution)/shard_map/all_to_all | solution.py:658
  222.4 11.7 %attention_backward.1 = (bf16[16,64,576]{2,1,0:T(8,128)(2,1)}, f32[3,32,128]{2,1,0:T(8,128)}) custom-call(s32[5]{0:T(128)} %stack.32.place_ref, bf16[3,512,1024]{2,1,0:T(8,128)(2,1)} %get-tuple-element.87.probs_ref, bf16[512,192]{1,0:T(8,128)(2,1)} %get-tuple-element.88.query_ref, bf16[1024,384]{1,0:T(8,128)(2,1)} %get-tuple-element.89.pair_ref, ...), custom_call_target="tpu_custom_call" | custom-call | flops 900000000 | bytes 1000000 | tf_op jit(solution)/shard_map/attention_backward/pallas_call | solution.py:942
  234.1 0.5 collective-permute-start.11
  234.6 3.6 %all-to-all-done.6 = bf16[16,24,768]{2,1,0:T(8,128)(2,1)S(1)} async-done(((bf16[16,24,768]{2,1,0:T(8,128)(2,1)}), bf16[16,24,768]{2,1,0:T(8,128)(2,1)S(1)}, u32[]{:S(2)}, u32[]{:S(2)}) %all-to-all-start.6) | async-done | bytes 589856 | tf_op jit(solution)/shard_map/all_to_all | solution.py:658
  238.2 0.1 convert_reduce_fusion.out_mine_ref
  238.3 0.9 collective-permute-done.8.d_other_ref
  239.3 7.8 %input_side.1 = bf16[16,56,768]{2,1,0:T(8,128)(2,1)} custom-call(s32[5]{0:T(128)} %stack.32.place_ref, bf16[16,64,576]{2,1,0:T(8,128)(2,1)} %get-tuple-element.95.d_own_ref, bf16[16,64,576]{2,1,0:T(8,128)(2,1)} %collective-permute-done.8.d_other_ref, bf16[768,576]{1,0:T(8,128)(2,1)} %get-tuple-element.96.weight_ref, ...), custom_call_target="tpu_custom_call" | custom-call | flops 900000000 | bytes 1000000 | tf_op jit(solution)/shard_map/input_side/pallas_call | solution.py:964
  247.2 6.9 %all-to-all-start.7 = ((bf16[16,56,768]{2,1,0:T(8,128)(2,1)}), bf16[16,56,768]{2,1,0:T(8,128)(2,1)}, u32[]{:S(2)}, u32[]{:S(2)}) async-start(bf16[16,56,768]{2,1,0:T(8,128)(2,1)} %input_side.1), calls=%async_computation.7 | async-start | bytes 2752512 | tf_op jit(solution)/shard_map/all_to_all | solution.py:658
  254.1 5.2 %convert_add_fusion.1 = f32[768,1536]{1,0:T(8,128)} fusion(bf16[768,1536]{1,0:T(8,128)(2,1)} %collective-permute-done.10, bf16[768,1536]{1,0:T(8,128)(2,1)} %convolution_convert_fusion.1), kind=kLoop, calls=%fused_computation.1 | loop fusion | flops 3538944 | bytes 9437184 | tf_op jit(solution)/shard_map/add | solution.py:894
  259.4 4.5 %convert_add_fusion = f32[1536,768]{1,0:T(8,128)} fusion(bf16[1536,768]{1,0:T(8,128)(2,1)} %collective-permute-done.11, bf16[1536,768]{1,0:T(8,128)(2,1)S(1)} %convolution_convert_fusion), kind=kLoop, calls=%fused_computation | loop fusion | flops 3538944 | bytes 9437184 | tf_op jit(solution)/shard_map/add | solution.py:894
  263.8 21.1 %all-to-all-done.7.final_ref = bf16[16,56,768]{2,1,0:T(8,128)(2,1)} async-done(((bf16[16,56,768]{2,1,0:T(8,128)(2,1)}), bf16[16,56,768]{2,1,0:T(8,128)(2,1)}, u32[]{:S(2)}, u32[]{:S(2)}) %all-to-all-start.7) | async-done | bytes 1376288 | tf_op jit(solution)/shard_map/all_to_all | solution.py:658
  284.9 2.3 sums.1
  287.2 0.5 collective-permute-start.12
  287.7 0.9 convert_element_type.46
  288.7 0.7 add.57
  289.5 0.5 slice_bitcast_fusion.1
  290.0 0.6 slice_bitcast_fusion
  290.6 0.6 reshape_squeeze.3
  291.3 0.6 copy-done.15
  291.9 2.6 input_grad.1
  (73 shorter events, 0.9 us)
Async XLA Ops:
  0.6 4.0 %copy-start = (bf16[48,768]{1,0:T(8,128)(2,1)S(1)}, bf16[48,768]{1,0:T(8,128)(2,1)}, u32[]{:S(2)}) copy-start(bf16[48,768]{1,0:T(8,128)(2,1)} %param.15) | copy-start | bytes 221188
  1.4 4.6 %collective-permute-start.1 = (bf16[2,64]{1,0:T(2,128)(2,1)S(1)}, bf16[2,64]{1,0:T(2,128)(2,1)S(1)}, u32[]{:S(2)}, u32[]{:S(2)}) collective-permute-start(bf16[2,64]{1,0:T(2,128)(2,1)S(1)} %convert_element_type.38), channel_id=1, source_target_pairs={{0,16},{16,0},{1,17},{17,1},{2,18},{18,2},{3,19},{19,3},{4,20},{20... | collective-permute-start | bytes 776 | tf_op jit(solution)/shard_map/ppermute | solution.py:701
  2.8 3.3 %collective-permute-start = (bf16[2,32,768]{2,1,0:T(8,128)(2,1)S(1)}, bf16[2,32,768]{2,1,0:T(8,128)(2,1)S(1)}, u32[]{:S(2)}, u32[]{:S(2)}) collective-permute-start(bf16[2,32,768]{2,1,0:T(8,128)(2,1)S(1)} %get-tuple-element.121), channel_id=1, source_target_pairs={{0,16},{16,0},{1,17},{17,1},{2,18},{18,2},{3,19},{19,3},{4,20},{20... | collective-permute-start | bytes 294920 | tf_op jit(solution)/shard_map/ppermute | solution.py:701
  6.3 9.6 %copy-start.6 = (bf16[48,768]{1,0:T(8,128)(2,1)S(1)}, bf16[48,768]{1,0:T(8,128)(2,1)}, u32[]{:S(2)}) copy-start(bf16[48,768]{1,0:T(8,128)(2,1)} %param.18) | copy-start | bytes 221188
  7.5 39.1 %all-to-all-start = ((bf16[16,56,768]{2,1,0:T(8,128)(2,1)}), bf16[16,56,768]{2,1,0:T(8,128)(2,1)S(1)}, u32[]{:S(2)}, u32[]{:S(2)}) async-start(bf16[16,56,768]{2,1,0:T(8,128)(2,1)} %bitcast.9), calls=%async_computation | async-start | bytes 2752512 | tf_op jit(solution)/shard_map/all_to_all | solution.py:658
  46.6 11.3 %copy-start.1 = (bf16[16,56,768]{2,1,0:T(8,128)(2,1)}, bf16[16,56,768]{2,1,0:T(8,128)(2,1)S(1)}, u32[]{:S(2)}) copy-start(bf16[16,56,768]{2,1,0:T(8,128)(2,1)S(1)} %all-to-all-done.own_ref) | copy-start | bytes 4128772
  46.6 3.1 %collective-permute-start.2 = (bf16[16,56,768]{2,1,0:T(8,128)(2,1)S(1)}, bf16[16,56,768]{2,1,0:T(8,128)(2,1)S(1)}, u32[]{:S(2)}, u32[]{:S(2)}) collective-permute-start(bf16[16,56,768]{2,1,0:T(8,128)(2,1)S(1)} %all-to-all-done.own_ref), channel_id=1, source_target_pairs={{0,16},{16,0},{1,17},{17,1},{2,18},{18,2},{3,19},{19,3},{4,20},{20... | collective-permute-start | bytes 4128776 | tf_op jit(solution)/shard_map/ppermute | solution.py:701
  49.7 8.1 %copy-start.8 = (bf16[16,56,768]{2,1,0:T(8,128)(2,1)}, bf16[16,56,768]{2,1,0:T(8,128)(2,1)S(1)}, u32[]{:S(2)}) copy-start(bf16[16,56,768]{2,1,0:T(8,128)(2,1)S(1)} %collective-permute-done.2.other_ref) | copy-start | bytes 4128772
  50.7 26.7 %all-to-all-start.1 = ((bf16[16,48,384]{2,1,0:T(8,128)(2,1)}), bf16[16,48,384]{2,1,0:T(8,128)(2,1)S(1)}, u32[]{:S(2)}, u32[]{:S(2)}) async-start(bf16[16,48,384]{2,1,0:T(8,128)(2,1)} %broadcast_in_dim.48), calls=%async_computation.1 | async-start | bytes 1179648 | tf_op jit(solution)/shard_map/all_to_all | solution.py:658
  57.8 37.7 %copy-start.7 = (s32[2,64,1]{1,2,0:T(1,128)S(1)}, s32[2,64,1]{1,2,0:T(1,128)}, u32[]{:S(2)}) copy-start(s32[2,64,1]{1,2,0:T(1,128)} %param.25) | copy-start | bytes 1540
  77.4 19.6 %copy-start.3 = (bf16[16,48,384]{2,1,0:T(8,128)(2,1)}, bf16[16,48,384]{2,1,0:T(8,128)(2,1)S(1)}, u32[]{:S(2)}) copy-start(bf16[16,48,384]{2,1,0:T(8,128)(2,1)S(1)} %all-to-all-done.1) | copy-start | bytes 1769476
  77.4 19.6 %collective-permute-start.4 = (bf16[768,384]{1,0:T(8,128)(2,1)S(1)}, bf16[768,384]{1,0:T(8,128)(2,1)S(1)}, u32[]{:S(2)}, u32[]{:S(2)}) collective-permute-start(bf16[768,384]{1,0:T(8,128)(2,1)S(1)} %bitcast.27), channel_id=1, source_target_pairs={{0,16},{16,0},{1,17},{17,1},{2,18},{18,2},{3,19},{19,3},{4,20},{20... | collective-permute-start | bytes 1769480 | tf_op jit(solution)/shard_map/ppermute | solution.py:701
  77.5 17.4 %all-to-all-start.2 = ((bf16[16,32,192]{2,1,0:T(8,128)(2,1)}), bf16[16,32,192]{2,1,0:T(8,128)(2,1)S(1)}, u32[]{:S(2)}, u32[]{:S(2)}) async-start(bf16[16,32,192]{2,1,0:T(8,128)(2,1)} %bitcast.30), calls=%async_computation.2 | async-start | bytes 524288 | tf_op jit(solution)/shard_map/all_to_all | solution.py:658
  94.9 2.1 copy-start.4
  94.9 2.0 collective-permute-start.3
  96.9 0.7 copy-start.13
  97.0 0.9 copy-start.9
  154.7 4.8 %copy-start.17 = (bf16[512,1536]{1,0:T(8,128)(2,1)S(1)}, bf16[512,1536]{1,0:T(8,128)(2,1)}, u32[]{:S(2)}) copy-start(bf16[512,1536]{1,0:T(8,128)(2,1)} %get-tuple-element.78) | copy-start | bytes 4718596
  154.7 4.8 %copy-start.19 = (bf16[512,768]{1,0:T(8,128)(2,1)S(1)}, bf16[512,768]{1,0:T(8,128)(2,1)}, u32[]{:S(2)}) copy-start(bf16[512,768]{1,0:T(8,128)(2,1)} %get-tuple-element.77) | copy-start | bytes 2359300
  154.7 38.7 %all-to-all-start.4 = ((bf16[16,64,768]{2,1,0:T(8,128)(2,1)}), bf16[16,64,768]{2,1,0:T(8,128)(2,1)}, u32[]{:S(2)}, u32[]{:S(2)}) async-start(bf16[16,64,768]{2,1,0:T(8,128)(2,1)} %get-tuple-element.76), calls=%async_computation.4 | async-start | bytes 3145728 | tf_op jit(solution)/shard_map/all_to_all | solution.py:658
  159.5 2.9 copy-start.18
  159.5 2.9 copy-start.20
  193.5 4.6 %copy-start.10 = (bf16[128,768]{1,0:T(8,128)(2,1)S(1)}, bf16[128,768]{1,0:T(8,128)(2,1)}, u32[]{:S(2)}) copy-start(bf16[128,768]{1,0:T(8,128)(2,1)} %get-tuple-element.92.attended_ref) | copy-start | bytes 589828
  198.0 1.6 collective-permute-start.5
  198.0 10.6 %collective-permute-start.6 = (bf16[128,768]{1,0:T(8,128)(2,1)S(1)}, bf16[128,768]{1,0:T(8,128)(2,1)S(1)}, u32[]{:S(2)}, u32[]{:S(2)}) collective-permute-start(bf16[128,768]{1,0:T(8,128)(2,1)S(1)} %copy-done.10), channel_id=1, source_target_pairs={{0,16},{16,0},{1,17},{17,1},{2,18},{18,2},{3,19},{19,3},{4,20},{20... | collective-permute-start | bytes 589832 | tf_op jit(solution)/shard_map/ppermute | solution.py:701
  198.5 10.1 %collective-permute-start.7 = (bf16[128,768]{1,0:T(8,128)(2,1)}, bf16[128,768]{1,0:T(8,128)(2,1)S(1)}, u32[]{:S(2)}, u32[]{:S(2)}) collective-permute-start(bf16[128,768]{1,0:T(8,128)(2,1)} %get-tuple-element.93.d_ref), channel_id=1, source_target_pairs={{0,16},{16,0},{1,17},{17,1},{2,18},{18,2},{3,19},{19,3},{4,20},{20... | collective-permute-start | bytes 589832 | tf_op jit(solution)/shard_map/ppermute | solution.py:701
  201.4 17.4 %all-to-all-start.5 = ((bf16[16,32,192]{2,1,0:T(8,128)(2,1)}), bf16[16,32,192]{2,1,0:T(8,128)(2,1)S(1)}, u32[]{:S(2)}, u32[]{:S(2)}) async-start(bf16[16,32,192]{2,1,0:T(8,128)(2,1)} %maximum_select_fusion), calls=%async_computation.5 | async-start | bytes 524288 | tf_op jit(solution)/shard_map/all_to_all | solution.py:658
  208.6 45.5 %collective-permute-start.10 = (bf16[768,1536]{1,0:T(8,128)(2,1)}, bf16[768,1536]{1,0:T(8,128)(2,1)}, u32[]{:S(2)}, u32[]{:S(2)}) collective-permute-start(bf16[768,1536]{1,0:T(8,128)(2,1)} %convolution_convert_fusion.1), channel_id=1, source_target_pairs={{0,16},{16,0},{1,17},{17,1},{2,18},{18,2},{3,19},{19,3},{4,20},{20... | collective-permute-start | bytes 7077896 | tf_op jit(solution)/shard_map/ppermute | solution.py:701
  208.7 0.7 copy-start.11
  209.3 0.7 copy-start.12
  218.7 3.6 %copy-start.2 = (bf16[16,32,192]{2,1,0:T(8,128)(2,1)}, bf16[16,32,192]{2,1,0:T(8,128)(2,1)S(1)}, u32[]{:S(2)}) copy-start(bf16[16,32,192]{2,1,0:T(8,128)(2,1)S(1)} %all-to-all-done.5) | copy-start | bytes 589828
  218.8 19.4 %all-to-all-start.6 = ((bf16[16,24,768]{2,1,0:T(8,128)(2,1)}), bf16[16,24,768]{2,1,0:T(8,128)(2,1)S(1)}, u32[]{:S(2)}, u32[]{:S(2)}) async-start(bf16[16,24,768]{2,1,0:T(8,128)(2,1)} %out_grad.1), calls=%async_computation.6 | async-start | bytes 1179648 | tf_op jit(solution)/shard_map/all_to_all | solution.py:658
  234.1 5.2 %collective-permute-start.8 = (bf16[16,64,576]{2,1,0:T(8,128)(2,1)}, bf16[16,64,576]{2,1,0:T(8,128)(2,1)}, u32[]{:S(2)}, u32[]{:S(2)}) collective-permute-start(bf16[16,64,576]{2,1,0:T(8,128)(2,1)} %get-tuple-element.95.d_own_ref), channel_id=1, source_target_pairs={{0,16},{16,0},{1,17},{17,1},{2,18},{18,2},{3,19},{19,3},{4,20},{20... | collective-permute-start | bytes 3538952 | tf_op jit(solution)/shard_map/ppermute | solution.py:701
  234.1 25.3 %collective-permute-start.11 = (bf16[1536,768]{1,0:T(8,128)(2,1)S(1)}, bf16[1536,768]{1,0:T(8,128)(2,1)}, u32[]{:S(2)}, u32[]{:S(2)}) collective-permute-start(bf16[1536,768]{1,0:T(8,128)(2,1)S(1)} %convolution_convert_fusion), channel_id=1, source_target_pairs={{0,16},{16,0},{1,17},{17,1},{2,18},{18,2},{3,19},{19,3},{4,20},{20... | collective-permute-start | bytes 7077896 | tf_op jit(solution)/shard_map/ppermute | solution.py:701
  238.2 8.9 %copy-start.5 = (f32[24,768]{1,0:T(8,128)}, f32[24,768]{1,0:T(8,128)S(1)}, u32[]{:S(2)}) copy-start(f32[24,768]{1,0:T(8,128)S(1)} %convert_reduce_fusion.out_mine_ref) | copy-start | bytes 221188
  238.3 8.9 %collective-permute-start.9 = (f32[24,768]{1,0:T(8,128)S(1)}, f32[24,768]{1,0:T(8,128)S(1)}, u32[]{:S(2)}, u32[]{:S(2)}) collective-permute-start(f32[24,768]{1,0:T(8,128)S(1)} %convert_reduce_fusion.out_mine_ref), channel_id=1, source_target_pairs={{0,16},{16,0},{1,17},{17,1},{2,18},{18,2},{3,19},{19,3},{4,20},{20... | collective-permute-start | bytes 221192 | tf_op jit(solution)/shard_map/ppermute | solution.py:701
  247.1 12.2 %copy-start.16 = (f32[24,768]{1,0:T(8,128)}, f32[24,768]{1,0:T(8,128)S(1)}, u32[]{:S(2)}) copy-start(f32[24,768]{1,0:T(8,128)S(1)} %collective-permute-done.9.out_other_ref) | copy-start | bytes 221188
  247.2 37.8 %all-to-all-start.7 = ((bf16[16,56,768]{2,1,0:T(8,128)(2,1)}), bf16[16,56,768]{2,1,0:T(8,128)(2,1)}, u32[]{:S(2)}, u32[]{:S(2)}) async-start(bf16[16,56,768]{2,1,0:T(8,128)(2,1)} %input_side.1), calls=%async_computation.7 | async-start | bytes 2752512 | tf_op jit(solution)/shard_map/all_to_all | solution.py:658
  287.2 1.5 collective-permute-start.14
  287.2 4.1 %collective-permute-start.12 = (bf16[2,32,768]{2,1,0:T(8,128)(2,1)}, bf16[2,32,768]{2,1,0:T(8,128)(2,1)S(1)}, u32[]{:S(2)}, u32[]{:S(2)}) collective-permute-start(bf16[2,32,768]{2,1,0:T(8,128)(2,1)} %get-tuple-element.107), channel_id=1, source_target_pairs={{0,16},{16,0},{1,17},{17,1},{2,18},{18,2},{3,19},{19,3},{4,20},{20... | collective-permute-start | bytes 294920 | tf_op jit(solution)/shard_map/ppermute | solution.py:701
  288.7 2.6 collective-permute-start.13
  291.3 0.6 copy-start.15
  291.3 0.7 copy-start.14
where the time goes:
time: 298 us; the launch traced here: 295 us
  waiting for transfers between devices  106 us (36%)
  Pallas kernels  65.8 us (22%)
  starting transfers between devices  47.4 us (16%)
  blocking collectives  42.4 us (14%)
  other arithmetic  16.8 us (6%)
  local copies, waits for them, and re-layouts  10.9 us (4%)
  matrix products  4.29 us (1%)
    all_to_all x7, waiting for transfers between devices, exchange(): return lax.all_to_all(value, 'sq', split_axis=0, concat_axis=0, tiled=True)  101 us
    all_to_all x7, starting transfers between devices, exchange(): return lax.all_to_all(value, 'sq', split_axis=0, concat_axis=0, tiled=True)  44.9 us
    all_to_all x1, blocking collectives, exchange(): return lax.all_to_all(value, 'sq', split_axis=0, concat_axis=0, tiled=True)  42.4 us
    pallas_call x1, Pallas kernels, local(): pl.pallas_call(partial(forward_kernel, shard=shard, all_heads=heads, **si...  19.5 us
    pallas_call x1, Pallas kernels, local(): pl.pallas_call(partial(backward_kernel, **sizes), name='attention_backwar...  11.7 us
    pallas_call x1, Pallas kernels, local(): pl.pallas_call(partial(expert_kernel, few=few), name='experts', grid=(hid...  10.4 us
    add x2, other arithmetic, both_reps(): return value.astype(f32) + swap(value).astype(f32)  9.71 us
    pallas_call x1, Pallas kernels, local(): pl.pallas_call(partial(last_kernel, groups=groups, half=half, rows=rows,...  7.85 us
  transfers between devices with their start and end apart: 22, of which 9 were waited for; matrix products, arithmetic and copies ran while one was open for 9% of the time, Pallas kernels for 14%

commit v1 on v0

--- a/solution.py
+++ b/solution.py
@@ -26,6 +26,65 @@
     row = lax.broadcasted_iota(jnp.int32, shape, 0)
     col = lax.broadcasted_iota(jnp.int32, shape, 1)
     return col - LANES - (rows * (row // sub) + offset + row % sub)
+
+
+def pack_kernel(
+    place_ref,
+    x_ref,
+    x_other_ref,
+    seg_ref,
+    seg_other_ref,
+    query_ref,
+    key_ref,
+    value_ref,
+    gain_one_ref,
+    gain_two_ref,
+    router_ref,
+    table_ref,
+    send_ref,
+    weights,
+    small,
+    *,
+    half,
+    split,
+):
+    seqs, rows, width = x_ref.shape
+    shard = query_ref.shape[0]
+    part = shard // 2
+    head_width = width // HEAD_GROUPS
+    base = 3 * head_width
+    per_seq = HEAD_GROUPS * split
+    heads = table_ref.shape[1]
+    for c in range(2):
+
+        @pl.when(place_ref[4] == c)
+        def _():
+            at = slice(c * part, (c + 1) * part)
+            for i, ref in enumerate((query_ref, key_ref, value_ref)):
+                for g in range(HEAD_GROUPS):
+                    weights[g, :, i * head_width : (i + 1) * head_width] = ref[
+                        at, g * head_width : (g + 1) * head_width
+                    ].astype(f32)
+
+    small[...] = jnp.zeros_like(small)
+    small[0:1, 0:shard] = gain_one_ref[...].astype(f32)
+    small[1:2, 0:shard] = gain_two_ref[...].astype(f32)
+    small[2 : 2 + EXPERTS, 0:shard] = router_ref[...].astype(f32)
+    for k in range(table_ref.shape[0]):
+        small[2 + EXPERTS : 3 + EXPERTS, k * heads : (k + 1) * heads] = table_ref[
+            k : k + 1, :
+        ].astype(f32)
+    x_at = pl.ds(pl.multiple_of(place_ref[0], half), half)
+    for c in range(2):
+        x, seg = (x_ref, seg_ref) if c == 0 else (x_other_ref, seg_other_ref)
+        first = (place_ref[3] if c == 0 else seqs - place_ref[3]) * per_seq
+        for l in range(seqs):
+            small[3 + EXPERTS : 4 + EXPERTS, 0:rows] = seg[l : l + 1, :].astype(f32)
+            for k in range(per_seq):
+                at = first + l * per_seq + k
+                send_ref[at, 0:half, :] = x[l, x_at, :]
+                send_ref[at, half:, 0:base] = weights[k // split].astype(bf16)
+                send_ref[at, half:, base:] = small[...].astype(bf16)
 
 
 def forward_kernel(
@@ -111,7 +170,7 @@
         normed_all[p, pl.ds(other_at, half), :] = norm(other_ref[p, 0:half, :])
         return carry
 
-    lax.fori_loop(0, groups, norm_step, 0)
+    lax.fori_loop(0, groups, norm_step, 0, unroll=2)
     chunk = 4
 
     def project_step(c, carry):
@@ -163,7 +222,7 @@
                 probs_ref[h, here, :] = (value * (1.0 / total)).astype(bf16)
             return carry
 
-        lax.fori_loop(0, steps, soft_step, 0)
+        lax.fori_loop(0, steps, soft_step, 0, unroll=2)
         attended_ref[:, at : at + head_dim] = dot(
             probs_ref[h], pair_ref[:, head_width + at : head_width + at + head_dim]
         ).astype(bf16)
@@ -233,7 +292,7 @@
                 strip[par * sub : (par + 1) * sub, pl.ds(start, length)] += value
             return carry
 
-        lax.fori_loop(0, steps, score_step, 0)
+        lax.fori_loop(0, steps, score_step, 0, unroll=2)
         d_query[:, at : at + head_dim] = dot(low[...], pair_ref[:, at : at + head_dim]) * factor
         flipped[at : at + head_dim, :] = (
             dot(query_ref[:, at : at + head_dim], low[...], ((0,), (0,))) * factor
@@ -349,7 +408,7 @@
 
 
 def sum_kernel(
-    place_ref, final_ref, keep_ref, give_ref, four_ref, small_ref, *, half, seqs
+    place_ref, final_ref, keep_ref, give_ref, four_ref, low_ref, small_ref, *, half, seqs
 ):
     groups, _, width = final_ref.shape
     part = four_ref.shape[1]
@@ -380,6 +439,7 @@
             four_ref[i, :, g * head_width : (g + 1) * head_width] = grad[
                 :, i * head_width : (i + 1) * head_width
             ]
+    low_ref[...] = four_ref[...].astype(bf16)
     small = final_ref[0, half:, base:].astype(f32)
     for p in range(1, groups):
         small = small + final_ref[p, half:, base:].astype(f32)
@@ -394,6 +454,8 @@
     other_ref,
     out_mine_ref,
     out_other_ref,
+    small_ref,
+    small_other_ref,
     x_ref,
     d_hidden_ref,
     gain_ref,
@@ -402,10 +464,22 @@
     key_ref,
     value_ref,
     out_ref,
+    table_ref,
+    gain_one_ref,
+    gain_two_ref,
+    router_ref,
     d_normed_ref,
     *,
     half,
 ):
+    small = small_ref[...] + small_other_ref[...]
+    shard = gain_one_ref.shape[1]
+    heads = table_ref.shape[1]
+    gain_one_ref[...] = small[0:1, 0:shard]
+    gain_two_ref[...] = small[1:2, 0:shard]
+    router_ref[...] = small[2 : 2 + EXPERTS, 0:shard]
+    for k in range(table_ref.shape[0]):
+        table_ref[k : k + 1, :] = small[2 + EXPERTS : 3 + EXPERTS, k * heads : (k + 1) * heads]
     core_at = pl.multiple_of(place_ref[0], half)
     other_at = pl.multiple_of(half - place_ref[0], half)
     seqs, rows, width = x_ref.shape
@@ -509,56 +583,26 @@
                 ]
 
 
-def expert_step(received, got, up, down):
+def expert_kernel(arrived_ref, up_ref, down_ref, results_ref, act_ref, d_pre_ref, *, few):
+    groups, _, width = arrived_ref.shape
+    rows = groups * few
+    received = arrived_ref[:, 0:few, :].reshape(rows, width)
+    got = arrived_ref[:, few:, :].reshape(rows, width)
+    root = 0.7978845608028654
+    up, down = up_ref[...], down_ref[...]
     pre = dot(received, up)
-    root = 0.7978845608028654
     square = pre * pre
     bend = jnp.tanh(root * (pre + 0.044715 * (square * pre)))
     side = 0.5 * (1.0 + bend)
     act = (pre * side).astype(bf16)
     slope = side + 0.5 * pre * (1.0 - bend * bend) * (root * (1.0 + 3 * 0.044715 * square))
     d_pre = (dot(got, down, ((1,), (1,))) * slope).astype(bf16)
-    return act, d_pre, dot(act, down), dot(d_pre, up, ((1,), (1,)))
-
-
-def expert_kernel(
-    arrived_ref,
-    up_ref,
-    down_ref,
-    results_ref,
-    received_ref,
-    got_ref,
-    act_ref,
-    d_pre_ref,
-    out_sum,
-    row_sum,
-    *,
-    few,
-):
-    groups, _, width = arrived_ref.shape
-    step = pl.program_id(0)
-
-    @pl.when(step == 0)
-    def _():
-        out_sum[...] = jnp.zeros_like(out_sum)
-        row_sum[...] = jnp.zeros_like(row_sum)
-        shape = (groups * few, width)
-        received_ref[...] = arrived_ref[:, 0:few, :].reshape(shape)
-        got_ref[...] = arrived_ref[:, few:, :].reshape(shape)
-
-    act, d_pre, out, rows = expert_step(
-        received_ref[...], got_ref[...], up_ref[...], down_ref[...]
-    )
     act_ref[...] = act
     d_pre_ref[...] = d_pre
-    out_sum[...] += out
-    row_sum[...] += rows
-
-    @pl.when(step == pl.num_programs(0) - 1)
-    def _():
-        shape = (groups, few, width)
-        results_ref[:, 0:few, :] = out_sum[...].reshape(shape).astype(bf16)
-        results_ref[:, few:, :] = row_sum[...].reshape(shape).astype(bf16)
+    out = dot(act, down).astype(bf16)
+    back = dot(d_pre, up, ((1,), (1,))).astype(bf16)
+    results_ref[:, 0:few, :] = out.reshape(groups, few, width)
+    results_ref[:, few:, :] = back.reshape(groups, few, width)
 
 
 def turn_kernel(
@@ -719,54 +763,6 @@
         sets = [list(range(0, reps, 2)), list(range(1, reps, 2))]
         return lax.psum(value, "rep", axis_index_groups=sets)
 
-    x_pair = by_core(mine(inputs, 1, half), swap(yours(inputs, 1, half)), 0)
-    seg_low = segments.astype(bf16)
-    seg_pair = by_core(seg_low, swap(seg_low), 0)
-    w_three = jnp.stack([mine(w, 0, part) for w in (w_query, w_key, w_value)], axis=1)
-    w_three = w_three.reshape(part, 3, HEAD_GROUPS, head_width)
-    w_send = jnp.transpose(w_three, (2, 0, 1, 3)).reshape(HEAD_GROUPS, part, 3 * head_width)
-    spare = width - 3 * head_width
-
-    def widen(value):
-        return jnp.pad(value, ((0, 0), (0, spare - value.shape[1])))
-
-    small = jnp.concatenate(
-        [
-            widen(gain_one[None]),
-            widen(gain_two[None]),
-            widen(w_router.T),
-            widen(table.reshape(1, -1)),
-        ],
-        axis=0,
-    )
-    small = jnp.broadcast_to(small[None], (all_seqs,) + small.shape)
-    small = jnp.concatenate(
-        [small, jnp.pad(seg_pair, ((0, 0), (0, spare - rows)))[:, None, :]], axis=1
-    )
-    small = jnp.pad(small, ((0, 0), (0, part - small.shape[1]), (0, 0)))
-
-    shape = (all_seqs, HEAD_GROUPS, split)
-    lower = jnp.concatenate(
-        [
-            jnp.broadcast_to(w_send[None, :, None], shape + w_send.shape[1:]),
-            jnp.broadcast_to(small[:, None, None], shape + small.shape[1:]),
-        ],
-        axis=-1,
-    )
-    send = jnp.concatenate(
-        [jnp.broadcast_to(x_pair[:, None, None], shape + x_pair.shape[1:]), lower], axis=3
-    ).reshape(groups, half + part, width)
-    own = exchange(send)
-    own, out_half = lax.optimization_barrier((own, mine(w_out, 1, width // 2)))
-    other, out_half = lax.optimization_barrier((swap(own), out_half))
-    out_mine = exchange(jnp.broadcast_to(out_half[None], (groups, shard, width // 2)))
-    query_at = core * half + (me % split) * sub
-    place = jnp.stack([core * half, query_at, group_at * group_heads, core * seqs, core])
-    place = place.astype(jnp.int32)
-    shard_table = bucket_rows * heads
-    queries_count = groups * sub
-    tile = (LANES // rows) * sub
-    sizes = dict(groups=groups, half=half, rows=rows, sub=sub, head_dim=head_dim)
     smem = pl.BlockSpec(memory_space=pltpu.SMEM)
     vmem = pl.BlockSpec(memory_space=pltpu.VMEM)
 
@@ -778,6 +774,48 @@
         )
 
     limit = pltpu.CompilerParams(vmem_limit_bytes=56 * 1024 * 1024)
+    spare = width - 3 * head_width
+    query_at = core * half + (me % split) * sub
+    place = jnp.stack([core * half, query_at, group_at * group_heads, core * seqs, core])
+    place = place.astype(jnp.int32)
+    shard_table = bucket_rows * heads
+    send = pl.pallas_call(
+        partial(pack_kernel, half=half, split=split),
+        name="pack",
+        out_shape=jax.ShapeDtypeStruct((groups, half + part, width), bf16),
+        in_specs=[smem] + [vmem] * 11,
+        out_specs=vmem,
+        scratch_shapes=[
+            pltpu.VMEM((HEAD_GROUPS, part, 3 * head_width), f32),
+            pltpu.VMEM((part, spare), f32),
+        ],
+        compiler_params=limit,
+        cost_estimate=cost(3),
+    )(
+        place,
+        inputs,
+        swap(inputs),
+        segments,
+        swap(segments),
+        w_query,
+        w_key,
+        w_value,
+        gain_one.reshape(1, shard),
+        gain_two.reshape(1, shard),
+        w_router.T,
+        table,
+    )
+    own = exchange(send)
+    out_half = mine(w_out, 1, width // 2)
+    out_send = jnp.broadcast_to(out_half[None], (groups, shard, width // 2))
+    own, out_send, place, routes_flat = lax.optimization_barrier(
+        (own, out_send, place, routes.reshape(tokens, 1))
+    )
+    other, out_send = lax.optimization_barrier((swap(own), out_send))
+    out_mine = exchange(out_send)
+    queries_count = groups * sub
+    tile = (LANES // rows) * sub
+    sizes = dict(groups=groups, half=half, rows=rows, sub=sub, head_dim=head_dim)
     (
         attended_part,
         probs,
@@ -822,7 +860,6 @@
     out_yours = swap(out_mine)
     back_given = swap(yours(back, 0, groups // 2))
     few = CAP
-    routes_flat = routes.reshape(tokens, 1)
     pieces = dict(half=half, sub=sub, split=split, few=few)
     buffer, attended, hidden, normed_two, router_probs, spread = pl.pallas_call(
         partial(middle_kernel, share=share, **pieces),
@@ -854,37 +891,23 @@
     )
     arrived = exchange(buffer)
     expert_rows = groups * few
-    hidden_units = w_up.shape[1]
-    chunk = hidden_units // 3 if hidden_units % (3 * LANES) == 0 else hidden_units
-    whole = [
-        pl.BlockSpec((groups, 2 * few, width), lambda i: (0, 0, 0)),
-        pl.BlockSpec((expert_rows, width), lambda i: (0, 0)),
-        pl.BlockSpec((expert_rows, chunk), lambda i: (0, i)),
-    ]
-    rows_low = jax.ShapeDtypeStruct((expert_rows, width), bf16)
-    units_low = jax.ShapeDtypeStruct((expert_rows, hidden_units), bf16)
-    results, received, got, act, d_pre = pl.pallas_call(
+    units_low = jax.ShapeDtypeStruct((expert_rows, w_up.shape[1]), bf16)
+    results, act, d_pre = pl.pallas_call(
         partial(expert_kernel, few=few),
         name="experts",
-        grid=(hidden_units // chunk,),
         out_shape=(
             jax.ShapeDtypeStruct((groups, 2 * few, width), bf16),
-            rows_low,
-            rows_low,
             units_low,
             units_low,
         ),
-        in_specs=[
-            whole[0],
-            pl.BlockSpec((width, chunk), lambda i: (0, i)),
-            pl.BlockSpec((chunk, width), lambda i: (i, 0)),
-        ],
-        out_specs=[whole[0]] + [whole[1]] * 2 + [whole[2]] * 2,
-        scratch_shapes=[pltpu.VMEM((expert_rows, width), f32)] * 2,
+        in_specs=[vmem] * 3,
+        out_specs=[vmem] * 3,
         compiler_params=limit,
         cost_estimate=cost(8),
     )(arrived, w_up, w_down)
     returned = exchange(results)
+    received = arrived[:, :few].reshape(expert_rows, width)
+    got = arrived[:, few:].reshape(expert_rows, width)
     up_local = dot(received, d_pre, ((0,), (0,))).astype(bf16)
     down_local = dot(act, got, ((0,), (0,))).astype(bf16)
     returned, up_local, down_local = lax.optimization_barrier((returned, up_local, down_local))
@@ -991,30 +1014,47 @@
     up_grad = both_reps(up_local)
     down_grad = both_reps(down_local)
     final, up_grad, down_grad = lax.optimization_barrier((final, up_grad, down_grad))
-    keep, give, four, small_sum = pl.pallas_call(
+    keep, give, four, four_low, small_sum = pl.pallas_call(
         partial(sum_kernel, half=half, seqs=seqs),
         name="sums",
         out_shape=(
             jax.ShapeDtypeStruct((seqs, half, width), f32),
             jax.ShapeDtypeStruct((seqs, half, width), bf16),
             jax.ShapeDtypeStruct((3, part, width), f32),
+            jax.ShapeDtypeStruct((3, part, width), bf16),
             jax.ShapeDtypeStruct((part, spare), f32),
         ),
         in_specs=[smem] + [vmem],
-        out_specs=[vmem] * 4,
+        out_specs=[vmem] * 5,
         compiler_params=limit,
         cost_estimate=cost(2),
     )(place, final)
-    four = over_pairs(four)
-    small_sum = over_pairs(small_sum)
-    small_sum = small_sum + swap(small_sum)
-    input_grad, query_grad, key_grad, value_grad, out_grad = pl.pallas_call(
+    if reps > 2:
+        four, small_sum = over_pairs(four), over_pairs(small_sum)
+        four_low = four.astype(bf16)
+    (
+        input_grad,
+        query_grad,
+        key_grad,
+        value_grad,
+        out_grad,
+        table_grad,
+        gain_one_grad,
+        gain_two_grad,
+        router_grad,
+    ) = pl.pallas_call(
         partial(input_kernel, half=half),
         name="input_grad",
         out_shape=(jax.ShapeDtypeStruct((seqs, rows, width), f32),)
-        + (jax.ShapeDtypeStruct((shard, width), f32),) * 4,
-        in_specs=[smem] + [vmem] * 9,
-        out_specs=[vmem] * 5,
+        + (jax.ShapeDtypeStruct((shard, width), f32),) * 4
+        + (
+            jax.ShapeDtypeStruct((bucket_rows, heads), f32),
+            jax.ShapeDtypeStruct((1, shard), f32),
+            jax.ShapeDtypeStruct((1, shard), f32),
+            jax.ShapeDtypeStruct((EXPERTS, shard), f32),
+        ),
+        in_specs=[smem] + [vmem] * 11,
+        out_specs=[vmem] * 9,
         scratch_shapes=[pltpu.VMEM((seqs, rows, width), f32)],
         compiler_params=limit,
         cost_estimate=cost(2),
@@ -1023,9 +1063,11 @@
         keep,
         swap(give),
         four,
-        swap(four.astype(bf16)),
+        swap(four_low),
         out_sum,
         out_other,
+        small_sum,
+        swap(small_sum),
         inputs,
         d_hidden,
         gain_one_full,
@@ -1037,10 +1079,10 @@
         key_grad,
         value_grad,
         out_grad,
-        small_sum[2 + EXPERTS, :shard_table].reshape(bucket_rows, heads),
-        small_sum[0, :shard],
-        small_sum[1, :shard],
-        small_sum[2 : 2 + EXPERTS, :shard].T,
+        table_grad,
+        gain_one_grad.reshape(shard),
+        gain_two_grad.reshape(shard),
+        router_grad.T,
         up_grad,
         down_grad,
     )

time: 298 us -> 287 us (0.963)
  other arithmetic: 16.8 us -> 12.2 us
  local copies, waits for them, and re-layouts: 10.9 us -> 7.89 us
    pallas_call x1, Pallas kernels: 19.5 us -> 16 us  [local(): pl.pallas_call(partial(forward_kernel, shard=shard, all_heads=heads, **si...]
    pallas_call x1 -> x2, Pallas kernels: 10.4 us -> 12.1 us  [the longest x1 9.45 us: local(): pl.pallas_call(partial(expert_kernel, few=few), name='experts', out_shape...]
  transfers between devices with their start and end apart: 22 -> 22, of which waited for: 9 -> 13; matrix products, arithmetic and copies ran while one was open for 9% -> 7% of each run, Pallas kernels for 14% -> 13%
where the time goes in v1:
time: 287 us; the launch traced here: 285 us
  waiting for transfers between devices  107 us (37%)
  Pallas kernels  63.2 us (22%)
  starting transfers between devices  46.9 us (16%)
  blocking collectives  42.3 us (15%)
  other arithmetic  12.2 us (4%)
  local copies, waits for them, and re-layouts  7.89 us (3%)
  matrix products  4.24 us (1%)
    all_to_all x7, waiting for transfers between devices, exchange(): return lax.all_to_all(value, 'sq', split_axis=0, concat_axis=0, tiled=True)  99.6 us
    all_to_all x7, starting transfers between devices, exchange(): return lax.all_to_all(value, 'sq', split_axis=0, concat_axis=0, tiled=True)  44.5 us
    all_to_all x1, blocking collectives, exchange(): return lax.all_to_all(value, 'sq', split_axis=0, concat_axis=0, tiled=True)  42.3 us
    pallas_call x1, Pallas kernels, local(): pl.pallas_call(partial(forward_kernel, shard=shard, all_heads=heads, **si...  16 us
    pallas_call x1, Pallas kernels, local(): pl.pallas_call(partial(backward_kernel, **sizes), name='attention_backwar...  10.7 us
    add x2, other arithmetic, both_reps(): return value.astype(f32) + swap(value).astype(f32)  9.71 us
    pallas_call x1, Pallas kernels, local(): pl.pallas_call(partial(expert_kernel, few=few), name='experts', out_shape...  9.45 us
    pallas_call x1, Pallas kernels, local(): pl.pallas_call(partial(last_kernel, groups=groups, half=half, rows=rows,...  7.93 us
  transfers between devices with their start and end apart: 22, of which 13 were waited for; matrix products, arithmetic and copies ran while one was open for 7% of the time, Pallas kernels for 13%

profile of v1, /device:TPU:0, one launch (start us, length us, event | category | flops | bytes accessed | tf_op | source)
XLA Modules:
  0.0 284.6 jit_solution(15774040345766662019)
XLA Ops:
  0.6 0.0 copy-start
  0.7 0.5 collective-permute-start
  1.2 0.1 collective-permute-start.1
  1.3 0.6 stack.20.place_ref
  1.9 0.7 collective-permute-done.1.seg_other_ref
  2.5 0.6 copy-done.18
  3.1 0.1 copy-done.10
  3.2 2.6 pack.1
  5.8 8.3 %all-to-all-start = ((bf16[16,56,768]{2,1,0:T(8,128)(2,1)}), bf16[16,56,768]{2,1,0:T(8,128)(2,1)S(1)}, u32[]{:S(2)}, u32[]{:S(2)}) async-start(bf16[16,56,768]{2,1,0:T(8,128)(2,1)} %pack.1), calls=%async_computation | async-start | bytes 2752512 | tf_op jit(solution)/shard_map/all_to_all | solution.py:702
  14.1 0.5 broadcast.8
  14.7 0.7 reduce.3
  15.3 0.1 reshape.57
  15.4 29.5 %all-to-all-done.own_ref = bf16[16,56,768]{2,1,0:T(8,128)(2,1)S(1)} async-done(((bf16[16,56,768]{2,1,0:T(8,128)(2,1)}), bf16[16,56,768]{2,1,0:T(8,128)(2,1)S(1)}, u32[]{:S(2)}, u32[]{:S(2)}) %all-to-all-start) | async-done | bytes 1376288 | tf_op jit(solution)/shard_map/all_to_all | solution.py:702
  44.9 0.9 broadcast_in_dim.2
  45.8 3.3 %collective-permute-done.2.other_ref = bf16[16,56,768]{2,1,0:T(8,128)(2,1)} collective-permute-done((bf16[16,56,768]{2,1,0:T(8,128)(2,1)S(1)}, bf16[16,56,768]{2,1,0:T(8,128)(2,1)}, u32[]{:S(2)}, u32[]{:S(2)}) %collective-permute-start.2) | collective-permute-done | bytes 1376288 | tf_op jit(solution)/shard_map/ppermute | solution.py:745
  49.1 7.4 %all-to-all-start.1 = ((bf16[16,48,384]{2,1,0:T(8,128)(2,1)}), bf16[16,48,384]{2,1,0:T(8,128)(2,1)S(1)}, u32[]{:S(2)}, u32[]{:S(2)}) async-start(bf16[16,48,384]{2,1,0:T(8,128)(2,1)} %broadcast_in_dim.2), calls=%async_computation.1 | async-start | bytes 1179648 | tf_op jit(solution)/shard_map/all_to_all | solution.py:702
  56.6 16.0 %attention_forward.1 = (bf16[512,192]{1,0:T(8,128)(2,1)}, bf16[3,512,1024]{2,1,0:T(8,128)(2,1)}, bf16[512,192]{1,0:T(8,128)(2,1)}, bf16[1024,384]{1,0:T(8,128)(2...) custom-call(s32[5]{0:T(128)} %stack.20.place_ref, ...), custom_call_target="tpu_custom_call" | custom-call | flops 54000001024 | bytes 60000000 | tf_op jit(solution)/shard_map/attention_forward/pallas_call | solution.py:829
  72.5 0.6 all-to-all-done.1
  73.1 6.4 %all-to-all-start.2 = ((bf16[16,32,192]{2,1,0:T(8,128)(2,1)}), bf16[16,32,192]{2,1,0:T(8,128)(2,1)S(1)}, u32[]{:S(2)}, u32[]{:S(2)}) async-start(bf16[16,32,192]{2,1,0:T(8,128)(2,1)} %bitcast.26), calls=%async_computation.2 | async-start | bytes 524288 | tf_op jit(solution)/shard_map/all_to_all | solution.py:702
  79.5 10.5 %all-to-all-done.2.back_ref = bf16[16,32,192]{2,1,0:T(8,128)(2,1)S(1)} async-done(((bf16[16,32,192]{2,1,0:T(8,128)(2,1)}), bf16[16,32,192]{2,1,0:T(8,128)(2,1)S(1)}, u32[]{:S(2)}, u32[]{:S(2)}) %all-to-all-start.2) | async-done | bytes 196640 | tf_op jit(solution)/shard_map/all_to_all | solution.py:702
  90.1 0.1 collective-permute-start.3
  90.1 0.7 copy.26.routes_ref
  90.9 0.6 collective-permute-done.3.swapped_ref
  91.5 0.6 copy-done.13
  92.1 0.2 copy-done.8
  92.3 4.1 %router_and_dispatch.1 = (bf16[16,64,768]{2,1,0:T(8,128)(2,1)}, bf16[128,768]{1,0:T(8,128)(2,1)}, f32[128,768]{1,0:T(8,128)}, bf16[128,768]{1,0:T(8,128)(2,1)}, ...) custom-call(s32[5]{0:T(128)} %stack.20.place_ref, bf16[16,32,192]{2,1,0:T(8,128)(2,1)} %copy-done.5, ...), custom_call_target="tpu_custom_call" | custom-call | flops 4499999744 | bytes 5000000 | tf_op jit(solution)/shard_map/router_and_dispatch/pallas_call | solution.py:864
  96.4 42.3 %all_to_all.40.arrived_ref = bf16[16,64,768]{2,1,0:T(8,128)(2,1)} all-to-all(bf16[16,64,768]{2,1,0:T(8,128)(2,1)} %get-tuple-element.82), channel_id=1, replica_groups=mesh['rep'=2,'sq'=16] {'sq'}, dimensions={0} | all-to-all | bytes 3145728 | tf_op jit(solution)/shard_map/all_to_all | solution.py:702
  138.7 9.4 %experts.1 = (bf16[16,64,768]{2,1,0:T(8,128)(2,1)}, bf16[512,1536]{1,0:T(8,128)(2,1)}, bf16[512,1536]{1,0:T(8,128)(2,1)}) custom-call(bf16[16,64,768]{2,1,0:T(8,128)(2,1)} %all_to_all.40.arrived_ref, bf16[768,1536]{1,0:T(8,128)(2,1)} %up_ref.1, bf16[1536,768]{1,0:T(8,128)(2,1)} %down_ref.1), custom_call_target="tpu_custom_call" | custom-call | flops 7200000000 | bytes 8000000 | tf_op jit(solution)/shard_map/experts/pallas_call | solution.py:895
  148.2 4.5 %all-to-all-start.4 = ((bf16[16,64,768]{2,1,0:T(8,128)(2,1)}), bf16[16,64,768]{2,1,0:T(8,128)(2,1)}, u32[]{:S(2)}, u32[]{:S(2)}) async-start(bf16[16,64,768]{2,1,0:T(8,128)(2,1)} %get-tuple-element.83), calls=%async_computation.4 | async-start | bytes 3145728 | tf_op jit(solution)/shard_map/all_to_all | solution.py:702
  152.8 0.1 fusion
  152.9 1.3 copy-done.19
  154.2 2.8 convolution_convert_fusion.1
  157.0 1.4 convolution_convert_fusion
  158.4 27.8 %all-to-all-done.4.returned_ref = bf16[16,64,768]{2,1,0:T(8,128)(2,1)} async-done(((bf16[16,64,768]{2,1,0:T(8,128)(2,1)}), bf16[16,64,768]{2,1,0:T(8,128)(2,1)}, u32[]{:S(2)}, u32[]{:S(2)}) %all-to-all-start.4) | async-done | bytes 1572896 | tf_op jit(solution)/shard_map/all_to_all | solution.py:702
  186.2 4.6 %combine_and_turn.1 = (bf16[2,64,768]{2,1,0:T(8,128)(2,1)}, f32[128,768]{1,0:T(8,128)}, bf16[128,768]{1,0:T(8,128)(2,1)}, bf16[8,32,192]{2,1,0:T(8,128)(2,1)}, b...) custom-call(s32[5]{0:T(128)} %stack.20.place_ref, ...), custom_call_target="tpu_custom_call" | custom-call | flops 4499999744 | bytes 5000000 | tf_op jit(solution)/shard_map/combine_and_turn/pallas_call | solution.py:920
  190.8 0.5 collective-permute-start.6
  191.3 0.1 collective-permute-start.7
  191.3 1.0 collective-permute-done.5
  192.3 1.8 maximum_select_fusion
  194.1 7.3 %all-to-all-start.5 = ((bf16[16,32,192]{2,1,0:T(8,128)(2,1)}), bf16[16,32,192]{2,1,0:T(8,128)(2,1)S(1)}, u32[]{:S(2)}, u32[]{:S(2)}) async-start(bf16[16,32,192]{2,1,0:T(8,128)(2,1)} %maximum_select_fusion), calls=%async_computation.5 | async-start | bytes 524288 | tf_op jit(solution)/shard_map/all_to_all | solution.py:702
  201.4 0.1 collective-permute-start.10
  201.5 0.7 copy-done.11
  202.2 0.7 copy-done.12
  202.9 2.9 %out_grad.1 = bf16[16,24,768]{2,1,0:T(8,128)(2,1)} custom-call(s32[5]{0:T(128)} %stack.20.place_ref, bf16[128,768]{1,0:T(8,128)(2,1)} %get-tuple-element.97.attended_ref, bf16[128,768]{1,0:T(8,128)(2,1)} %copy-done.11, bf16[128,768]{1,0:T(8,128)(2,1)} %get-tuple-element.98.d_ref, bf16[128,768]{1,0:T(8,128)(2,1)} %copy-done.12), custom_call_target="tpu_custom_call" | custom-call | flops 2700000000 | bytes 3000000 | tf_op jit(solution)/shard_map/out_grad/pallas_call | solution.py:952
  205.8 5.8 %all-to-all-done.5 = bf16[16,32,192]{2,1,0:T(8,128)(2,1)S(1)} async-done(((bf16[16,32,192]{2,1,0:T(8,128)(2,1)}), bf16[16,32,192]{2,1,0:T(8,128)(2,1)S(1)}, u32[]{:S(2)}, u32[]{:S(2)}) %all-to-all-start.5) | async-done | bytes 196640 | tf_op jit(solution)/shard_map/all_to_all | solution.py:702
  211.6 3.8 %all-to-all-start.6 = ((bf16[16,24,768]{2,1,0:T(8,128)(2,1)}), bf16[16,24,768]{2,1,0:T(8,128)(2,1)S(1)}, u32[]{:S(2)}, u32[]{:S(2)}) async-start(bf16[16,24,768]{2,1,0:T(8,128)(2,1)} %out_grad.1), calls=%async_computation.6 | async-start | bytes 1179648 | tf_op jit(solution)/shard_map/all_to_all | solution.py:702
  215.4 10.7 %attention_backward.1 = (bf16[16,64,576]{2,1,0:T(8,128)(2,1)}, f32[3,32,128]{2,1,0:T(8,128)}) custom-call(s32[5]{0:T(128)} %stack.20.place_ref, bf16[3,512,1024]{2,1,0:T(8,128)(2,1)} %get-tuple-element.92.probs_ref, bf16[512,192]{1,0:T(8,128)(2,1)} %get-tuple-element.93.query_ref, bf16[1024,384]{1,0:T(8,128)(2,1)} %get-tuple-element.94.pair_ref, ...), custom_call_target="tpu_custom_call" | custom-call | flops 900000000 | bytes 1000000 | tf_op jit(solution)/shard_map/attention_backward/pallas_call | solution.py:965
  226.1 0.5 collective-permute-start.11
  226.7 4.3 %all-to-all-done.6 = bf16[16,24,768]{2,1,0:T(8,128)(2,1)S(1)} async-done(((bf16[16,24,768]{2,1,0:T(8,128)(2,1)}), bf16[16,24,768]{2,1,0:T(8,128)(2,1)S(1)}, u32[]{:S(2)}, u32[]{:S(2)}) %all-to-all-start.6) | async-done | bytes 589856 | tf_op jit(solution)/shard_map/all_to_all | solution.py:702
  231.0 0.1 convert_reduce_fusion.out_mine_ref
  231.1 0.1 collective-permute-start.9
  231.2 0.2 collective-permute-done.8.d_other_ref
  231.4 7.9 %input_side.1 = bf16[16,56,768]{2,1,0:T(8,128)(2,1)} custom-call(s32[5]{0:T(128)} %stack.20.place_ref, bf16[16,64,576]{2,1,0:T(8,128)(2,1)} %get-tuple-element.100.d_own_ref, bf16[16,64,576]{2,1,0:T(8,128)(2,1)} %collective-permute-done.8.d_other_ref, bf16[768,576]{1,0:T(8,128)(2,1)} %get-tuple-element.101.weight_ref, ...), custom_call_target="tpu_custom_call" | custom-call | flops 900000000 | bytes 1000000 | tf_op jit(solution)/shard_map/input_side/pallas_call | solution.py:987
  239.3 6.7 %all-to-all-start.7 = ((bf16[16,56,768]{2,1,0:T(8,128)(2,1)}), bf16[16,56,768]{2,1,0:T(8,128)(2,1)}, u32[]{:S(2)}, u32[]{:S(2)}) async-start(bf16[16,56,768]{2,1,0:T(8,128)(2,1)} %input_side.1), calls=%async_computation.7 | async-start | bytes 2752512 | tf_op jit(solution)/shard_map/all_to_all | solution.py:702
  246.0 5.2 %convert_add_fusion.1 = f32[768,1536]{1,0:T(8,128)} fusion(bf16[768,1536]{1,0:T(8,128)(2,1)} %collective-permute-done.10, bf16[768,1536]{1,0:T(8,128)(2,1)} %convolution_convert_fusion.1), kind=kLoop, calls=%fused_computation.1 | loop fusion | flops 3538944 | bytes 9437184 | tf_op jit(solution)/shard_map/add | solution.py:917
  251.3 4.5 %convert_add_fusion = f32[1536,768]{1,0:T(8,128)} fusion(bf16[1536,768]{1,0:T(8,128)(2,1)} %collective-permute-done.11, bf16[1536,768]{1,0:T(8,128)(2,1)S(1)} %convolution_convert_fusion), kind=kLoop, calls=%fused_computation | loop fusion | flops 3538944 | bytes 9437184 | tf_op jit(solution)/shard_map/add | solution.py:917
  255.8 21.1 %all-to-all-done.7.final_ref = bf16[16,56,768]{2,1,0:T(8,128)(2,1)} async-done(((bf16[16,56,768]{2,1,0:T(8,128)(2,1)}), bf16[16,56,768]{2,1,0:T(8,128)(2,1)}, u32[]{:S(2)}, u32[]{:S(2)}) %all-to-all-start.7) | async-done | bytes 1376288 | tf_op jit(solution)/shard_map/all_to_all | solution.py:702
  276.9 2.3 sums.1
  279.2 0.5 collective-permute-start.12
  279.7 1.4 collective-permute-done.14.small_other_ref
  281.1 0.6 copy-done.17
  281.7 0.0 copy-done.15
  281.7 0.1 copy-done.14
  281.8 2.6 input_grad.1
  (48 shorter events, 0.1 us)
Async XLA Ops:
  0.6 14.8 %copy-start = (bf16[48,768]{1,0:T(8,128)(2,1)S(1)}, bf16[48,768]{1,0:T(8,128)(2,1)}, u32[]{:S(2)}) copy-start(bf16[48,768]{1,0:T(8,128)(2,1)} %param.18) | copy-start | bytes 221188
  0.7 1.9 collective-permute-start
  1.2 1.4 collective-permute-start.1
  2.5 0.6 copy-start.18
  2.5 0.7 copy-start.10
  5.8 8.8 %copy-start.7 = (s32[2,64,1]{1,2,0:T(1,128)S(1)}, s32[2,64,1]{1,2,0:T(1,128)}, u32[]{:S(2)}) copy-start(s32[2,64,1]{1,2,0:T(1,128)} %param.25) | copy-start | bytes 1540
  5.8 39.1 %all-to-all-start = ((bf16[16,56,768]{2,1,0:T(8,128)(2,1)}), bf16[16,56,768]{2,1,0:T(8,128)(2,1)S(1)}, u32[]{:S(2)}, u32[]{:S(2)}) async-start(bf16[16,56,768]{2,1,0:T(8,128)(2,1)} %pack.1), calls=%async_computation | async-start | bytes 2752512 | tf_op jit(solution)/shard_map/all_to_all | solution.py:702
  44.9 11.7 %copy-start.2 = (bf16[16,56,768]{2,1,0:T(8,128)(2,1)}, bf16[16,56,768]{2,1,0:T(8,128)(2,1)S(1)}, u32[]{:S(2)}) copy-start(bf16[16,56,768]{2,1,0:T(8,128)(2,1)S(1)} %all-to-all-done.own_ref) | copy-start | bytes 4128772
  45.8 3.3 %collective-permute-start.2 = (bf16[16,56,768]{2,1,0:T(8,128)(2,1)S(1)}, bf16[16,56,768]{2,1,0:T(8,128)(2,1)}, u32[]{:S(2)}, u32[]{:S(2)}) collective-permute-start(bf16[16,56,768]{2,1,0:T(8,128)(2,1)S(1)} %all-to-all-done.own_ref), channel_id=1, source_target_pairs={{0,16},{16,0},{1,17},{17,1},{2,18},{18,2},{3,19},{19,3},{4,20},{20... | collective-permute-start | bytes 4128776 | tf_op jit(solution)/shard_map/ppermute | solution.py:745
  49.1 24.0 %all-to-all-start.1 = ((bf16[16,48,384]{2,1,0:T(8,128)(2,1)}), bf16[16,48,384]{2,1,0:T(8,128)(2,1)S(1)}, u32[]{:S(2)}, u32[]{:S(2)}) async-start(bf16[16,48,384]{2,1,0:T(8,128)(2,1)} %broadcast_in_dim.2), calls=%async_computation.1 | async-start | bytes 1179648 | tf_op jit(solution)/shard_map/all_to_all | solution.py:702
  73.1 18.4 %copy-start.4 = (bf16[16,48,384]{2,1,0:T(8,128)(2,1)}, bf16[16,48,384]{2,1,0:T(8,128)(2,1)S(1)}, u32[]{:S(2)}) copy-start(bf16[16,48,384]{2,1,0:T(8,128)(2,1)S(1)} %all-to-all-done.1) | copy-start | bytes 1769476
  73.1 18.4 %collective-permute-start.4 = (bf16[768,384]{1,0:T(8,128)(2,1)S(1)}, bf16[768,384]{1,0:T(8,128)(2,1)S(1)}, u32[]{:S(2)}, u32[]{:S(2)}) collective-permute-start(bf16[768,384]{1,0:T(8,128)(2,1)S(1)} %bitcast.23), channel_id=1, source_target_pairs={{0,16},{16,0},{1,17},{17,1},{2,18},{18,2},{3,19},{19,3},{4,20},{20... | collective-permute-start | bytes 1769480 | tf_op jit(solution)/shard_map/ppermute | solution.py:745
  73.1 17.0 %all-to-all-start.2 = ((bf16[16,32,192]{2,1,0:T(8,128)(2,1)}), bf16[16,32,192]{2,1,0:T(8,128)(2,1)S(1)}, u32[]{:S(2)}, u32[]{:S(2)}) async-start(bf16[16,32,192]{2,1,0:T(8,128)(2,1)} %bitcast.26), calls=%async_computation.2 | async-start | bytes 524288 | tf_op jit(solution)/shard_map/all_to_all | solution.py:702
  90.0 1.4 copy-start.5
  90.1 1.4 collective-permute-start.3
  91.5 0.7 copy-start.13
  91.5 0.8 copy-start.8
  148.2 4.5 %copy-start.1 = (bf16[16,64,768]{2,1,0:T(8,128)(2,1)S(1)}, bf16[16,64,768]{2,1,0:T(8,128)(2,1)}, u32[]{:S(2)}) copy-start(bf16[16,64,768]{2,1,0:T(8,128)(2,1)} %all_to_all.40.arrived_ref) | copy-start | bytes 4718596
  148.2 38.0 %all-to-all-start.4 = ((bf16[16,64,768]{2,1,0:T(8,128)(2,1)}), bf16[16,64,768]{2,1,0:T(8,128)(2,1)}, u32[]{:S(2)}, u32[]{:S(2)}) async-start(bf16[16,64,768]{2,1,0:T(8,128)(2,1)} %get-tuple-element.83), calls=%async_computation.4 | async-start | bytes 3145728 | tf_op jit(solution)/shard_map/all_to_all | solution.py:702
  152.7 1.4 copy-start.19
  154.2 2.8 copy-start.20
  186.2 4.6 %copy-start.9 = (bf16[128,768]{1,0:T(8,128)(2,1)S(1)}, bf16[128,768]{1,0:T(8,128)(2,1)}, u32[]{:S(2)}) copy-start(bf16[128,768]{1,0:T(8,128)(2,1)} %get-tuple-element.97.attended_ref) | copy-start | bytes 589828
  190.7 1.6 collective-permute-start.5
  190.8 10.7 %collective-permute-start.6 = (bf16[128,768]{1,0:T(8,128)(2,1)S(1)}, bf16[128,768]{1,0:T(8,128)(2,1)S(1)}, u32[]{:S(2)}, u32[]{:S(2)}) collective-permute-start(bf16[128,768]{1,0:T(8,128)(2,1)S(1)} %copy-done.9), channel_id=1, source_target_pairs={{0,16},{16,0},{1,17},{17,1},{2,18},{18,2},{3,19},{19,3},{4,20},{20... | collective-permute-start | bytes 589832 | tf_op jit(solution)/shard_map/ppermute | solution.py:745
  191.3 10.2 %collective-permute-start.7 = (bf16[128,768]{1,0:T(8,128)(2,1)}, bf16[128,768]{1,0:T(8,128)(2,1)S(1)}, u32[]{:S(2)}, u32[]{:S(2)}) collective-permute-start(bf16[128,768]{1,0:T(8,128)(2,1)} %get-tuple-element.98.d_ref), channel_id=1, source_target_pairs={{0,16},{16,0},{1,17},{17,1},{2,18},{18,2},{3,19},{19,3},{4,20},{20... | collective-permute-start | bytes 589832 | tf_op jit(solution)/shard_map/ppermute | solution.py:745
  194.1 17.5 %all-to-all-start.5 = ((bf16[16,32,192]{2,1,0:T(8,128)(2,1)}), bf16[16,32,192]{2,1,0:T(8,128)(2,1)S(1)}, u32[]{:S(2)}, u32[]{:S(2)}) async-start(bf16[16,32,192]{2,1,0:T(8,128)(2,1)} %maximum_select_fusion), calls=%async_computation.5 | async-start | bytes 524288 | tf_op jit(solution)/shard_map/all_to_all | solution.py:702
  201.4 44.6 %collective-permute-start.10 = (bf16[768,1536]{1,0:T(8,128)(2,1)}, bf16[768,1536]{1,0:T(8,128)(2,1)}, u32[]{:S(2)}, u32[]{:S(2)}) collective-permute-start(bf16[768,1536]{1,0:T(8,128)(2,1)} %convolution_convert_fusion.1), channel_id=1, source_target_pairs={{0,16},{16,0},{1,17},{17,1},{2,18},{18,2},{3,19},{19,3},{4,20},{20... | collective-permute-start | bytes 7077896 | tf_op jit(solution)/shard_map/ppermute | solution.py:745
  201.5 0.7 copy-start.11
  202.2 0.7 copy-start.12
  211.6 3.8 %copy-start.3 = (bf16[16,32,192]{2,1,0:T(8,128)(2,1)}, bf16[16,32,192]{2,1,0:T(8,128)(2,1)S(1)}, u32[]{:S(2)}) copy-start(bf16[16,32,192]{2,1,0:T(8,128)(2,1)S(1)} %all-to-all-done.5) | copy-start | bytes 589828
  211.6 19.4 %all-to-all-start.6 = ((bf16[16,24,768]{2,1,0:T(8,128)(2,1)}), bf16[16,24,768]{2,1,0:T(8,128)(2,1)S(1)}, u32[]{:S(2)}, u32[]{:S(2)}) async-start(bf16[16,24,768]{2,1,0:T(8,128)(2,1)} %out_grad.1), calls=%async_computation.6 | async-start | bytes 1179648 | tf_op jit(solution)/shard_map/all_to_all | solution.py:702
  226.1 5.2 %collective-permute-start.8 = (bf16[16,64,576]{2,1,0:T(8,128)(2,1)}, bf16[16,64,576]{2,1,0:T(8,128)(2,1)}, u32[]{:S(2)}, u32[]{:S(2)}) collective-permute-start(bf16[16,64,576]{2,1,0:T(8,128)(2,1)} %get-tuple-element.100.d_own_ref), channel_id=1, source_target_pairs={{0,16},{16,0},{1,17},{17,1},{2,18},{18,2},{3,19},{19,3},{4,20},{20... | collective-permute-start | bytes 3538952 | tf_op jit(solution)/shard_map/ppermute | solution.py:745
  226.1 25.1 %collective-permute-start.11 = (bf16[1536,768]{1,0:T(8,128)(2,1)S(1)}, bf16[1536,768]{1,0:T(8,128)(2,1)}, u32[]{:S(2)}, u32[]{:S(2)}) collective-permute-start(bf16[1536,768]{1,0:T(8,128)(2,1)S(1)} %convolution_convert_fusion), channel_id=1, source_target_pairs={{0,16},{16,0},{1,17},{17,1},{2,18},{18,2},{3,19},{19,3},{4,20},{20... | collective-permute-start | bytes 7077896 | tf_op jit(solution)/shard_map/ppermute | solution.py:745
  231.1 8.2 %copy-start.6 = (f32[24,768]{1,0:T(8,128)}, f32[24,768]{1,0:T(8,128)S(1)}, u32[]{:S(2)}) copy-start(f32[24,768]{1,0:T(8,128)S(1)} %convert_reduce_fusion.out_mine_ref) | copy-start | bytes 221188
  231.1 8.2 %collective-permute-start.9 = (f32[24,768]{1,0:T(8,128)S(1)}, f32[24,768]{1,0:T(8,128)S(1)}, u32[]{:S(2)}, u32[]{:S(2)}) collective-permute-start(f32[24,768]{1,0:T(8,128)S(1)} %convert_reduce_fusion.out_mine_ref), channel_id=1, source_target_pairs={{0,16},{16,0},{1,17},{17,1},{2,18},{18,2},{3,19},{19,3},{4,20},{20... | collective-permute-start | bytes 221192 | tf_op jit(solution)/shard_map/ppermute | solution.py:745
  239.3 12.0 %copy-start.16 = (f32[24,768]{1,0:T(8,128)}, f32[24,768]{1,0:T(8,128)S(1)}, u32[]{:S(2)}) copy-start(f32[24,768]{1,0:T(8,128)S(1)} %collective-permute-done.9.out_other_ref) | copy-start | bytes 221188
  239.3 37.6 %all-to-all-start.7 = ((bf16[16,56,768]{2,1,0:T(8,128)(2,1)}), bf16[16,56,768]{2,1,0:T(8,128)(2,1)}, u32[]{:S(2)}, u32[]{:S(2)}) async-start(bf16[16,56,768]{2,1,0:T(8,128)(2,1)} %input_side.1), calls=%async_computation.7 | async-start | bytes 2752512 | tf_op jit(solution)/shard_map/all_to_all | solution.py:702
  279.2 1.9 collective-permute-start.13
  279.2 1.9 collective-permute-start.12
  279.7 1.4 collective-permute-start.14
  281.1 0.6 copy-start.17
  281.1 0.6 copy-start.15
  281.1 0.7 copy-start.14

commit v2 on v1

--- a/solution.py
+++ b/solution.py
@@ -30,10 +30,8 @@
 
 def pack_kernel(
     place_ref,
-    x_ref,
-    x_other_ref,
-    seg_ref,
-    seg_other_ref,
+    marks_ref,
+    marks_other_ref,
     query_ref,
     key_ref,
     value_ref,
@@ -45,11 +43,11 @@
     weights,
     small,
     *,
-    half,
     split,
 ):
-    seqs, rows, width = x_ref.shape
-    shard = query_ref.shape[0]
+    seqs = marks_ref.shape[0]
+    rows = marks_ref.shape[1] // 2
+    shard, width = query_ref.shape
     part = shard // 2
     head_width = width // HEAD_GROUPS
     base = 3 * head_width
@@ -74,40 +72,22 @@
         small[2 + EXPERTS : 3 + EXPERTS, k * heads : (k + 1) * heads] = table_ref[
             k : k + 1, :
         ].astype(f32)
-    x_at = pl.ds(pl.multiple_of(place_ref[0], half), half)
     for c in range(2):
-        x, seg = (x_ref, seg_ref) if c == 0 else (x_other_ref, seg_other_ref)
+        marks = marks_ref if c == 0 else marks_other_ref
         first = (place_ref[3] if c == 0 else seqs - place_ref[3]) * per_seq
         for l in range(seqs):
-            small[3 + EXPERTS : 4 + EXPERTS, 0:rows] = seg[l : l + 1, :].astype(f32)
+            small[3 + EXPERTS : 4 + EXPERTS, 0 : 2 * rows] = marks[l : l + 1, :].astype(f32)
             for k in range(per_seq):
                 at = first + l * per_seq + k
-                send_ref[at, 0:half, :] = x[l, x_at, :]
-                send_ref[at, half:, 0:base] = weights[k // split].astype(bf16)
-                send_ref[at, half:, base:] = small[...].astype(bf16)
+                send_ref[at, :, 0:base] = weights[k // split].astype(bf16)
+                send_ref[at, :, base:] = small[...].astype(bf16)
 
 
 def forward_kernel(
     place_ref,
     own_ref,
     other_ref,
-    attended_ref,
-    probs_ref,
-    query_ref,
-    pair_ref,
-    normed_all,
-    weight_ref,
-    gain_one_ref,
-    gain_two_ref,
-    router_ref,
-    weights,
-    project,
-    scores,
-    strip,
-    seg_key_ref,
-    seg_query_ref,
-    table_ref,
-    *,
+    *refs,
     groups,
     half,
     rows,
@@ -116,8 +96,21 @@
     shard,
     all_heads,
 ):
-    core_at = pl.multiple_of(place_ref[0], half)
-    other_at = pl.multiple_of(half - place_ref[0], half)
+    chips = (len(refs) - 17) // 4
+    x_refs = refs[: 2 * chips]
+    (
+        probs_ref,
+        query_ref,
+        pair_ref,
+        normed_all,
+        weight_ref,
+        gain_one_ref,
+        gain_two_ref,
+        router_ref,
+        routes_ref,
+    ) = refs[2 * chips : 2 * chips + 9]
+    pieces = refs[2 * chips + 9 : -8]
+    weights, project, scores, strip, seg_key_ref, seg_query_ref, table_ref, attended_ref = refs[-8:]
     query_at = pl.multiple_of(place_ref[1], sub)
     width = gain_one_ref.shape[1]
     length = groups * rows
@@ -133,7 +126,7 @@
     seg_pick = seg_col == seg_row + place_ref[1]
     for p in range(groups):
         at = slice(p * shard, (p + 1) * shard)
-        small = own_ref[p, half:, base:].astype(f32)
+        small = own_ref[p, :, base:].astype(f32)
         gain_one_ref[:, at] = small[0:1, 0:shard]
         gain_two_ref[:, at] = small[1:2, 0:shard]
         router_ref[:, at] = small[2 : 2 + EXPERTS, 0:shard]
@@ -142,6 +135,7 @@
                 2 + EXPERTS : 3 + EXPERTS, k * all_heads : (k + 1) * all_heads
             ]
         seg = small[3 + EXPERTS : 4 + EXPERTS, 0:rows]
+        routes_ref[p : p + 1, :] = small[3 + EXPERTS : 4 + EXPERTS, rows : 2 * rows]
         seg_key_ref[:, p * rows : (p + 1) * rows] = seg
         seg_query_ref[p * sub : (p + 1) * sub, :] = jnp.sum(
             jnp.where(seg_pick, jnp.broadcast_to(seg, (sub, rows)), 0.0), axis=1, keepdims=True
@@ -152,9 +146,9 @@
         @pl.when(place_ref[4] == c)
         def _():
             at = slice(c * part, (c + 1) * part)
-            weights[:, at, :] = own_ref[:, half:, 0:base].astype(f32)
+            weights[:, at, :] = own_ref[:, :, 0:base].astype(f32)
             at = slice((1 - c) * part, (2 - c) * part)
-            weights[:, at, :] = other_ref[:, half:, 0:base].astype(f32)
+            weights[:, at, :] = other_ref[:, :, 0:base].astype(f32)
 
     weight_ref[...] = weights[...].reshape(width, base).astype(bf16)
     gain = gain_one_ref[...]
@@ -165,12 +159,11 @@
         scale = lax.rsqrt(jnp.mean(x * x, axis=-1, keepdims=True) + EPS)
         return ((x * scale) * gain).astype(bf16)
 
-    def norm_step(p, carry):
-        normed_all[p, pl.ds(core_at, half), :] = norm(own_ref[p, 0:half, :])
-        normed_all[p, pl.ds(other_at, half), :] = norm(other_ref[p, 0:half, :])
-        return carry
-
-    lax.fori_loop(0, groups, norm_step, 0, unroll=2)
+    for k in range(chips):
+        for c in range(2):
+            at = 2 * (place_ref[4] ^ c) * chips + (place_ref[5] ^ k)
+            for b in range(2):
+                normed_all[at + b * chips] = norm(x_refs[c * chips + k][b])
     chunk = 4
 
     def project_step(c, carry):
@@ -226,6 +219,13 @@
         attended_ref[:, at : at + head_dim] = dot(
             probs_ref[h], pair_ref[:, head_width + at : head_width + at + head_dim]
         ).astype(bf16)
+    for k in range(len(pieces) // 2):
+        for c in range(2):
+            at = 2 * (place_ref[4] ^ c) * (len(pieces) // 2) + (place_ref[5] ^ k)
+            for b in range(2):
+                block = at + b * (len(pieces) // 2)
+                rows_at = pl.ds(pl.multiple_of(block * sub, sub), sub)
+                pieces[2 * k + c][b] = attended_ref[rows_at, :]
 
 
 def backward_kernel(
@@ -233,21 +233,22 @@
     probs_ref,
     query_ref,
     pair_ref,
-    grad_ref,
-    d_all_ref,
-    table_ref,
-    scores,
-    low,
-    strip,
-    flipped,
-    d_query,
-    *,
+    *refs,
     groups,
     half,
     rows,
     sub,
     head_dim,
 ):
+    pieces = refs[:-8]
+    d_all_ref, table_ref, scores, low, strip, flipped, d_query, grad_ref = refs[-8:]
+    for k in range(len(pieces) // 2):
+        for c in range(2):
+            at = 2 * (place_ref[4] ^ c) * (len(pieces) // 2) + (place_ref[5] ^ k)
+            for b in range(2):
+                block = at + b * (len(pieces) // 2)
+                rows_at = pl.ds(pl.multiple_of(block * sub, sub), sub)
+                grad_ref[rows_at, :] = pieces[2 * k + c][b]
     query_at = pl.multiple_of(place_ref[1], sub)
     length = groups * rows
     head_width = query_ref.shape[1]
@@ -321,48 +322,62 @@
     lax.fori_loop(0, groups, place_step, 0)
 
 
-def last_kernel(
+def rows_kernel(
     place_ref,
     d_own_ref,
     d_other_ref,
     weight_ref,
     normed_ref,
-    own_ref,
+    gain_ref,
+    rows_ref,
+    d_sum,
+    gain_sum,
+    *,
+    half,
+):
+    core_at = pl.multiple_of(place_ref[0], half)
+    groups, _, base = d_own_ref.shape
+    chips = rows_ref.shape[0]
+    width = weight_ref.shape[0]
+    d_sum[...] = (d_own_ref[...].astype(f32) + d_other_ref[...].astype(f32)).astype(bf16)
+    gain_sum[...] = jnp.zeros_like(gain_sum)
+    chunk = 4
+
+    def normed_step(c, carry):
+        at = pl.ds(c * chunk, chunk)
+        block = d_sum[at, pl.ds(core_at, half), :].reshape(chunk * half, base)
+        d_normed = dot(block, weight_ref[...], ((1,), (1,)))
+        normed = normed_ref[at, pl.ds(core_at, half), :].astype(f32).reshape(chunk * half, width)
+        gain_sum[...] += jnp.sum(d_normed * normed, axis=0, keepdims=True)
+        d_rows = d_normed.reshape(chunk, half, width).astype(bf16)
+        for k in range(chunk):
+            p = c * chunk + k
+            rows_ref[lax.rem(p, chips), lax.div(p, chips)] = d_rows[k]
+        return carry
+
+    lax.fori_loop(0, groups // chunk, normed_step, 0)
+    gain_sum[...] = gain_sum[...] / gain_ref[...]
+
+
+def weight_kernel(
+    place_ref,
+    d_sum,
+    normed_ref,
+    gain_sum,
     gain_two_ref,
     router_ref,
     table_ref,
     last_ref,
-    d_sum,
     w_grad,
-    gain_sum,
     small,
     *,
-    groups,
-    half,
-    rows,
     shard,
     all_heads,
 ):
-    core_at = pl.multiple_of(place_ref[0], half)
-    width = weight_ref.shape[0]
-    base = weight_ref.shape[1]
+    groups, rows, width = normed_ref.shape
+    base = d_sum.shape[2]
     part = shard // 2
     length = groups * rows
-    d_sum[...] = (d_own_ref[...].astype(f32) + d_other_ref[...].astype(f32)).astype(bf16)
-    gain_sum[...] = jnp.zeros_like(gain_sum)
-    chunk = 4
-
-    def normed_step(c, carry):
-        at = pl.ds(c * chunk, chunk)
-        block = d_sum[at, pl.ds(core_at, half), :].reshape(chunk * half, base)
-        d_normed = dot(block, weight_ref[...], ((1,), (1,)))
-        x = own_ref[at, 0:half, :].astype(f32).reshape(chunk * half, width)
-        unit = x * lax.rsqrt(jnp.mean(x * x, axis=-1, keepdims=True) + EPS)
-        gain_sum[...] += jnp.sum(d_normed * unit, axis=0, keepdims=True)
-        last_ref[at, 0:half, :] = d_normed.reshape(chunk, half, width).astype(bf16)
-        return carry
-
-    lax.fori_loop(0, groups // chunk, normed_step, 0)
     w_grad[...] = dot(
         normed_ref[...].reshape(length, width), d_sum[...].reshape(length, base), ((0,), (0,))
     ).reshape(groups, shard, base)
@@ -370,7 +385,7 @@
 
         @pl.when(place_ref[4] == c)
         def _():
-            last_ref[:, half:, 0:base] = w_grad[:, c * part : (c + 1) * part, :].astype(bf16)
+            last_ref[:, :, 0:base] = w_grad[:, c * part : (c + 1) * part, :].astype(bf16)
 
     heads = table_ref.shape[0]
     head_col = lax.broadcasted_iota(jnp.int32, (32, all_heads), 1)
@@ -389,7 +404,7 @@
             small[p, 2 + EXPERTS : 3 + EXPERTS, k * all_heads : (k + 1) * all_heads] = table[
                 p * table_rows + k : p * table_rows + k + 1, :
             ]
-    last_ref[:, half:, base:] = small[...].astype(bf16)
+    last_ref[:, :, base:] = small[...].astype(bf16)
 
 
 def out_grad_kernel(
@@ -407,58 +422,85 @@
             out_ref[...] = total[:, c * part : (c + 1) * part, :].astype(bf16)
 
 
-def sum_kernel(
-    place_ref, final_ref, keep_ref, give_ref, four_ref, low_ref, small_ref, *, half, seqs
-):
-    groups, _, width = final_ref.shape
-    part = four_ref.shape[1]
+def sum_kernel(final_ref, four_ref, low_ref, small_ref, *, seqs):
+    groups, part, width = final_ref.shape
     base = width - small_ref.shape[1]
     head_width = base // 3
-    per_seq = groups // (2 * seqs)
-    split = per_seq // HEAD_GROUPS
-    mine = place_ref[3]
-    yours = seqs - mine
-    for l in range(seqs):
-
-        def total(first):
-            value = final_ref[first, 0:half, :].astype(f32)
-            for k in range(1, per_seq):
-                value = value + final_ref[first + k, 0:half, :].astype(f32)
-            return value
-
-        keep_ref[l] = total((mine + l) * per_seq)
-        give_ref[l] = total((yours + l) * per_seq).astype(bf16)
+    split = groups // (2 * seqs * HEAD_GROUPS)
     for g in range(HEAD_GROUPS):
         grad = jnp.zeros((part, base), f32)
         for s in range(2 * seqs):
             for t in range(split):
-                grad = grad + final_ref[(s * HEAD_GROUPS + g) * split + t, half:, 0:base].astype(
-                    f32
-                )
+                at = (s * HEAD_GROUPS + g) * split + t
+                grad = grad + final_ref[at, :, 0:base].astype(f32)
         for i in range(3):
             four_ref[i, :, g * head_width : (g + 1) * head_width] = grad[
                 :, i * head_width : (i + 1) * head_width
             ]
     low_ref[...] = four_ref[...].astype(bf16)
-    small = final_ref[0, half:, base:].astype(f32)
+    small = final_ref[0, :, base:].astype(f32)
     for p in range(1, groups):
-        small = small + final_ref[p, half:, base:].astype(f32)
+        small = small + final_ref[p, :, base:].astype(f32)
     small_ref[...] = small
+
+
+def total_kernel(place_ref, rows_ref, keep_ref, give_ref):
+    blocks = keep_ref.shape[0]
+    for b in range(blocks):
+
+        def total(w):
+            value = rows_ref[0, w].astype(f32)
+            for j in range(1, rows_ref.shape[0]):
+                value = value + rows_ref[j, w].astype(f32)
+            return value
+
+        keep_ref[b] = total(place_ref[4] * blocks + b)
+        give_ref[b] = total((1 - place_ref[4]) * blocks + b).astype(bf16)
+
+
+def token_kernel(
+    place_ref,
+    x_ref,
+    d_hidden_ref,
+    gain_ref,
+    keep_ref,
+    given_ref,
+    first_ref,
+    second_ref,
+    d_normed_ref,
+    grad_ref,
+    *,
+    half,
+):
+    blocks, rows, width = x_ref.shape
+    core_at = pl.multiple_of(place_ref[0], half)
+    other_at = pl.multiple_of(half - place_ref[0], half)
+    d_normed_ref[:, pl.ds(core_at, half), :] = keep_ref[...]
+    d_normed_ref[:, pl.ds(other_at, half), :] = given_ref[...].astype(f32)
+    d_normed = d_normed_ref[...].reshape(blocks * rows, width)
+    x = x_ref[...].reshape(blocks * rows, width).astype(f32)
+    scale = lax.rsqrt(jnp.mean(x * x, axis=-1, keepdims=True) + EPS)
+    unit = x * scale
+    d_unit = d_normed * gain_ref[...]
+    grad = scale * (d_unit - unit * jnp.mean(d_unit * unit, axis=-1, keepdims=True))
+    grad_ref[...] = (d_hidden_ref[...] + grad).reshape(blocks, rows, width)
+    first_ref[...] = grad_ref[place_ref[7]].astype(bf16)
+    second_ref[...] = grad_ref[1 - place_ref[7]].astype(bf16)
 
 
 def input_kernel(
     place_ref,
-    keep_ref,
-    given_ref,
+    grad_first_ref,
+    grad_second_ref,
+    out_first_ref,
+    out_second_ref,
     four_ref,
     other_ref,
     out_mine_ref,
     out_other_ref,
     small_ref,
     small_other_ref,
-    x_ref,
-    d_hidden_ref,
-    gain_ref,
+    output_ref,
     input_ref,
     query_ref,
     key_ref,
@@ -468,10 +510,11 @@
     gain_one_ref,
     gain_two_ref,
     router_ref,
-    d_normed_ref,
-    *,
-    half,
 ):
+    output_ref[place_ref[7]] = out_first_ref[...]
+    output_ref[1 - place_ref[7]] = out_second_ref[...]
+    input_ref[place_ref[7]] = grad_first_ref[...].astype(f32)
+    input_ref[1 - place_ref[7]] = grad_second_ref[...].astype(f32)
     small = small_ref[...] + small_other_ref[...]
     shard = gain_one_ref.shape[1]
     heads = table_ref.shape[1]
@@ -480,19 +523,7 @@
     router_ref[...] = small[2 : 2 + EXPERTS, 0:shard]
     for k in range(table_ref.shape[0]):
         table_ref[k : k + 1, :] = small[2 + EXPERTS : 3 + EXPERTS, k * heads : (k + 1) * heads]
-    core_at = pl.multiple_of(place_ref[0], half)
-    other_at = pl.multiple_of(half - place_ref[0], half)
-    seqs, rows, width = x_ref.shape
     part = four_ref.shape[1]
-    d_normed_ref[:, pl.ds(core_at, half), :] = keep_ref[...]
-    d_normed_ref[:, pl.ds(other_at, half), :] = given_ref[...].astype(f32)
-    d_normed = d_normed_ref[...].reshape(seqs * rows, width)
-    x = x_ref[...].reshape(seqs * rows, width).astype(f32)
-    scale = lax.rsqrt(jnp.mean(x * x, axis=-1, keepdims=True) + EPS)
-    unit = x * scale
-    d_unit = d_normed * gain_ref[...]
-    grad = scale * (d_unit - unit * jnp.mean(d_unit * unit, axis=-1, keepdims=True))
-    input_ref[...] = (d_hidden_ref[...] + grad).reshape(seqs, rows, width)
     for c in range(2):
 
         @pl.when(place_ref[4] == c)
@@ -508,44 +539,55 @@
 
 def middle_kernel(
     place_ref,
-    back_ref,
-    swapped_ref,
     x_ref,
     out_ref,
     out_other_ref,
     gain_ref,
     router_ref,
-    routes_ref,
-    cotangent_ref,
-    send_ref,
-    attended_ref,
-    hidden_ref,
-    normed_ref,
-    probs_ref,
-    spread_ref,
-    attended,
-    *,
+    routes_in_ref,
+    first_ref,
+    second_ref,
+    *refs,
     half,
     sub,
     split,
     few,
     share,
 ):
-    seqs, rows, width = attended.shape
-    tokens = seqs * rows
-    head_width = back_ref.shape[2]
-    core_at = place_ref[0]
-    first = place_ref[3]
-    for l in range(seqs):
-        for g in range(HEAD_GROUPS):
-            lanes = slice(g * head_width, (g + 1) * head_width)
-            for t in range(split):
-                here = pl.multiple_of(core_at + t * sub, sub)
-                there = pl.multiple_of(half - core_at + t * sub, sub)
-                at = (l * HEAD_GROUPS + g) * split + t
-                kept = first * (HEAD_GROUPS * split) + at
-                attended[l, pl.ds(here, sub), lanes] = back_ref[kept]
-                attended[l, pl.ds(there, sub), lanes] = swapped_ref[at]
+    pieces = refs[:-11]
+    (
+        send_ref,
+        attended_ref,
+        hidden_ref,
+        normed_ref,
+        probs_ref,
+        spread_ref,
+        cotangent_ref,
+        routes_ref,
+        attended,
+        stage,
+        routes_turned,
+    ) = refs[-11:]
+    blocks, rows, width = attended.shape
+    tokens = blocks * rows
+    head_width = width // HEAD_GROUPS
+    for k in range(len(pieces) // 2):
+        for c in range(2):
+            stage[place_ref[5] ^ k, place_ref[4] ^ c] = pieces[2 * k + c][...]
+    for g in range(HEAD_GROUPS):
+        lanes = slice(g * head_width, (g + 1) * head_width)
+        for t in range(split):
+            for c in range(2):
+                at = c * half + t * sub
+                attended[:, at : at + sub, lanes] = stage[g * split + t, c]
+    cotangent_ref[place_ref[7]] = first_ref[...]
+    cotangent_ref[1 - place_ref[7]] = second_ref[...]
+    routes_turned[...] = routes_in_ref[...].T
+    block_col = lax.broadcasted_iota(jnp.int32, routes_turned.shape, 1)
+    for b in range(blocks):
+        mine = block_col == place_ref[6] + b * (len(pieces) // 2)
+        column = jnp.sum(jnp.where(mine, routes_turned[...], 0.0), axis=1, keepdims=True)
+        routes_ref[b * rows : (b + 1) * rows, :] = column.astype(jnp.int32)
     low = attended[...].reshape(tokens, width)
     attended_ref[...] = low
     out_half = width // 2
@@ -618,25 +660,28 @@
     router_ref,
     out_ref,
     out_other_ref,
-    output_ref,
-    d_hidden_ref,
-    d_branch_ref,
-    keep_ref,
-    give_ref,
-    router_grad_ref,
-    gain_grad_ref,
-    d_attended,
-    *,
+    *refs,
     half,
     sub,
     split,
     few,
     share,
 ):
-    seqs, rows, width = output_ref.shape
+    pieces = refs[:-9]
+    (
+        first_ref,
+        second_ref,
+        d_hidden_ref,
+        d_branch_ref,
+        router_grad_ref,
+        gain_grad_ref,
+        output,
+        d_attended,
+        stage,
+    ) = refs[-9:]
+    seqs, rows, width = cotangent_ref.shape
     tokens = seqs * rows
-    head_width = keep_ref.shape[2]
-    core_at = place_ref[0]
+    head_width = width // HEAD_GROUPS
     spread = spread_ref[...]
 
     def collect(at):
@@ -659,7 +704,9 @@
         routes_ref[...] == lax.broadcasted_iota(jnp.int32, (tokens, EXPERTS), 1)
     ).astype(f32)
     gate = jnp.sum(probs * picked, axis=-1, keepdims=True)
-    output_ref[...] = (hidden + gate * expert_out).astype(bf16).reshape(seqs, rows, width)
+    output[...] = (hidden + gate * expert_out).astype(bf16).reshape(seqs, rows, width)
+    first_ref[...] = output[place_ref[7]]
+    second_ref[...] = output[1 - place_ref[7]]
     d_final = cotangent_ref[...].reshape(tokens, width).astype(f32)
     d_gate = jnp.sum(d_final * expert_out, axis=-1, keepdims=True)
     d_logits = gate * (picked - probs) * d_gate
@@ -687,15 +734,15 @@
     d_low = dot(d_branch_ref[:, pl.ds(here, out_half)], out_ref[...], ((1,), (1,)))
     d_low = d_low + dot(d_branch_ref[:, pl.ds(there, out_half)], out_other_ref[...], ((1,), (1,)))
     d_attended[...] = d_low.astype(bf16).reshape(seqs, rows, width)
-    for l in range(seqs):
-        for g in range(HEAD_GROUPS):
-            lanes = slice(g * head_width, (g + 1) * head_width)
-            for t in range(split):
-                here = pl.multiple_of(core_at + t * sub, sub)
-                there = pl.multiple_of(half - core_at + t * sub, sub)
-                at = (l * HEAD_GROUPS + g) * split + t
-                keep_ref[at] = d_attended[l, pl.ds(here, sub), lanes]
-                give_ref[at] = d_attended[l, pl.ds(there, sub), lanes]
+    for g in range(HEAD_GROUPS):
+        lanes = slice(g * head_width, (g + 1) * head_width)
+        for t in range(split):
+            for c in range(2):
+                at = c * half + t * sub
+                stage[g * split + t, c] = d_attended[:, at : at + sub, lanes]
+    for k in range(len(pieces) // 2):
+        for c in range(2):
+            pieces[2 * k + c][...] = stage[place_ref[5] ^ k, place_ref[4] ^ c]
 
 
 def exchange(value):
@@ -744,6 +791,30 @@
     def swap(value):
         return lax.ppermute(value, "rep", pairs)
 
+    chips = HEAD_GROUPS * split
+
+    def plane(value, k, c):
+        if k == 0 and c == 0:
+            return value
+        moves = [
+            (r * groups + q, (r ^ c) * groups + (q ^ k)) for r in range(reps) for q in range(groups)
+        ]
+        return lax.ppermute(value, ("rep", "sq"), moves)
+
+    def plane_all(pieces):
+        return [plane(pieces[2 * k + c], k, c) for k in range(chips) for c in range(2)]
+
+    def to_tokens(value, turn, back):
+        moves = []
+        for r in range(reps):
+            for p in range(groups):
+                w = p // chips
+                s = seqs * (r % 2) + (w + turn) % 2
+                there = (r // 2 * 2 + w // 2) * groups + s * chips + p % chips
+                here = r * groups + p
+                moves.append((there, here) if back else (here, there))
+        return lax.ppermute(value, ("rep", "sq"), moves)
+
     def by_core(own, other, axis):
         return jnp.where(
             first,
@@ -776,14 +847,29 @@
     limit = pltpu.CompilerParams(vmem_limit_bytes=56 * 1024 * 1024)
     spare = width - 3 * head_width
     query_at = core * half + (me % split) * sub
-    place = jnp.stack([core * half, query_at, group_at * group_heads, core * seqs, core])
+    inner = me % chips
+    first_block = 2 * core * chips + inner
+    parity = (me // chips) % 2
+    place = jnp.stack(
+        [
+            core * half,
+            query_at,
+            group_at * group_heads,
+            core * seqs,
+            core,
+            inner,
+            first_block,
+            parity,
+        ]
+    )
     place = place.astype(jnp.int32)
     shard_table = bucket_rows * heads
+    marks = jnp.concatenate([segments, routes.reshape(seqs, rows)], axis=1)
     send = pl.pallas_call(
-        partial(pack_kernel, half=half, split=split),
+        partial(pack_kernel, split=split),
         name="pack",
-        out_shape=jax.ShapeDtypeStruct((groups, half + part, width), bf16),
-        in_specs=[smem] + [vmem] * 11,
+        out_shape=jax.ShapeDtypeStruct((groups, part, width), bf16),
+        in_specs=[smem] + [vmem] * 9,
         out_specs=vmem,
         scratch_shapes=[
             pltpu.VMEM((HEAD_GROUPS, part, 3 * head_width), f32),
@@ -793,10 +879,8 @@
         cost_estimate=cost(3),
     )(
         place,
-        inputs,
-        swap(inputs),
-        segments,
-        swap(segments),
+        marks,
+        swap(marks),
         w_query,
         w_key,
         w_value,
@@ -805,19 +889,30 @@
         w_router.T,
         table,
     )
+    def half_at(value, turn):
+        return lax.dynamic_index_in_dim(value, (parity + turn) % 2, 0, keepdims=False)
+
+    x_first, x_second = [to_tokens(half_at(inputs, turn), turn, False) for turn in range(2)]
+    send, x_first, x_second = lax.optimization_barrier((send, x_first, x_second))
+    x_tokens = jnp.where(
+        parity == 0, jnp.stack([x_first, x_second]), jnp.stack([x_second, x_first])
+    )
+    x_parts = [x_tokens] + [plane(x_tokens, k, 0) for k in range(1, chips)]
     own = exchange(send)
     out_half = mine(w_out, 1, width // 2)
     out_send = jnp.broadcast_to(out_half[None], (groups, shard, width // 2))
-    own, out_send, place, routes_flat = lax.optimization_barrier(
-        (own, out_send, place, routes.reshape(tokens, 1))
-    )
+    first, second = [to_tokens(half_at(cotangent, turn), turn, False) for turn in range(2)]
+    own, out_send, place, x_parts, first, second = lax.optimization_barrier(
+        (own, out_send, place, x_parts, first, second)
+    )
+    x_parts = x_parts + [swap(v) for v in x_parts]
     other, out_send = lax.optimization_barrier((swap(own), out_send))
     out_mine = exchange(out_send)
     queries_count = groups * sub
     tile = (LANES // rows) * sub
     sizes = dict(groups=groups, half=half, rows=rows, sub=sub, head_dim=head_dim)
+    piece = jax.ShapeDtypeStruct((2, sub, head_width), bf16)
     (
-        attended_part,
         probs,
         queries,
         pair,
@@ -826,11 +921,12 @@
         gain_one_full,
         gain_two_full,
         router_full,
+        routes_all,
+        *attended_parts,
     ) = pl.pallas_call(
         partial(forward_kernel, shard=shard, all_heads=heads, **sizes),
         name="attention_forward",
         out_shape=(
-            jax.ShapeDtypeStruct((queries_count, head_width), bf16),
             jax.ShapeDtypeStruct((group_heads, queries_count, length), bf16),
             jax.ShapeDtypeStruct((queries_count, head_width), bf16),
             jax.ShapeDtypeStruct((length, 2 * head_width), bf16),
@@ -839,9 +935,11 @@
             jax.ShapeDtypeStruct((1, width), f32),
             jax.ShapeDtypeStruct((1, width), f32),
             jax.ShapeDtypeStruct((EXPERTS, width), f32),
-        ),
-        in_specs=[smem] + [vmem] * 2,
-        out_specs=[vmem] * 9,
+            jax.ShapeDtypeStruct((groups, rows), f32),
+        )
+        + (piece,) * (2 * chips),
+        in_specs=[smem] + [vmem] * (2 + 2 * chips),
+        out_specs=[vmem] * (9 + 2 * chips),
         scratch_shapes=[
             pltpu.VMEM((groups, shard, 3 * head_width), f32),
             pltpu.VMEM((groups, rows, 3 * head_width), bf16),
@@ -850,18 +948,27 @@
             pltpu.VMEM((1, length), f32),
             pltpu.VMEM((queries_count, 1), f32),
             pltpu.VMEM((32, heads), f32),
+            pltpu.VMEM((queries_count, head_width), bf16),
         ],
         compiler_params=limit,
         cost_estimate=cost(60),
-    )(place, own, other)
-    attended_part, out_mine = lax.optimization_barrier((attended_part, out_mine))
-    back = exchange(attended_part.reshape(groups, sub, head_width))
+    )(place, own, other, *x_parts)
+    attended_parts, out_mine = lax.optimization_barrier((attended_parts, out_mine))
+    back = plane_all(attended_parts)
     out_mine = out_mine.reshape(width, width // 2)
     out_yours = swap(out_mine)
-    back_given = swap(yours(back, 0, groups // 2))
     few = CAP
     pieces = dict(half=half, sub=sub, split=split, few=few)
-    buffer, attended, hidden, normed_two, router_probs, spread = pl.pallas_call(
+    (
+        buffer,
+        attended,
+        hidden,
+        normed_two,
+        router_probs,
+        spread,
+        cotangent_tokens,
+        routes_tokens,
+    ) = pl.pallas_call(
         partial(middle_kernel, share=share, **pieces),
         name="router_and_dispatch",
         out_shape=(
@@ -871,23 +978,29 @@
             jax.ShapeDtypeStruct((tokens, width), bf16),
             jax.ShapeDtypeStruct((tokens, EXPERTS), f32),
             jax.ShapeDtypeStruct((tokens, EXPERTS * CAP), bf16),
+            jax.ShapeDtypeStruct((seqs, rows, width), bf16),
+            jax.ShapeDtypeStruct((tokens, 1), jnp.int32),
         ),
-        in_specs=[smem] + [vmem] * 9,
-        out_specs=[vmem] * 6,
-        scratch_shapes=[pltpu.VMEM((seqs, rows, width), bf16)],
+        in_specs=[smem] + [vmem] * (8 + 2 * chips),
+        out_specs=[vmem] * 8,
+        scratch_shapes=[
+            pltpu.VMEM((seqs, rows, width), bf16),
+            pltpu.VMEM((chips, 2, seqs, sub, head_width), bf16),
+            pltpu.VMEM((rows, groups), f32),
+        ],
         compiler_params=limit,
         cost_estimate=cost(5),
     )(
         place,
-        back,
-        back_given,
-        inputs,
+        x_tokens,
         out_mine,
         out_yours,
         gain_two_full,
         router_full,
-        routes_flat,
-        cotangent,
+        routes_all,
+        first,
+        second,
+        *back,
     )
     arrived = exchange(buffer)
     expert_rows = groups * few
@@ -910,28 +1023,32 @@
     got = arrived[:, few:].reshape(expert_rows, width)
     up_local = dot(received, d_pre, ((0,), (0,))).astype(bf16)
     down_local = dot(act, got, ((0,), (0,))).astype(bf16)
-    returned, up_local, down_local = lax.optimization_barrier((returned, up_local, down_local))
 
     def both_reps(value):
         if reps == 2:
             return value.astype(f32) + swap(value).astype(f32)
         return lax.psum(value, "rep").astype(f32)
 
-    output, d_hidden, d_branch, keep, give, router_grad, gain_two_grad = pl.pallas_call(
+    returned, up_local, down_local = lax.optimization_barrier((returned, up_local, down_local))
+    *d_parts, out_first, out_second, d_hidden, d_branch, router_grad, gain_two_grad = pl.pallas_call(
         partial(turn_kernel, share=share, **pieces),
         name="combine_and_turn",
-        out_shape=(
-            jax.ShapeDtypeStruct((seqs, rows, width), bf16),
+        out_shape=[piece] * (2 * chips)
+        + [
+            jax.ShapeDtypeStruct((rows, width), bf16),
+            jax.ShapeDtypeStruct((rows, width), bf16),
             jax.ShapeDtypeStruct((tokens, width), f32),
             jax.ShapeDtypeStruct((tokens, width), bf16),
-            jax.ShapeDtypeStruct((groups // 2, sub, head_width), bf16),
-            jax.ShapeDtypeStruct((groups // 2, sub, head_width), bf16),
             jax.ShapeDtypeStruct((EXPERTS, width), f32),
             jax.ShapeDtypeStruct((1, width), f32),
-        ),
+        ],
         in_specs=[smem] + [vmem] * 11,
-        out_specs=[vmem] * 7,
-        scratch_shapes=[pltpu.VMEM((seqs, rows, width), bf16)],
+        out_specs=[vmem] * (6 + 2 * chips),
+        scratch_shapes=[
+            pltpu.VMEM((seqs, rows, width), bf16),
+            pltpu.VMEM((seqs, rows, width), bf16),
+            pltpu.VMEM((chips, 2, seqs, sub, head_width), bf16),
+        ],
         compiler_params=limit,
         cost_estimate=cost(5),
     )(
@@ -941,14 +1058,14 @@
         hidden,
         normed_two,
         router_probs,
-        routes_flat,
-        cotangent,
+        routes_tokens,
+        cotangent_tokens,
         gain_two_full,
         router_full,
         out_mine,
         out_yours,
     )
-    grads = exchange(by_core(keep, swap(give), 0))
+    grads = plane_all(d_parts)
     out_send = pl.pallas_call(
         partial(out_grad_kernel, groups=groups, shard=shard),
         name="out_grad",
@@ -960,7 +1077,6 @@
         cost_estimate=cost(3),
     )(place, attended, swap(attended), d_branch, swap(d_branch))
     grads, out_send = lax.optimization_barrier((grads, out_send))
-    grads = grads.reshape(queries_count, head_width)
     out_back = exchange(out_send)
     d_all, table_part = pl.pallas_call(
         partial(backward_kernel, **sizes),
@@ -969,7 +1085,7 @@
             jax.ShapeDtypeStruct((groups, rows, 3 * head_width), bf16),
             jax.ShapeDtypeStruct((group_heads, groups * bucket_rows, LANES), f32),
         ),
-        in_specs=[smem] + [vmem] * 4,
+        in_specs=[smem] + [vmem] * (3 + 2 * chips),
         out_specs=[vmem] * 2,
         scratch_shapes=[
             pltpu.VMEM((queries_count, length), f32),
@@ -977,62 +1093,99 @@
             pltpu.VMEM((tile, 2 * length - LANES), f32),
             pltpu.VMEM((2 * head_width, length), f32),
             pltpu.VMEM((queries_count, head_width), f32),
+            pltpu.VMEM((queries_count, head_width), bf16),
         ],
         compiler_params=limit,
         cost_estimate=cost(1),
-    )(place, probs, queries, pair, grads)
+    )(place, probs, queries, pair, *grads)
+    d_all, out_back = lax.optimization_barrier((d_all, out_back))
+    d_all_other = swap(d_all)
+    out_first = to_tokens(out_first, 0, True)
+    out_second = to_tokens(out_second, 1, True)
     out_sum = jnp.sum(out_back.astype(f32), axis=0)
     out_sum = over_pairs(out_sum)
     out_other = swap(out_sum)
+    d_normed_parts, d_sum, gain_one_part = pl.pallas_call(
+        partial(rows_kernel, half=half),
+        name="d_normed",
+        out_shape=[
+            jax.ShapeDtypeStruct((chips, groups // chips, half, width), bf16),
+            jax.ShapeDtypeStruct((groups, rows, 3 * head_width), bf16),
+            jax.ShapeDtypeStruct((1, width), f32),
+        ],
+        in_specs=[smem] + [vmem] * 5,
+        out_specs=[vmem] * 3,
+        compiler_params=limit,
+        cost_estimate=cost(1),
+    )(place, d_all, d_all_other, w_group, normed_all, gain_one_full)
     last = pl.pallas_call(
-        partial(last_kernel, groups=groups, half=half, rows=rows, shard=shard, all_heads=heads),
-        name="input_side",
-        out_shape=jax.ShapeDtypeStruct((groups, half + part, width), bf16),
-        in_specs=[smem] + [vmem] * 8,
+        partial(weight_kernel, shard=shard, all_heads=heads),
+        name="weight_grads",
+        out_shape=jax.ShapeDtypeStruct((groups, part, width), bf16),
+        in_specs=[smem] + [vmem] * 6,
         out_specs=vmem,
         scratch_shapes=[
-            pltpu.VMEM((groups, rows, 3 * head_width), bf16),
             pltpu.VMEM((groups, shard, 3 * head_width), f32),
-            pltpu.VMEM((1, width), f32),
             pltpu.VMEM((groups, part, spare), f32),
         ],
         compiler_params=limit,
+        cost_estimate=cost(8),
+    )(place, d_sum, normed_all, gain_one_part, gain_two_grad, router_grad, table_part)
+    planes = [list(range(q, q + chips)) for q in range(0, groups, chips)]
+    d_normed_parts = lax.all_to_all(
+        d_normed_parts, "sq", 0, 0, axis_index_groups=planes, tiled=True
+    )
+    last, d_normed_parts, out_first, out_second = lax.optimization_barrier(
+        (last, d_normed_parts, out_first, out_second)
+    )
+    final = exchange(last)
+    d_keep, d_give = pl.pallas_call(
+        total_kernel,
+        name="d_normed_total",
+        out_shape=[
+            jax.ShapeDtypeStruct((seqs, half, width), f32),
+            jax.ShapeDtypeStruct((seqs, half, width), bf16),
+        ],
+        in_specs=[smem, vmem],
+        out_specs=[vmem] * 2,
+        compiler_params=limit,
         cost_estimate=cost(1),
-    )(
-        place,
-        d_all,
-        swap(d_all),
-        w_group,
-        normed_all,
-        own,
-        gain_two_grad,
-        router_grad,
-        table_part,
-    )
-    last, out_other = lax.optimization_barrier((last, out_other))
-    final = exchange(last)
+    )(place, d_normed_parts)
+    grad_first, grad_second = pl.pallas_call(
+        partial(token_kernel, half=half),
+        name="token_grad",
+        out_shape=[jax.ShapeDtypeStruct((rows, width), bf16)] * 2,
+        in_specs=[smem] + [vmem] * 5,
+        out_specs=[vmem] * 2,
+        scratch_shapes=[pltpu.VMEM((seqs, rows, width), f32)] * 2,
+        compiler_params=limit,
+        cost_estimate=cost(2),
+    )(place, x_tokens, d_hidden, gain_one_full, d_keep, swap(d_give))
+    grad_first = to_tokens(grad_first, 0, True)
+    grad_second = to_tokens(grad_second, 1, True)
     up_grad = both_reps(up_local)
     down_grad = both_reps(down_local)
-    final, up_grad, down_grad = lax.optimization_barrier((final, up_grad, down_grad))
-    keep, give, four, four_low, small_sum = pl.pallas_call(
-        partial(sum_kernel, half=half, seqs=seqs),
+    final, grad_first, grad_second, up_grad, down_grad = lax.optimization_barrier(
+        (final, grad_first, grad_second, up_grad, down_grad)
+    )
+    four, four_low, small_sum = pl.pallas_call(
+        partial(sum_kernel, seqs=seqs),
         name="sums",
         out_shape=(
-            jax.ShapeDtypeStruct((seqs, half, width), f32),
-            jax.ShapeDtypeStruct((seqs, half, width), bf16),
             jax.ShapeDtypeStruct((3, part, width), f32),
             jax.ShapeDtypeStruct((3, part, width), bf16),
             jax.ShapeDtypeStruct((part, spare), f32),
         ),
-        in_specs=[smem] + [vmem],
-        out_specs=[vmem] * 5,
+        in_specs=[vmem],
+        out_specs=[vmem] * 3,
         compiler_params=limit,
         cost_estimate=cost(2),
-    )(place, final)
+    )(final)
     if reps > 2:
         four, small_sum = over_pairs(four), over_pairs(small_sum)
         four_low = four.astype(bf16)
     (
+        output,
         input_grad,
         query_grad,
         key_grad,
@@ -1043,9 +1196,12 @@
         gain_two_grad,
         router_grad,
     ) = pl.pallas_call(
-        partial(input_kernel, half=half),
+        input_kernel,
         name="input_grad",
-        out_shape=(jax.ShapeDtypeStruct((seqs, rows, width), f32),)
+        out_shape=(
+            jax.ShapeDtypeStruct((seqs, rows, width), bf16),
+            jax.ShapeDtypeStruct((seqs, rows, width), f32),
+        )
         + (jax.ShapeDtypeStruct((shard, width), f32),) * 4
         + (
             jax.ShapeDtypeStruct((bucket_rows, heads), f32),
@@ -1053,24 +1209,22 @@
             jax.ShapeDtypeStruct((1, shard), f32),
             jax.ShapeDtypeStruct((EXPERTS, shard), f32),
         ),
-        in_specs=[smem] + [vmem] * 11,
-        out_specs=[vmem] * 9,
-        scratch_shapes=[pltpu.VMEM((seqs, rows, width), f32)],
+        in_specs=[smem] + [vmem] * 10,
+        out_specs=[vmem] * 10,
         compiler_params=limit,
         cost_estimate=cost(2),
     )(
         place,
-        keep,
-        swap(give),
+        grad_first,
+        grad_second,
+        out_first,
+        out_second,
         four,
         swap(four_low),
         out_sum,
         out_other,
         small_sum,
         swap(small_sum),
-        inputs,
-        d_hidden,
-        gain_one_full,
     )
     return (
         output,

time: 287 us -> 271 us (0.944)
  waiting for transfers between devices: 107 us -> 61.1 us
  starting transfers between devices: 46.9 us -> 72.1 us
  Pallas kernels: 63.2 us -> 68 us
    all_to_all x7 -> x5, waiting for transfers between devices: 99.6 us -> 33.1 us  [exchange(): return lax.all_to_all(value, 'sq', split_axis=0, concat_axis=0, tiled=True)]
    ppermute x0 -> x25, starting transfers between devices: none -> 29.8 us  [the longest x17 18.4 us: plane(): return lax.ppermute(value, ('rep', 'sq'), moves)]
    ppermute x0 -> x25, waiting for transfers between devices: none -> 16.1 us  [the longest x17 12 us: plane(): return lax.ppermute(value, ('rep', 'sq'), moves)]
    all_to_all x7 -> x5, starting transfers between devices: 44.5 us -> 30.4 us  [exchange(): return lax.all_to_all(value, 'sq', split_axis=0, concat_axis=0, tiled=True)]
    all_to_all x0 -> x1, waiting for transfers between devices: none -> 7.79 us  [local(): lax.all_to_all(d_normed_parts, 'sq', 0, 0, axis_index_groups=planes, tile...]
    pallas_call x4 -> x7, Pallas kernels: 15.5 us -> 21 us  [the longest x1 5.9 us: local(): pl.pallas_call(partial(rows_kernel, half=half), name='d_normed', out_shap...]
    ppermute x15 -> x16, starting transfers between devices: 2.42 us -> 7.6 us  [swap(): return lax.ppermute(value, 'rep', pairs)]
    all_to_all x0 -> x1, starting transfers between devices: none -> 4.21 us  [local(): lax.all_to_all(d_normed_parts, 'sq', 0, 0, axis_index_groups=planes, tile...]
  transfers between devices with their start and end apart: 22 -> 47, of which waited for: 13 -> 15; matrix products, arithmetic and copies ran while one was open for 7% -> 6% of each run, Pallas kernels for 13% -> 19%
where the time goes in v2:
time: 271 us; the launch traced here: 269 us
  starting transfers between devices  72.1 us (27%)
  Pallas kernels  68 us (25%)
  waiting for transfers between devices  61.1 us (23%)
  blocking collectives  42.7 us (16%)
  other arithmetic  9.91 us (4%)
  local copies, waits for them, and re-layouts  9.8 us (4%)
  matrix products  4.24 us (2%)
    all_to_all x1, blocking collectives, exchange(): return lax.all_to_all(value, 'sq', split_axis=0, concat_axis=0, tiled=True)  42.7 us
    all_to_all x5, waiting for transfers between devices, exchange(): return lax.all_to_all(value, 'sq', split_axis=0, concat_axis=0, tiled=True)  33.1 us
    all_to_all x5, starting transfers between devices, exchange(): return lax.all_to_all(value, 'sq', split_axis=0, concat_axis=0, tiled=True)  30.4 us
    ppermute x17, starting transfers between devices, plane(): return lax.ppermute(value, ('rep', 'sq'), moves)  18.4 us
    pallas_call x1, Pallas kernels, local(): pl.pallas_call(partial(forward_kernel, shard=shard, all_heads=heads, **si...  15.1 us
    ppermute x17, waiting for transfers between devices, plane(): return lax.ppermute(value, ('rep', 'sq'), moves)  12 us
    ppermute x8, starting transfers between devices, to_tokens(): return lax.ppermute(value, ('rep', 'sq'), moves)  11.5 us
    pallas_call x1, Pallas kernels, local(): pl.pallas_call(partial(backward_kernel, **sizes), name='attention_backwar...  10.9 us
  transfers between devices with their start and end apart: 47, of which 15 were waited for; matrix products, arithmetic and copies ran while one was open for 6% of the time, Pallas kernels for 19%

profile of v2, /device:TPU:0, one launch (start us, length us, event | category | flops | bytes accessed | tf_op | source)
XLA Modules:
  0.0 269.3 jit_solution(17642689790739913170)
XLA Ops:
  0.7 0.8 pad_add_fusion.marks_ref
  1.9 1.0 dynamic-slice_bitcast_fusion.2
  2.9 0.7 collective-permute-start.1
  3.5 2.7 %collective-permute-start.2 = (bf16[64,768]{1,0:T(8,128)(2,1)S(1)}, bf16[64,768]{1,0:T(8,128)(2,1)S(1)}, u32[]{:S(2)}, u32[]{:S(2)}) collective-permute-start(bf16[64,768]{1,0:T(8,128)(2,1)S(1)} %get-tuple-element.236), channel_id=1, source_target_pairs={{0,4},{1,5},{2,6},{3,7},{4,0},{5,1},{6,2},{7,3},{8,20},{9,21},{10,... | collective-permute-start | bytes 294920 | tf_op jit(solution)/shard_map/ppermute | solution.py:816
  6.3 0.6 stack.46.place_ref
  7.5 2.2 pack.1
  9.6 10.2 %all-to-all-start = ((bf16[16,24,768]{2,1,0:T(8,128)(2,1)}), bf16[16,24,768]{2,1,0:T(8,128)(2,1)S(1)}, u32[]{:S(2)}, u32[]{:S(2)}) async-start(bf16[16,24,768]{2,1,0:T(8,128)(2,1)} %pack.1), calls=%async_computation | async-start | bytes 1179648 | tf_op jit(solution)/shard_map/all_to_all | solution.py:749
  19.9 2.0 collective-permute-start.3
  21.8 1.5 collective-permute-start.4
  23.4 0.7 collective-permute-start.6
  24.1 2.0 collective-permute-start.7
  26.1 4.1 %collective-permute-done.7.second_ref = bf16[64,768]{1,0:T(8,128)(2,1)S(1)} collective-permute-done((bf16[64,768]{1,0:T(8,128)(2,1)S(1)}, bf16[64,768]{1,0:T(8,128)(2,1)S(1)}, u32[]{:S(2)}, u32[]{:S(2)}) %collective-permute-start.7) | collective-permute-done | bytes 98336 | tf_op jit(solution)/shard_map/ppermute | solution.py:816
  30.2 2.8 %collective-permute-done.3.refs_1_ = bf16[2,64,768]{2,1,0:T(8,128)(2,1)S(1)} collective-permute-done((bf16[2,64,768]{2,1,0:T(8,128)(2,1)S(1)}, bf16[2,64,768]{2,1,0:T(8,128)(2,1)S(1)}, u32[]{:S(2)}, u32[]{:S(2)}) %collective-permute-start.3) | collective-permute-done | bytes 196640 | tf_op jit(solution)/shard_map/ppermute | solution.py:802
  33.2 3.5 %collective-permute-done.5.refs_3_ = bf16[2,64,768]{2,1,0:T(8,128)(2,1)S(1)} collective-permute-done((bf16[2,64,768]{2,1,0:T(8,128)(2,1)S(1)}, bf16[2,64,768]{2,1,0:T(8,128)(2,1)S(1)}, u32[]{:S(2)}, u32[]{:S(2)}) %collective-permute-start.5) | collective-permute-done | bytes 196640 | tf_op jit(solution)/shard_map/ppermute | solution.py:802
  36.7 1.0 broadcast_in_dim.2
  37.7 1.5 collective-permute-start.8
  40.2 0.6 collective-permute-done.8.other_ref
  40.8 5.4 %all-to-all-start.1 = ((bf16[16,48,384]{2,1,0:T(8,128)(2,1)}), bf16[16,48,384]{2,1,0:T(8,128)(2,1)S(1)}, u32[]{:S(2)}, u32[]{:S(2)}) async-start(bf16[16,48,384]{2,1,0:T(8,128)(2,1)} %broadcast_in_dim.2), calls=%async_computation.1 | async-start | bytes 1179648 | tf_op jit(solution)/shard_map/all_to_all | solution.py:749
  47.0 0.7 copy-done.27
  47.7 15.1 %attention_forward.1 = (bf16[3,512,1024]{2,1,0:T(8,128)(2,1)}, bf16[512,192]{1,0:T(8,128)(2,1)}, bf16[1024,384]{1,0:T(8,128)(2,1)}, bf16[16,64,768]{2,1,0:T(8,12...) custom-call(s32[8]{0:T(128)} %stack.46.place_ref, ...), custom_call_target="tpu_custom_call" | custom-call | flops 54000001024 | bytes 60000000 | tf_op jit(solution)/shard_map/attention_forward/pallas_call | solution.py:926
  63.4 1.9 collective-permute-start.15
  65.4 1.5 collective-permute-start.17
  67.6 3.2 %collective-permute-start.19 = (bf16[2,32,192]{2,1,0:T(8,128)(2,1)}, bf16[2,32,192]{2,1,0:T(8,128)(2,1)S(1)}, u32[]{:S(2)}, u32[]{:S(2)}) collective-permute-start(bf16[2,32,192]{2,1,0:T(8,128)(2,1)} %get-tuple-element.157), channel_id=1, source_target_pairs={{0,3},{1,2},{2,1},{3,0},{4,7},{5,6},{6,5},{7,4},{8,11},{9,10},{10,... | collective-permute-start | bytes 73736 | tf_op jit(solution)/shard_map/ppermute | solution.py:802
  70.8 2.0 collective-permute-done.19.refs_6_
  72.8 2.4 collective-permute-done.20.refs_7_
  76.1 4.0 %router_and_dispatch.1 = (bf16[16,64,768]{2,1,0:T(8,128)(2,1)}, bf16[128,768]{1,0:T(8,128)(2,1)}, f32[128,768]{1,0:T(8,128)}, bf16[128,768]{1,0:T(8,128)(2,1)}, ...) custom-call(s32[8]{0:T(128)} %stack.46.place_ref, ...), custom_call_target="tpu_custom_call" | custom-call | flops 4499999744 | bytes 5000000 | tf_op jit(solution)/shard_map/router_and_dispatch/pallas_call | solution.py:971
  80.1 42.7 %all_to_all.35.arrived_ref = bf16[16,64,768]{2,1,0:T(8,128)(2,1)} all-to-all(bf16[16,64,768]{2,1,0:T(8,128)(2,1)} %get-tuple-element.159), channel_id=1, replica_groups=mesh['rep'=2,'sq'=16] {'sq'}, dimensions={0} | all-to-all | bytes 3145728 | tf_op jit(solution)/shard_map/all_to_all | solution.py:749
  122.7 9.5 %experts.1 = (bf16[16,64,768]{2,1,0:T(8,128)(2,1)}, bf16[512,1536]{1,0:T(8,128)(2,1)}, bf16[512,1536]{1,0:T(8,128)(2,1)}) custom-call(bf16[16,64,768]{2,1,0:T(8,128)(2,1)} %all_to_all.35.arrived_ref, bf16[768,1536]{1,0:T(8,128)(2,1)} %up_ref.1, bf16[1536,768]{1,0:T(8,128)(2,1)} %down_ref.1), custom_call_target="tpu_custom_call" | custom-call | flops 7200000000 | bytes 8000000 | tf_op jit(solution)/shard_map/experts/pallas_call | solution.py:1008
  132.3 4.5 %all-to-all-start.3 = ((bf16[16,64,768]{2,1,0:T(8,128)(2,1)}), bf16[16,64,768]{2,1,0:T(8,128)(2,1)}, u32[]{:S(2)}, u32[]{:S(2)}) async-start(bf16[16,64,768]{2,1,0:T(8,128)(2,1)} %get-tuple-element.160), calls=%async_computation.3 | async-start | bytes 3145728 | tf_op jit(solution)/shard_map/all_to_all | solution.py:749
  137.0 1.2 copy-done.49
  138.2 2.8 %convolution_convert_fusion.1 = bf16[768,1536]{1,0:T(8,128)(2,1)} fusion(bf16[512,768]{1,0:T(8,128)(2,1)S(1)} %bitcast.32, bf16[512,1536]{1,0:T(8,128)(2,1)S(1)} %copy-done.49), kind=kOutput, calls=%fused_computation.3 | convolution fusion | flops 1209139200 | bytes 4718592 | tf_op jit(solution)/shard_map/dot_general | solution.py:22
  141.0 1.4 convolution_convert_fusion
  142.5 27.6 %all-to-all-done.3.returned_ref = bf16[16,64,768]{2,1,0:T(8,128)(2,1)} async-done(((bf16[16,64,768]{2,1,0:T(8,128)(2,1)}), bf16[16,64,768]{2,1,0:T(8,128)(2,1)}, u32[]{:S(2)}, u32[]{:S(2)}) %all-to-all-start.3) | async-done | bytes 1572896 | tf_op jit(solution)/shard_map/all_to_all | solution.py:749
  170.1 4.6 %combine_and_turn.1 = (bf16[2,32,192]{2,1,0:T(8,128)(2,1)}, bf16[2,32,192]{2,1,0:T(8,128)(2,1)}, bf16[2,32,192]{2,1,0:T(8,128)(2,1)}, bf16[2,32,192]{2,1,0:T(8,1...) custom-call(s32[8]{0:T(128)} %stack.46.place_ref, ...), custom_call_target="tpu_custom_call" | custom-call | flops 4499999744 | bytes 5000000 | tf_op jit(solution)/shard_map/combine_and_turn/pallas_call | solution.py:1033
  175.2 0.7 collective-permute-start.22
  175.9 0.8 collective-permute-start.23
  176.7 2.7 collective-permute-start.24
  179.8 2.4 collective-permute-start.26
  182.2 0.7 copy-done.28
  182.9 2.9 %out_grad.1 = bf16[16,24,768]{2,1,0:T(8,128)(2,1)} custom-call(s32[8]{0:T(128)} %stack.46.place_ref, bf16[128,768]{1,0:T(8,128)(2,1)} %get-tuple-element.178.attended_ref, bf16[128,768]{1,0:T(8,128)(2,1)} %copy-done.23, bf16[128,768]{1,0:T(8,128)(2,1)} %get-tuple-element.179.d_ref, bf16[128,768]{1,0:T(8,128)(2,1)} %copy-done.28), custom_call_target="tpu_custom_call" | custom-call | flops 2700000000 | bytes 3000000 | tf_op jit(solution)/shard_map/out_grad/pallas_call | solution.py:1069
  185.8 0.8 collective-permute-done.27.refs_7_
  186.6 6.1 %all-to-all-start.4 = ((bf16[16,24,768]{2,1,0:T(8,128)(2,1)}), bf16[16,24,768]{2,1,0:T(8,128)(2,1)S(1)}, u32[]{:S(2)}, u32[]{:S(2)}) async-start(bf16[16,24,768]{2,1,0:T(8,128)(2,1)} %out_grad.1), calls=%async_computation.4 | async-start | bytes 1179648 | tf_op jit(solution)/shard_map/all_to_all | solution.py:749
  192.9 10.9 %attention_backward.1 = (bf16[16,64,576]{2,1,0:T(8,128)(2,1)}, f32[3,32,128]{2,1,0:T(8,128)}) custom-call(s32[8]{0:T(128)} %stack.46.place_ref, bf16[3,512,1024]{2,1,0:T(8,128)(2,1)} %get-tuple-element.133.probs_ref, bf16[512,192]{1,0:T(8,128)(2,1)} %get-tuple-element.134.query_ref, bf16[1024,384]{1,0:T(8,128)(2,1)} %get-tuple-element.135.pair_ref, ...), custom_call_target="tpu_custom_call" | custom-call | flops 900000000 | bytes 1000000 | tf_op jit(solution)/shard_map/attention_backward/pallas_call | solution.py:1081
  203.8 5.5 %all-to-all-done.4 = bf16[16,24,768]{2,1,0:T(8,128)(2,1)S(1)} async-done(((bf16[16,24,768]{2,1,0:T(8,128)(2,1)}), bf16[16,24,768]{2,1,0:T(8,128)(2,1)S(1)}, u32[]{:S(2)}, u32[]{:S(2)}) %all-to-all-start.4) | async-done | bytes 589856 | tf_op jit(solution)/shard_map/all_to_all | solution.py:749
  209.8 0.7 collective-permute-start.31
  210.5 1.6 collective-permute-start.32
  212.1 2.3 collective-permute-done.30.d_other_ref
  214.4 1.1 copy-done.3
  215.5 5.9 %d_normed.1 = (bf16[4,4,32,768]{3,2,1,0:T(8,128)(2,1)}, bf16[16,64,576]{2,1,0:T(8,128)(2,1)}, f32[1,768]{1,0:T(1,128)}) custom-call(s32[8]{0:T(128)} %stack.46.place_ref, bf16[16,64,576]{2,1,0:T(8,128)(2,1)} %get-tuple-element.190.d_own_ref, bf16[16,64,576]{2,1,0:T(8,128)(2,1)} %copy-done.3, bf16[768,576]{1,0:T(8,128)(2,1)} %get-tuple-element.191.weight_ref, ...), custom_call_target="tpu_custom_call" | custom-call | flops 900000000 | bytes 1000000 | tf_op jit(solution)/shard_map/d_normed/pallas_call | solution.py:1108
  221.4 4.2 %all-to-all-start.5 = ((bf16[4,4,32,768]{3,2,1,0:T(8,128)(2,1)}), bf16[4,4,32,768]{3,2,1,0:T(8,128)(2,1)}, u32[]{:S(2)}, u32[]{:S(2)}) async-start(bf16[4,4,32,768]{3,2,1,0:T(8,128)(2,1)} %get-tuple-element.199), calls=%async_computation.5 | async-start | bytes 1572864 | tf_op jit(solution)/shard_map/all_to_all | solution.py:1135
  225.6 4.4 %weight_grads.1 = bf16[16,24,768]{2,1,0:T(8,128)(2,1)} custom-call(s32[8]{0:T(128)} %stack.46.place_ref, bf16[16,64,576]{2,1,0:T(8,128)(2,1)} %get-tuple-element.194.d_sum, bf16[16,64,768]{2,1,0:T(8,128)(2,1)} %get-tuple-element.192.normed_ref, f32[1,768]{1,0:T(1,128)} %get-tuple-element.195.gain_sum, f32[1,768]{1,0:T(1,128)} %get-tuple-element.196.gain_two_ref, ...), custom_call_target="tpu_custom_call" | custom-call | flops 7200000000 | bytes 8000000 | tf_op jit(solution)/shard_map/weight_grads/pallas_call | solution.py:1121
  230.0 7.8 %all-to-all-done.5.rows_ref = bf16[4,4,32,768]{3,2,1,0:T(8,128)(2,1)} async-done(((bf16[4,4,32,768]{3,2,1,0:T(8,128)(2,1)}), bf16[4,4,32,768]{3,2,1,0:T(8,128)(2,1)}, u32[]{:S(2)}, u32[]{:S(2)}) %all-to-all-start.5) | async-done | bytes 786464 | tf_op jit(solution)/shard_map/all_to_all | solution.py:1135
  237.8 4.2 %all-to-all-start.6 = ((bf16[16,24,768]{2,1,0:T(8,128)(2,1)}), bf16[16,24,768]{2,1,0:T(8,128)(2,1)}, u32[]{:S(2)}, u32[]{:S(2)}) async-start(bf16[16,24,768]{2,1,0:T(8,128)(2,1)} %weight_grads.1), calls=%async_computation.6 | async-start | bytes 1179648 | tf_op jit(solution)/shard_map/all_to_all | solution.py:749
  242.1 2.1 d_normed_total.1
  244.3 4.5 %convert_add_fusion.1 = f32[768,1536]{1,0:T(8,128)} fusion(bf16[768,1536]{1,0:T(8,128)(2,1)} %collective-permute-done.36, bf16[768,1536]{1,0:T(8,128)(2,1)S(1)} %copy-done.2), kind=kLoop, calls=%fused_computation.1 | loop fusion | flops 3538944 | bytes 9437184 | tf_op jit(solution)/shard_map/add | solution.py:1029
  248.8 0.6 copy-done.38
  249.5 2.1 token_grad.1
  251.6 1.5 collective-permute-start.34
  253.1 1.7 collective-permute-start.35
  254.8 4.5 %convert_add_fusion = f32[1536,768]{1,0:T(8,128)} fusion(bf16[1536,768]{1,0:T(8,128)(2,1)} %collective-permute-done.37, bf16[1536,768]{1,0:T(8,128)(2,1)S(1)} %convolution_convert_fusion), kind=kLoop, calls=%fused_computation | loop fusion | flops 3538944 | bytes 9437184 | tf_op jit(solution)/shard_map/add | solution.py:1029
  259.3 2.0 sums.1
  261.3 3.1 %collective-permute-start.38 = (bf16[3,24,768]{2,1,0:T(8,128)(2,1)}, bf16[3,24,768]{2,1,0:T(8,128)(2,1)S(1)}, u32[]{:S(2)}, u32[]{:S(2)}) collective-permute-start(bf16[3,24,768]{2,1,0:T(8,128)(2,1)} %get-tuple-element.217), channel_id=1, source_target_pairs={{0,16},{16,0},{1,17},{17,1},{2,18},{18,2},{3,19},{19,3},{4,20},{20... | collective-permute-start | bytes 331784 | tf_op jit(solution)/shard_map/ppermute | solution.py:792
  265.0 0.8 collective-permute-done.39.out_other_ref
  266.8 2.4 input_grad.1
  (159 shorter events, 8.9 us)
Async XLA Ops:
  0.6 25.4 %copy-start = (bf16[48,768]{1,0:T(8,128)(2,1)S(1)}, bf16[48,768]{1,0:T(8,128)(2,1)}, u32[]{:S(2)}) copy-start(bf16[48,768]{1,0:T(8,128)(2,1)} %param.18) | copy-start | bytes 221188
  1.5 5.4 %collective-permute-start = (s32[2,128]{1,0:T(2,128)S(1)}, s32[2,128]{1,0:T(2,128)S(1)}, u32[]{:S(2)}, u32[]{:S(2)}) collective-permute-start(s32[2,128]{1,0:T(2,128)S(1)} %pad_add_fusion.marks_ref), channel_id=1, source_target_pairs={{0,16},{16,0},{1,17},{17,1},{2,18},{18,2},{3,19},{19,3},{4,20},{20... | collective-permute-start | bytes 3080 | tf_op jit(solution)/shard_map/ppermute | solution.py:792
  2.9 6.8 %collective-permute-start.1 = (bf16[64,768]{1,0:T(8,128)(2,1)S(1)}, bf16[64,768]{1,0:T(8,128)(2,1)S(1)}, u32[]{:S(2)}, u32[]{:S(2)}) collective-permute-start(bf16[64,768]{1,0:T(8,128)(2,1)S(1)} %get-tuple-element.237), channel_id=1, source_target_pairs={{0,0},{1,1},{2,2},{3,3},{4,4},{5,5},{6,6},{7,7},{8,16},{9,17},{10,... | collective-permute-start | bytes 294920 | tf_op jit(solution)/shard_map/ppermute | solution.py:816
  3.5 6.1 %collective-permute-start.2 = (bf16[64,768]{1,0:T(8,128)(2,1)S(1)}, bf16[64,768]{1,0:T(8,128)(2,1)S(1)}, u32[]{:S(2)}, u32[]{:S(2)}) collective-permute-start(bf16[64,768]{1,0:T(8,128)(2,1)S(1)} %get-tuple-element.236), channel_id=1, source_target_pairs={{0,4},{1,5},{2,6},{3,7},{4,0},{5,1},{6,2},{7,3},{8,20},{9,21},{10,... | collective-permute-start | bytes 294920 | tf_op jit(solution)/shard_map/ppermute | solution.py:816
  7.5 16.0 %copy-start.6 = (bf16[2,64,768]{2,1,0:T(8,128)(2,1)S(1)}, bf16[2,64,768]{2,1,0:T(8,128)(2,1)}, u32[]{:S(2)}) copy-start(bf16[2,64,768]{2,1,0:T(8,128)(2,1)} %param.27) | copy-start | bytes 589828
  9.6 27.0 %all-to-all-start = ((bf16[16,24,768]{2,1,0:T(8,128)(2,1)}), bf16[16,24,768]{2,1,0:T(8,128)(2,1)S(1)}, u32[]{:S(2)}, u32[]{:S(2)}) async-start(bf16[16,24,768]{2,1,0:T(8,128)(2,1)} %pack.1), calls=%async_computation | async-start | bytes 1179648 | tf_op jit(solution)/shard_map/all_to_all | solution.py:749
  19.8 26.4 %copy-start.7 = (bf16[2,64,768]{2,1,0:T(8,128)(2,1)}, bf16[2,64,768]{2,1,0:T(8,128)(2,1)S(1)}, u32[]{:S(2)}) copy-start(bf16[2,64,768]{2,1,0:T(8,128)(2,1)S(1)} %maximum_select_fusion.refs_0_.x_ref) | copy-start | bytes 589828
  19.9 13.1 %collective-permute-start.3 = (bf16[2,64,768]{2,1,0:T(8,128)(2,1)S(1)}, bf16[2,64,768]{2,1,0:T(8,128)(2,1)S(1)}, u32[]{:S(2)}, u32[]{:S(2)}) collective-permute-start(bf16[2,64,768]{2,1,0:T(8,128)(2,1)S(1)} %maximum_select_fusion.refs_0_.x_ref), channel_id=1, source_target_pairs={{0,1},{1,0},{2,3},{3,2},{4,5},{5,4},{6,7},{7,6},{8,9},{9,8},{10,11... | collective-permute-start | bytes 589832 | tf_op jit(solution)/shard_map/ppermute | solution.py:802
  21.8 11.3 %collective-permute-start.4 = (bf16[2,64,768]{2,1,0:T(8,128)(2,1)S(1)}, bf16[2,64,768]{2,1,0:T(8,128)(2,1)S(1)}, u32[]{:S(2)}, u32[]{:S(2)}) collective-permute-start(bf16[2,64,768]{2,1,0:T(8,128)(2,1)S(1)} %maximum_select_fusion.refs_0_.x_ref), channel_id=1, source_target_pairs={{0,2},{1,3},{2,0},{3,1},{4,6},{5,7},{6,4},{7,5},{8,10},{9,11},{10,... | collective-permute-start | bytes 589832 | tf_op jit(solution)/shard_map/ppermute | solution.py:802
  23.3 13.4 %collective-permute-start.5 = (bf16[2,64,768]{2,1,0:T(8,128)(2,1)S(1)}, bf16[2,64,768]{2,1,0:T(8,128)(2,1)S(1)}, u32[]{:S(2)}, u32[]{:S(2)}) collective-permute-start(bf16[2,64,768]{2,1,0:T(8,128)(2,1)S(1)} %maximum_select_fusion.refs_0_.x_ref), channel_id=1, source_target_pairs={{0,3},{1,2},{2,1},{3,0},{4,7},{5,6},{6,5},{7,4},{8,11},{9,10},{10,... | collective-permute-start | bytes 589832 | tf_op jit(solution)/shard_map/ppermute | solution.py:802
  23.4 2.7 collective-permute-start.6
  24.1 6.1 %collective-permute-start.7 = (bf16[64,768]{1,0:T(8,128)(2,1)S(1)}, bf16[64,768]{1,0:T(8,128)(2,1)S(1)}, u32[]{:S(2)}, u32[]{:S(2)}) collective-permute-start(bf16[64,768]{1,0:T(8,128)(2,1)S(1)} %get-tuple-element.234), channel_id=1, source_target_pairs={{0,4},{1,5},{2,6},{3,7},{4,0},{5,1},{6,2},{7,3},{8,20},{9,21},{10,... | collective-permute-start | bytes 294920 | tf_op jit(solution)/shard_map/ppermute | solution.py:816
  26.1 36.7 %copy-start.30 = (bf16[64,768]{1,0:T(8,128)(2,1)}, bf16[64,768]{1,0:T(8,128)(2,1)S(1)}, u32[]{:S(2)}) copy-start(bf16[64,768]{1,0:T(8,128)(2,1)S(1)} %collective-permute-done.6.first_ref) | copy-start | bytes 294916
  33.0 13.3 %copy-start.19 = (bf16[2,64,768]{2,1,0:T(8,128)(2,1)}, bf16[2,64,768]{2,1,0:T(8,128)(2,1)S(1)}, u32[]{:S(2)}) copy-start(bf16[2,64,768]{2,1,0:T(8,128)(2,1)S(1)} %collective-permute-done.3.refs_1_) | copy-start | bytes 589828
  33.2 13.1 %copy-start.21 = (bf16[2,64,768]{2,1,0:T(8,128)(2,1)}, bf16[2,64,768]{2,1,0:T(8,128)(2,1)S(1)}, u32[]{:S(2)}) copy-start(bf16[2,64,768]{2,1,0:T(8,128)(2,1)S(1)} %collective-permute-done.4.refs_2_) | copy-start | bytes 589828
  36.7 9.6 %copy-start.22 = (bf16[2,64,768]{2,1,0:T(8,128)(2,1)}, bf16[2,64,768]{2,1,0:T(8,128)(2,1)S(1)}, u32[]{:S(2)}) copy-start(bf16[2,64,768]{2,1,0:T(8,128)(2,1)S(1)} %collective-permute-done.5.refs_3_) | copy-start | bytes 589828
  36.7 9.6 %copy-start.5 = (bf16[16,24,768]{2,1,0:T(8,128)(2,1)}, bf16[16,24,768]{2,1,0:T(8,128)(2,1)S(1)}, u32[]{:S(2)}) copy-start(bf16[16,24,768]{2,1,0:T(8,128)(2,1)S(1)} %all-to-all-done.own_ref) | copy-start | bytes 1769476
  37.7 3.2 %collective-permute-start.8 = (bf16[16,24,768]{2,1,0:T(8,128)(2,1)S(1)}, bf16[16,24,768]{2,1,0:T(8,128)(2,1)S(1)}, u32[]{:S(2)}, u32[]{:S(2)}) collective-permute-start(bf16[16,24,768]{2,1,0:T(8,128)(2,1)S(1)} %all-to-all-done.own_ref), channel_id=1, source_target_pairs={{0,16},{16,0},{1,17},{17,1},{2,18},{18,2},{3,19},{19,3},{4,20},{20... | collective-permute-start | bytes 1769480 | tf_op jit(solution)/shard_map/ppermute | solution.py:792
  39.2 7.0 %collective-permute-start.9 = (bf16[2,64,768]{2,1,0:T(8,128)(2,1)S(1)}, bf16[2,64,768]{2,1,0:T(8,128)(2,1)S(1)}, u32[]{:S(2)}, u32[]{:S(2)}) collective-permute-start(bf16[2,64,768]{2,1,0:T(8,128)(2,1)S(1)} %maximum_select_fusion.refs_0_.x_ref), channel_id=1, source_target_pairs={{0,16},{16,0},{1,17},{17,1},{2,18},{18,2},{3,19},{19,3},{4,20},{20... | collective-permute-start | bytes 589832 | tf_op jit(solution)/shard_map/ppermute | solution.py:792
  39.2 7.0 %collective-permute-start.10 = (bf16[2,64,768]{2,1,0:T(8,128)(2,1)S(1)}, bf16[2,64,768]{2,1,0:T(8,128)(2,1)S(1)}, u32[]{:S(2)}, u32[]{:S(2)}) collective-permute-start(bf16[2,64,768]{2,1,0:T(8,128)(2,1)S(1)} %collective-permute-done.3.refs_1_), channel_id=1, source_target_pairs={{0,16},{16,0},{1,17},{17,1},{2,18},{18,2},{3,19},{19,3},{4,20},{20... | collective-permute-start | bytes 589832 | tf_op jit(solution)/shard_map/ppermute | solution.py:792
  39.7 6.5 %collective-permute-start.11 = (bf16[2,64,768]{2,1,0:T(8,128)(2,1)S(1)}, bf16[2,64,768]{2,1,0:T(8,128)(2,1)S(1)}, u32[]{:S(2)}, u32[]{:S(2)}) collective-permute-start(bf16[2,64,768]{2,1,0:T(8,128)(2,1)S(1)} %collective-permute-done.4.refs_2_), channel_id=1, source_target_pairs={{0,16},{16,0},{1,17},{17,1},{2,18},{18,2},{3,19},{19,3},{4,20},{20... | collective-permute-start | bytes 589832 | tf_op jit(solution)/shard_map/ppermute | solution.py:792
  39.7 6.6 %collective-permute-start.12 = (bf16[2,64,768]{2,1,0:T(8,128)(2,1)S(1)}, bf16[2,64,768]{2,1,0:T(8,128)(2,1)S(1)}, u32[]{:S(2)}, u32[]{:S(2)}) collective-permute-start(bf16[2,64,768]{2,1,0:T(8,128)(2,1)S(1)} %collective-permute-done.5.refs_3_), channel_id=1, source_target_pairs={{0,16},{16,0},{1,17},{17,1},{2,18},{18,2},{3,19},{19,3},{4,20},{20... | collective-permute-start | bytes 589832 | tf_op jit(solution)/shard_map/ppermute | solution.py:792
  40.8 22.0 %all-to-all-start.1 = ((bf16[16,48,384]{2,1,0:T(8,128)(2,1)}), bf16[16,48,384]{2,1,0:T(8,128)(2,1)S(1)}, u32[]{:S(2)}, u32[]{:S(2)}) async-start(bf16[16,48,384]{2,1,0:T(8,128)(2,1)} %broadcast_in_dim.2), calls=%async_computation.1 | async-start | bytes 1179648 | tf_op jit(solution)/shard_map/all_to_all | solution.py:749
  62.9 12.3 %copy-start.4 = (bf16[16,48,384]{2,1,0:T(8,128)(2,1)}, bf16[16,48,384]{2,1,0:T(8,128)(2,1)S(1)}, u32[]{:S(2)}) copy-start(bf16[16,48,384]{2,1,0:T(8,128)(2,1)S(1)} %all-to-all-done.1) | copy-start | bytes 1769476
  62.9 12.3 %collective-permute-start.13 = (bf16[768,384]{1,0:T(8,128)(2,1)S(1)}, bf16[768,384]{1,0:T(8,128)(2,1)S(1)}, u32[]{:S(2)}, u32[]{:S(2)}) collective-permute-start(bf16[768,384]{1,0:T(8,128)(2,1)S(1)} %bitcast.33), channel_id=1, source_target_pairs={{0,16},{16,0},{1,17},{17,1},{2,18},{18,2},{3,19},{19,3},{4,20},{20... | collective-permute-start | bytes 1769480 | tf_op jit(solution)/shard_map/ppermute | solution.py:792
  62.9 3.9 %collective-permute-start.14 = (bf16[2,32,192]{2,1,0:T(8,128)(2,1)}, bf16[2,32,192]{2,1,0:T(8,128)(2,1)S(1)}, u32[]{:S(2)}, u32[]{:S(2)}) collective-permute-start(bf16[2,32,192]{2,1,0:T(8,128)(2,1)} %get-tuple-element.152), channel_id=1, source_target_pairs={{0,16},{1,17},{2,18},{3,19},{4,20},{5,21},{6,22},{7,23},{8,24},{9,... | collective-permute-start | bytes 73736 | tf_op jit(solution)/shard_map/ppermute | solution.py:802
  63.4 4.1 %collective-permute-start.15 = (bf16[2,32,192]{2,1,0:T(8,128)(2,1)}, bf16[2,32,192]{2,1,0:T(8,128)(2,1)S(1)}, u32[]{:S(2)}, u32[]{:S(2)}) collective-permute-start(bf16[2,32,192]{2,1,0:T(8,128)(2,1)} %get-tuple-element.153), channel_id=1, source_target_pairs={{0,1},{1,0},{2,3},{3,2},{4,5},{5,4},{6,7},{7,6},{8,9},{9,8},{10,11... | collective-permute-start | bytes 73736 | tf_op jit(solution)/shard_map/ppermute | solution.py:802
  65.4 5.4 %collective-permute-start.16 = (bf16[2,32,192]{2,1,0:T(8,128)(2,1)}, bf16[2,32,192]{2,1,0:T(8,128)(2,1)S(1)}, u32[]{:S(2)}, u32[]{:S(2)}) collective-permute-start(bf16[2,32,192]{2,1,0:T(8,128)(2,1)} %get-tuple-element.154), channel_id=1, source_target_pairs={{0,17},{1,16},{2,19},{3,18},{4,21},{5,20},{6,23},{7,22},{8,25},{9,... | collective-permute-start | bytes 73736 | tf_op jit(solution)/shard_map/ppermute | solution.py:802
  65.4 5.4 %collective-permute-start.17 = (bf16[2,32,192]{2,1,0:T(8,128)(2,1)}, bf16[2,32,192]{2,1,0:T(8,128)(2,1)S(1)}, u32[]{:S(2)}, u32[]{:S(2)}) collective-permute-start(bf16[2,32,192]{2,1,0:T(8,128)(2,1)} %get-tuple-element.155), channel_id=1, source_target_pairs={{0,2},{1,3},{2,0},{3,1},{4,6},{5,7},{6,4},{7,5},{8,10},{9,11},{10,... | collective-permute-start | bytes 73736 | tf_op jit(solution)/shard_map/ppermute | solution.py:802
  66.8 8.4 %copy-start.40 = (bf16[2,32,192]{2,1,0:T(8,128)(2,1)}, bf16[2,32,192]{2,1,0:T(8,128)(2,1)S(1)}, u32[]{:S(2)}) copy-start(bf16[2,32,192]{2,1,0:T(8,128)(2,1)S(1)} %collective-permute-done.14.refs_1_) | copy-start | bytes 73732
  66.8 3.9 %collective-permute-start.18 = (bf16[2,32,192]{2,1,0:T(8,128)(2,1)}, bf16[2,32,192]{2,1,0:T(8,128)(2,1)S(1)}, u32[]{:S(2)}, u32[]{:S(2)}) collective-permute-start(bf16[2,32,192]{2,1,0:T(8,128)(2,1)} %get-tuple-element.156), channel_id=1, source_target_pairs={{0,18},{1,19},{2,16},{3,17},{4,22},{5,23},{6,20},{7,21},{8,26},{9,... | collective-permute-start | bytes 73736 | tf_op jit(solution)/shard_map/ppermute | solution.py:802
  67.6 7.6 %copy-start.41 = (bf16[2,32,192]{2,1,0:T(8,128)(2,1)}, bf16[2,32,192]{2,1,0:T(8,128)(2,1)S(1)}, u32[]{:S(2)}) copy-start(bf16[2,32,192]{2,1,0:T(8,128)(2,1)S(1)} %collective-permute-done.15.refs_2_) | copy-start | bytes 73732
  67.6 5.3 %collective-permute-start.19 = (bf16[2,32,192]{2,1,0:T(8,128)(2,1)}, bf16[2,32,192]{2,1,0:T(8,128)(2,1)S(1)}, u32[]{:S(2)}, u32[]{:S(2)}) collective-permute-start(bf16[2,32,192]{2,1,0:T(8,128)(2,1)} %get-tuple-element.157), channel_id=1, source_target_pairs={{0,3},{1,2},{2,1},{3,0},{4,7},{5,6},{6,5},{7,4},{8,11},{9,10},{10,... | collective-permute-start | bytes 73736 | tf_op jit(solution)/shard_map/ppermute | solution.py:802
  70.7 4.5 %collective-permute-start.20 = (bf16[2,32,192]{2,1,0:T(8,128)(2,1)}, bf16[2,32,192]{2,1,0:T(8,128)(2,1)S(1)}, u32[]{:S(2)}, u32[]{:S(2)}) collective-permute-start(bf16[2,32,192]{2,1,0:T(8,128)(2,1)} %get-tuple-element.158), channel_id=1, source_target_pairs={{0,19},{1,18},{2,17},{3,16},{4,23},{5,22},{6,21},{7,20},{8,27},{9,... | collective-permute-start | bytes 73736 | tf_op jit(solution)/shard_map/ppermute | solution.py:802
  132.3 37.8 %all-to-all-start.3 = ((bf16[16,64,768]{2,1,0:T(8,128)(2,1)}), bf16[16,64,768]{2,1,0:T(8,128)(2,1)}, u32[]{:S(2)}, u32[]{:S(2)}) async-start(bf16[16,64,768]{2,1,0:T(8,128)(2,1)} %get-tuple-element.160), calls=%async_computation.3 | async-start | bytes 3145728 | tf_op jit(solution)/shard_map/all_to_all | solution.py:749
  136.8 39.8 %collective-permute-start.28 = (bf16[128,768]{1,0:T(8,128)(2,1)S(1)}, bf16[128,768]{1,0:T(8,128)(2,1)S(1)}, u32[]{:S(2)}, u32[]{:S(2)}) collective-permute-start(bf16[128,768]{1,0:T(8,128)(2,1)S(1)} %copy-done.20), channel_id=1, source_target_pairs={{0,16},{16,0},{1,17},{17,1},{2,18},{18,2},{3,19},{19,3},{4,20},{20... | collective-permute-start | bytes 589832 | tf_op jit(solution)/shard_map/ppermute | solution.py:792
  174.7 7.5 %collective-permute-start.29 = (bf16[128,768]{1,0:T(8,128)(2,1)}, bf16[128,768]{1,0:T(8,128)(2,1)S(1)}, u32[]{:S(2)}, u32[]{:S(2)}) collective-permute-start(bf16[128,768]{1,0:T(8,128)(2,1)} %get-tuple-element.179.d_ref), channel_id=1, source_target_pairs={{0,16},{16,0},{1,17},{17,1},{2,18},{18,2},{3,19},{19,3},{4,20},{20... | collective-permute-start | bytes 589832 | tf_op jit(solution)/shard_map/ppermute | solution.py:792
  174.7 4.6 %collective-permute-start.21 = (bf16[2,32,192]{2,1,0:T(8,128)(2,1)}, bf16[2,32,192]{2,1,0:T(8,128)(2,1)S(1)}, u32[]{:S(2)}, u32[]{:S(2)}) collective-permute-start(bf16[2,32,192]{2,1,0:T(8,128)(2,1)} %get-tuple-element.171), channel_id=1, source_target_pairs={{0,16},{1,17},{2,18},{3,19},{4,20},{5,21},{6,22},{7,23},{8,24},{9,... | collective-permute-start | bytes 73736 | tf_op jit(solution)/shard_map/ppermute | solution.py:802
  175.2 4.5 %collective-permute-start.22 = (bf16[2,32,192]{2,1,0:T(8,128)(2,1)}, bf16[2,32,192]{2,1,0:T(8,128)(2,1)S(1)}, u32[]{:S(2)}, u32[]{:S(2)}) collective-permute-start(bf16[2,32,192]{2,1,0:T(8,128)(2,1)} %get-tuple-element.172), channel_id=1, source_target_pairs={{0,1},{1,0},{2,3},{3,2},{4,5},{5,4},{6,7},{7,6},{8,9},{9,8},{10,11... | collective-permute-start | bytes 73736 | tf_op jit(solution)/shard_map/ppermute | solution.py:802
  175.9 9.9 %collective-permute-start.23 = (bf16[2,32,192]{2,1,0:T(8,128)(2,1)}, bf16[2,32,192]{2,1,0:T(8,128)(2,1)S(1)}, u32[]{:S(2)}, u32[]{:S(2)}) collective-permute-start(bf16[2,32,192]{2,1,0:T(8,128)(2,1)} %get-tuple-element.173), channel_id=1, source_target_pairs={{0,17},{1,16},{2,19},{3,18},{4,21},{5,20},{6,23},{7,22},{8,25},{9,... | collective-permute-start | bytes 73736 | tf_op jit(solution)/shard_map/ppermute | solution.py:802
  176.7 9.1 %collective-permute-start.24 = (bf16[2,32,192]{2,1,0:T(8,128)(2,1)}, bf16[2,32,192]{2,1,0:T(8,128)(2,1)S(1)}, u32[]{:S(2)}, u32[]{:S(2)}) collective-permute-start(bf16[2,32,192]{2,1,0:T(8,128)(2,1)} %get-tuple-element.174), channel_id=1, source_target_pairs={{0,2},{1,3},{2,0},{3,1},{4,6},{5,7},{6,4},{7,5},{8,10},{9,11},{10,... | collective-permute-start | bytes 73736 | tf_op jit(solution)/shard_map/ppermute | solution.py:802
  179.4 6.5 %collective-permute-start.25 = (bf16[2,32,192]{2,1,0:T(8,128)(2,1)}, bf16[2,32,192]{2,1,0:T(8,128)(2,1)S(1)}, u32[]{:S(2)}, u32[]{:S(2)}) collective-permute-start(bf16[2,32,192]{2,1,0:T(8,128)(2,1)} %get-tuple-element.175), channel_id=1, source_target_pairs={{0,18},{1,19},{2,16},{3,17},{4,22},{5,23},{6,20},{7,21},{8,26},{9,... | collective-permute-start | bytes 73736 | tf_op jit(solution)/shard_map/ppermute | solution.py:802
  179.8 6.1 %collective-permute-start.26 = (bf16[2,32,192]{2,1,0:T(8,128)(2,1)}, bf16[2,32,192]{2,1,0:T(8,128)(2,1)S(1)}, u32[]{:S(2)}, u32[]{:S(2)}) collective-permute-start(bf16[2,32,192]{2,1,0:T(8,128)(2,1)} %get-tuple-element.176), channel_id=1, source_target_pairs={{0,3},{1,2},{2,1},{3,0},{4,7},{5,6},{6,5},{7,4},{8,11},{9,10},{10,... | collective-permute-start | bytes 73736 | tf_op jit(solution)/shard_map/ppermute | solution.py:802
  182.2 4.5 %collective-permute-start.27 = (bf16[2,32,192]{2,1,0:T(8,128)(2,1)}, bf16[2,32,192]{2,1,0:T(8,128)(2,1)S(1)}, u32[]{:S(2)}, u32[]{:S(2)}) collective-permute-start(bf16[2,32,192]{2,1,0:T(8,128)(2,1)} %get-tuple-element.177), channel_id=1, source_target_pairs={{0,19},{1,18},{2,17},{3,16},{4,23},{5,22},{6,21},{7,20},{8,27},{9,... | collective-permute-start | bytes 73736 | tf_op jit(solution)/shard_map/ppermute | solution.py:802
  185.8 7.1 %copy-start.11 = (bf16[2,32,192]{2,1,0:T(8,128)(2,1)}, bf16[2,32,192]{2,1,0:T(8,128)(2,1)S(1)}, u32[]{:S(2)}) copy-start(bf16[2,32,192]{2,1,0:T(8,128)(2,1)S(1)} %collective-permute-done.23.refs_3_) | copy-start | bytes 73732
  185.8 7.1 %copy-start.12 = (bf16[2,32,192]{2,1,0:T(8,128)(2,1)}, bf16[2,32,192]{2,1,0:T(8,128)(2,1)S(1)}, u32[]{:S(2)}) copy-start(bf16[2,32,192]{2,1,0:T(8,128)(2,1)S(1)} %collective-permute-done.24.refs_4_) | copy-start | bytes 73732
  186.6 22.7 %all-to-all-start.4 = ((bf16[16,24,768]{2,1,0:T(8,128)(2,1)}), bf16[16,24,768]{2,1,0:T(8,128)(2,1)S(1)}, u32[]{:S(2)}, u32[]{:S(2)}) async-start(bf16[16,24,768]{2,1,0:T(8,128)(2,1)} %out_grad.1), calls=%async_computation.4 | async-start | bytes 1179648 | tf_op jit(solution)/shard_map/all_to_all | solution.py:749
  192.8 17.1 %copy-start.33 = (bf16[64,768]{1,0:T(8,128)(2,1)S(1)}, bf16[64,768]{1,0:T(8,128)(2,1)}, u32[]{:S(2)}) copy-start(bf16[64,768]{1,0:T(8,128)(2,1)} %get-tuple-element.200) | copy-start | bytes 294916
  192.8 17.7 %copy-start.32 = (bf16[64,768]{1,0:T(8,128)(2,1)S(1)}, bf16[64,768]{1,0:T(8,128)(2,1)}, u32[]{:S(2)}) copy-start(bf16[64,768]{1,0:T(8,128)(2,1)} %get-tuple-element.201) | copy-start | bytes 294916
  192.8 51.5 %collective-permute-start.36 = (bf16[768,1536]{1,0:T(8,128)(2,1)}, bf16[768,1536]{1,0:T(8,128)(2,1)}, u32[]{:S(2)}, u32[]{:S(2)}) collective-permute-start(bf16[768,1536]{1,0:T(8,128)(2,1)} %convolution_convert_fusion.1), channel_id=1, source_target_pairs={{0,16},{16,0},{1,17},{17,1},{2,18},{18,2},{3,19},{19,3},{4,20},{20... | collective-permute-start | bytes 7077896 | tf_op jit(solution)/shard_map/ppermute | solution.py:792
  209.3 5.1 %collective-permute-start.30 = (bf16[16,64,576]{2,1,0:T(8,128)(2,1)}, bf16[16,64,576]{2,1,0:T(8,128)(2,1)S(1)}, u32[]{:S(2)}, u32[]{:S(2)}) collective-permute-start(bf16[16,64,576]{2,1,0:T(8,128)(2,1)} %get-tuple-element.190.d_own_ref), channel_id=1, source_target_pairs={{0,16},{16,0},{1,17},{17,1},{2,18},{18,2},{3,19},{19,3},{4,20},{20... | collective-permute-start | bytes 3538952 | tf_op jit(solution)/shard_map/ppermute | solution.py:792
  209.3 45.4 %collective-permute-start.37 = (bf16[1536,768]{1,0:T(8,128)(2,1)S(1)}, bf16[1536,768]{1,0:T(8,128)(2,1)}, u32[]{:S(2)}, u32[]{:S(2)}) collective-permute-start(bf16[1536,768]{1,0:T(8,128)(2,1)S(1)} %convolution_convert_fusion), channel_id=1, source_target_pairs={{0,16},{16,0},{1,17},{17,1},{2,18},{18,2},{3,19},{19,3},{4,20},{20... | collective-permute-start | bytes 7077896 | tf_op jit(solution)/shard_map/ppermute | solution.py:792
  209.8 20.2 %collective-permute-start.31 = (bf16[64,768]{1,0:T(8,128)(2,1)S(1)}, bf16[64,768]{1,0:T(8,128)(2,1)S(1)}, u32[]{:S(2)}, u32[]{:S(2)}) collective-permute-start(bf16[64,768]{1,0:T(8,128)(2,1)S(1)} %copy-done.33), channel_id=1, source_target_pairs={{0,0},{1,1},{2,2},{3,3},{4,4},{5,5},{6,6},{7,7},{16,8},{17,9},{18,... | collective-permute-start | bytes 294920 | tf_op jit(solution)/shard_map/ppermute | solution.py:816
  210.5 19.5 %collective-permute-start.32 = (bf16[64,768]{1,0:T(8,128)(2,1)S(1)}, bf16[64,768]{1,0:T(8,128)(2,1)S(1)}, u32[]{:S(2)}, u32[]{:S(2)}) collective-permute-start(bf16[64,768]{1,0:T(8,128)(2,1)S(1)} %copy-done.32), channel_id=1, source_target_pairs={{4,0},{5,1},{6,2},{7,3},{0,4},{1,5},{2,6},{3,7},{20,8},{21,9},{22,... | collective-permute-start | bytes 294920 | tf_op jit(solution)/shard_map/ppermute | solution.py:816
  221.4 16.5 %all-to-all-start.5 = ((bf16[4,4,32,768]{3,2,1,0:T(8,128)(2,1)}), bf16[4,4,32,768]{3,2,1,0:T(8,128)(2,1)}, u32[]{:S(2)}, u32[]{:S(2)}) async-start(bf16[4,4,32,768]{3,2,1,0:T(8,128)(2,1)} %get-tuple-element.199), calls=%async_computation.5 | async-start | bytes 1572864 | tf_op jit(solution)/shard_map/all_to_all | solution.py:1135
  230.0 18.8 %copy-start.34 = (bf16[64,768]{1,0:T(8,128)(2,1)}, bf16[64,768]{1,0:T(8,128)(2,1)S(1)}, u32[]{:S(2)}) copy-start(bf16[64,768]{1,0:T(8,128)(2,1)S(1)} %collective-permute-done.31.out_first_ref) | copy-start | bytes 294916
  230.0 18.8 %copy-start.35 = (bf16[64,768]{1,0:T(8,128)(2,1)}, bf16[64,768]{1,0:T(8,128)(2,1)S(1)}, u32[]{:S(2)}) copy-start(bf16[64,768]{1,0:T(8,128)(2,1)S(1)} %collective-permute-done.32.out_second_ref) | copy-start | bytes 294916
  237.8 21.5 %all-to-all-start.6 = ((bf16[16,24,768]{2,1,0:T(8,128)(2,1)}), bf16[16,24,768]{2,1,0:T(8,128)(2,1)}, u32[]{:S(2)}, u32[]{:S(2)}) async-start(bf16[16,24,768]{2,1,0:T(8,128)(2,1)} %weight_grads.1), calls=%async_computation.6 | async-start | bytes 1179648 | tf_op jit(solution)/shard_map/all_to_all | solution.py:749
  244.1 4.7 %collective-permute-start.33 = (bf16[2,32,768]{2,1,0:T(8,128)(2,1)}, bf16[2,32,768]{2,1,0:T(8,128)(2,1)S(1)}, u32[]{:S(2)}, u32[]{:S(2)}) collective-permute-start(bf16[2,32,768]{2,1,0:T(8,128)(2,1)} %get-tuple-element.206), channel_id=1, source_target_pairs={{0,16},{16,0},{1,17},{17,1},{2,18},{18,2},{3,19},{19,3},{4,20},{20... | collective-permute-start | bytes 294920 | tf_op jit(solution)/shard_map/ppermute | solution.py:792
  251.6 7.7 %collective-permute-start.34 = (bf16[64,768]{1,0:T(8,128)(2,1)}, bf16[64,768]{1,0:T(8,128)(2,1)S(1)}, u32[]{:S(2)}, u32[]{:S(2)}) collective-permute-start(bf16[64,768]{1,0:T(8,128)(2,1)} %get-tuple-element.207), channel_id=1, source_target_pairs={{0,0},{1,1},{2,2},{3,3},{4,4},{5,5},{6,6},{7,7},{16,8},{17,9},{18,... | collective-permute-start | bytes 294920 | tf_op jit(solution)/shard_map/ppermute | solution.py:816
  253.1 6.1 %collective-permute-start.35 = (bf16[64,768]{1,0:T(8,128)(2,1)}, bf16[64,768]{1,0:T(8,128)(2,1)S(1)}, u32[]{:S(2)}, u32[]{:S(2)}) collective-permute-start(bf16[64,768]{1,0:T(8,128)(2,1)} %get-tuple-element.208), channel_id=1, source_target_pairs={{4,0},{5,1},{6,2},{7,3},{0,4},{1,5},{2,6},{3,7},{20,8},{21,9},{22,... | collective-permute-start | bytes 294920 | tf_op jit(solution)/shard_map/ppermute | solution.py:816
  261.3 4.8 %collective-permute-start.38 = (bf16[3,24,768]{2,1,0:T(8,128)(2,1)}, bf16[3,24,768]{2,1,0:T(8,128)(2,1)S(1)}, u32[]{:S(2)}, u32[]{:S(2)}) collective-permute-start(bf16[3,24,768]{2,1,0:T(8,128)(2,1)} %get-tuple-element.217), channel_id=1, source_target_pairs={{0,16},{16,0},{1,17},{17,1},{2,18},{18,2},{3,19},{19,3},{4,20},{20... | collective-permute-start | bytes 331784 | tf_op jit(solution)/shard_map/ppermute | solution.py:792
  264.5 1.3 collective-permute-start.39
  264.5 1.6 collective-permute-start.40
  (34 other events, 102.1 us)

commit v3 on v2

--- a/solution.py
+++ b/solution.py
@@ -1098,7 +1098,8 @@
         compiler_params=limit,
         cost_estimate=cost(1),
     )(place, probs, queries, pair, *grads)
-    d_all, out_back = lax.optimization_barrier((d_all, out_back))
+    down_grad = both_reps(down_local)
+    d_all, out_back, down_grad = lax.optimization_barrier((d_all, out_back, down_grad))
     d_all_other = swap(d_all)
     out_first = to_tokens(out_first, 0, True)
     out_second = to_tokens(out_second, 1, True)
@@ -1164,9 +1165,8 @@
     grad_first = to_tokens(grad_first, 0, True)
     grad_second = to_tokens(grad_second, 1, True)
     up_grad = both_reps(up_local)
-    down_grad = both_reps(down_local)
-    final, grad_first, grad_second, up_grad, down_grad = lax.optimization_barrier(
-        (final, grad_first, grad_second, up_grad, down_grad)
+    final, grad_first, grad_second, up_grad = lax.optimization_barrier(
+        (final, grad_first, grad_second, up_grad)
     )
     four, four_low, small_sum = pl.pallas_call(
         partial(sum_kernel, seqs=seqs),

time: 271 us -> 269 us (level)
  waiting for transfers between devices: 61.1 us -> 57.5 us
  transfers between devices with their start and end apart: 47 -> 47, of which waited for: 15 -> 18; matrix products, arithmetic and copies ran while one was open for 6% -> 6% of each run, Pallas kernels for 19% -> 19%
where the time goes in v3:
time: 269 us; the launch traced here: 268 us
  starting transfers between devices  74.5 us (28%)
  Pallas kernels  67.9 us (25%)
  waiting for transfers between devices  57.5 us (21%)
  blocking collectives  42.7 us (16%)
  other arithmetic  9.95 us (4%)
  local copies, waits for them, and re-layouts  9.29 us (3%)
  matrix products  4.25 us (2%)
    all_to_all x1, blocking collectives, exchange(): return lax.all_to_all(value, 'sq', split_axis=0, concat_axis=0, tiled=True)  42.7 us
    all_to_all x5, starting transfers between devices, exchange(): return lax.all_to_all(value, 'sq', split_axis=0, concat_axis=0, tiled=True)  31.2 us
    all_to_all x5, waiting for transfers between devices, exchange(): return lax.all_to_all(value, 'sq', split_axis=0, concat_axis=0, tiled=True)  30.8 us
    ppermute x17, starting transfers between devices, plane(): return lax.ppermute(value, ('rep', 'sq'), moves)  20.6 us
    pallas_call x1, Pallas kernels, local(): pl.pallas_call(partial(forward_kernel, shard=shard, all_heads=heads, **si...  15.1 us
    ppermute x8, starting transfers between devices, to_tokens(): return lax.ppermute(value, ('rep', 'sq'), moves)  12 us
    ppermute x17, waiting for transfers between devices, plane(): return lax.ppermute(value, ('rep', 'sq'), moves)  11.9 us
    pallas_call x1, Pallas kernels, local(): pl.pallas_call(partial(backward_kernel, **sizes), name='attention_backwar...  11 us
  transfers between devices with their start and end apart: 47, of which 18 were waited for; matrix products, arithmetic and copies ran while one was open for 6% of the time, Pallas kernels for 19%

profile of v3, /device:TPU:0, one launch (start us, length us, event | category | flops | bytes accessed | tf_op | source)
XLA Modules:
  0.0 267.5 jit_solution(6784059460117694333)
XLA Ops:
  0.7 0.8 pad_add_fusion.marks_ref
  1.9 1.0 dynamic-slice_bitcast_fusion.2
  2.9 0.7 collective-permute-start.1
  3.5 2.7 %collective-permute-start.2 = (bf16[64,768]{1,0:T(8,128)(2,1)S(1)}, bf16[64,768]{1,0:T(8,128)(2,1)S(1)}, u32[]{:S(2)}, u32[]{:S(2)}) collective-permute-start(bf16[64,768]{1,0:T(8,128)(2,1)S(1)} %get-tuple-element.236), channel_id=1, source_target_pairs={{0,4},{1,5},{2,6},{3,7},{4,0},{5,1},{6,2},{7,3},{8,20},{9,21},{10,... | collective-permute-start | bytes 294920 | tf_op jit(solution)/shard_map/ppermute | solution.py:816
  6.3 0.7 stack.46.place_ref
  7.5 2.2 pack.1
  9.7 10.1 %all-to-all-start = ((bf16[16,24,768]{2,1,0:T(8,128)(2,1)}), bf16[16,24,768]{2,1,0:T(8,128)(2,1)S(1)}, u32[]{:S(2)}, u32[]{:S(2)}) async-start(bf16[16,24,768]{2,1,0:T(8,128)(2,1)} %pack.1), calls=%async_computation | async-start | bytes 1179648 | tf_op jit(solution)/shard_map/all_to_all | solution.py:749
  19.9 2.0 collective-permute-start.3
  21.8 1.5 collective-permute-start.4
  23.4 0.7 collective-permute-start.6
  24.1 2.0 collective-permute-start.7
  26.1 4.1 %collective-permute-done.7.second_ref = bf16[64,768]{1,0:T(8,128)(2,1)S(1)} collective-permute-done((bf16[64,768]{1,0:T(8,128)(2,1)S(1)}, bf16[64,768]{1,0:T(8,128)(2,1)S(1)}, u32[]{:S(2)}, u32[]{:S(2)}) %collective-permute-start.7) | collective-permute-done | bytes 98336 | tf_op jit(solution)/shard_map/ppermute | solution.py:816
  30.2 2.8 %collective-permute-done.3.refs_1_ = bf16[2,64,768]{2,1,0:T(8,128)(2,1)S(1)} collective-permute-done((bf16[2,64,768]{2,1,0:T(8,128)(2,1)S(1)}, bf16[2,64,768]{2,1,0:T(8,128)(2,1)S(1)}, u32[]{:S(2)}, u32[]{:S(2)}) %collective-permute-start.3) | collective-permute-done | bytes 196640 | tf_op jit(solution)/shard_map/ppermute | solution.py:802
  33.2 3.5 %collective-permute-done.5.refs_3_ = bf16[2,64,768]{2,1,0:T(8,128)(2,1)S(1)} collective-permute-done((bf16[2,64,768]{2,1,0:T(8,128)(2,1)S(1)}, bf16[2,64,768]{2,1,0:T(8,128)(2,1)S(1)}, u32[]{:S(2)}, u32[]{:S(2)}) %collective-permute-start.5) | collective-permute-done | bytes 196640 | tf_op jit(solution)/shard_map/ppermute | solution.py:802
  36.7 1.0 broadcast_in_dim.2
  37.6 1.5 collective-permute-start.8
  40.8 5.4 %all-to-all-start.1 = ((bf16[16,48,384]{2,1,0:T(8,128)(2,1)}), bf16[16,48,384]{2,1,0:T(8,128)(2,1)S(1)}, u32[]{:S(2)}, u32[]{:S(2)}) async-start(bf16[16,48,384]{2,1,0:T(8,128)(2,1)} %broadcast_in_dim.2), calls=%async_computation.1 | async-start | bytes 1179648 | tf_op jit(solution)/shard_map/all_to_all | solution.py:749
  47.0 0.7 copy-done.28
  47.7 15.1 %attention_forward.1 = (bf16[3,512,1024]{2,1,0:T(8,128)(2,1)}, bf16[512,192]{1,0:T(8,128)(2,1)}, bf16[1024,384]{1,0:T(8,128)(2,1)}, bf16[16,64,768]{2,1,0:T(8,12...) custom-call(s32[8]{0:T(128)} %stack.46.place_ref, ...), custom_call_target="tpu_custom_call" | custom-call | flops 54000001024 | bytes 60000000 | tf_op jit(solution)/shard_map/attention_forward/pallas_call | solution.py:926
  63.5 1.9 collective-permute-start.15
  65.4 1.5 collective-permute-start.17
  67.6 3.2 %collective-permute-start.19 = (bf16[2,32,192]{2,1,0:T(8,128)(2,1)}, bf16[2,32,192]{2,1,0:T(8,128)(2,1)S(1)}, u32[]{:S(2)}, u32[]{:S(2)}) collective-permute-start(bf16[2,32,192]{2,1,0:T(8,128)(2,1)} %get-tuple-element.157), channel_id=1, source_target_pairs={{0,3},{1,2},{2,1},{3,0},{4,7},{5,6},{6,5},{7,4},{8,11},{9,10},{10,... | collective-permute-start | bytes 73736 | tf_op jit(solution)/shard_map/ppermute | solution.py:802
  70.8 2.0 collective-permute-done.19.refs_6_
  72.9 2.4 collective-permute-done.20.refs_7_
  76.1 4.0 %router_and_dispatch.1 = (bf16[16,64,768]{2,1,0:T(8,128)(2,1)}, bf16[128,768]{1,0:T(8,128)(2,1)}, f32[128,768]{1,0:T(8,128)}, bf16[128,768]{1,0:T(8,128)(2,1)}, ...) custom-call(s32[8]{0:T(128)} %stack.46.place_ref, ...), custom_call_target="tpu_custom_call" | custom-call | flops 4499999744 | bytes 5000000 | tf_op jit(solution)/shard_map/router_and_dispatch/pallas_call | solution.py:971
  80.1 42.7 %all_to_all.35.arrived_ref = bf16[16,64,768]{2,1,0:T(8,128)(2,1)} all-to-all(bf16[16,64,768]{2,1,0:T(8,128)(2,1)} %get-tuple-element.159), channel_id=1, replica_groups=mesh['rep'=2,'sq'=16] {'sq'}, dimensions={0} | all-to-all | bytes 3145728 | tf_op jit(solution)/shard_map/all_to_all | solution.py:749
  122.8 9.5 %experts.1 = (bf16[16,64,768]{2,1,0:T(8,128)(2,1)}, bf16[512,1536]{1,0:T(8,128)(2,1)}, bf16[512,1536]{1,0:T(8,128)(2,1)}) custom-call(bf16[16,64,768]{2,1,0:T(8,128)(2,1)} %all_to_all.35.arrived_ref, bf16[768,1536]{1,0:T(8,128)(2,1)} %up_ref.1, bf16[1536,768]{1,0:T(8,128)(2,1)} %down_ref.1), custom_call_target="tpu_custom_call" | custom-call | flops 7200000000 | bytes 8000000 | tf_op jit(solution)/shard_map/experts/pallas_call | solution.py:1008
  132.3 4.5 %all-to-all-start.3 = ((bf16[16,64,768]{2,1,0:T(8,128)(2,1)}), bf16[16,64,768]{2,1,0:T(8,128)(2,1)}, u32[]{:S(2)}, u32[]{:S(2)}) async-start(bf16[16,64,768]{2,1,0:T(8,128)(2,1)} %get-tuple-element.160), calls=%async_computation.3 | async-start | bytes 3145728 | tf_op jit(solution)/shard_map/all_to_all | solution.py:749
  137.0 1.3 copy-done.49
  138.3 1.4 convolution_convert_fusion.1
  139.7 2.8 %convolution_convert_fusion = bf16[1536,768]{1,0:T(8,128)(2,1)} fusion(bf16[512,1536]{1,0:T(8,128)(2,1)S(1)} %copy-done.50, bf16[512,768]{1,0:T(8,128)(2,1)S(1)} %bitcast.31), kind=kOutput, calls=%fused_computation.2 | convolution fusion | flops 1209139200 | bytes 4718592 | tf_op jit(solution)/shard_map/dot_general | solution.py:22
  142.6 27.6 %all-to-all-done.3.returned_ref = bf16[16,64,768]{2,1,0:T(8,128)(2,1)} async-done(((bf16[16,64,768]{2,1,0:T(8,128)(2,1)}), bf16[16,64,768]{2,1,0:T(8,128)(2,1)}, u32[]{:S(2)}, u32[]{:S(2)}) %all-to-all-start.3) | async-done | bytes 1572896 | tf_op jit(solution)/shard_map/all_to_all | solution.py:749
  170.7 4.6 %combine_and_turn.1 = (bf16[2,32,192]{2,1,0:T(8,128)(2,1)}, bf16[2,32,192]{2,1,0:T(8,128)(2,1)}, bf16[2,32,192]{2,1,0:T(8,128)(2,1)}, bf16[2,32,192]{2,1,0:T(8,1...) custom-call(s32[8]{0:T(128)} %stack.46.place_ref, ...), custom_call_target="tpu_custom_call" | custom-call | flops 4499999744 | bytes 5000000 | tf_op jit(solution)/shard_map/combine_and_turn/pallas_call | solution.py:1033
  175.8 0.7 collective-permute-start.22
  176.5 0.8 collective-permute-start.23
  177.3 2.7 collective-permute-start.24
  180.2 0.9 collective-permute-start.25
  181.2 2.7 %collective-permute-start.26 = (bf16[2,32,192]{2,1,0:T(8,128)(2,1)}, bf16[2,32,192]{2,1,0:T(8,128)(2,1)S(1)}, u32[]{:S(2)}, u32[]{:S(2)}) collective-permute-start(bf16[2,32,192]{2,1,0:T(8,128)(2,1)} %get-tuple-element.176), channel_id=1, source_target_pairs={{0,3},{1,2},{2,1},{3,0},{4,7},{5,6},{6,5},{7,4},{8,11},{9,10},{10,... | collective-permute-start | bytes 73736 | tf_op jit(solution)/shard_map/ppermute | solution.py:802
  183.9 1.4 collective-permute-start.27
  185.3 2.9 %out_grad.1 = bf16[16,24,768]{2,1,0:T(8,128)(2,1)} custom-call(s32[8]{0:T(128)} %stack.46.place_ref, bf16[128,768]{1,0:T(8,128)(2,1)} %get-tuple-element.178.attended_ref, bf16[128,768]{1,0:T(8,128)(2,1)} %copy-done.23, bf16[128,768]{1,0:T(8,128)(2,1)} %get-tuple-element.179.d_ref, bf16[128,768]{1,0:T(8,128)(2,1)} %copy-done.26), custom_call_target="tpu_custom_call" | custom-call | flops 2700000000 | bytes 3000000 | tf_op jit(solution)/shard_map/out_grad/pallas_call | solution.py:1069
  188.7 5.5 %all-to-all-start.4 = ((bf16[16,24,768]{2,1,0:T(8,128)(2,1)}), bf16[16,24,768]{2,1,0:T(8,128)(2,1)S(1)}, u32[]{:S(2)}, u32[]{:S(2)}) async-start(bf16[16,24,768]{2,1,0:T(8,128)(2,1)} %out_grad.1), calls=%async_computation.4 | async-start | bytes 1179648 | tf_op jit(solution)/shard_map/all_to_all | solution.py:749
  194.5 11.0 %attention_backward.1 = (bf16[16,64,576]{2,1,0:T(8,128)(2,1)}, f32[3,32,128]{2,1,0:T(8,128)}) custom-call(s32[8]{0:T(128)} %stack.46.place_ref, bf16[3,512,1024]{2,1,0:T(8,128)(2,1)} %get-tuple-element.133.probs_ref, bf16[512,192]{1,0:T(8,128)(2,1)} %get-tuple-element.134.query_ref, bf16[1024,384]{1,0:T(8,128)(2,1)} %get-tuple-element.135.pair_ref, ...), custom_call_target="tpu_custom_call" | custom-call | flops 900000000 | bytes 1000000 | tf_op jit(solution)/shard_map/attention_backward/pallas_call | solution.py:1081
  205.5 4.5 %convert_add_fusion.1 = f32[1536,768]{1,0:T(8,128)} fusion(bf16[1536,768]{1,0:T(8,128)(2,1)} %collective-permute-done.30, bf16[1536,768]{1,0:T(8,128)(2,1)S(1)} %copy-done.2), kind=kLoop, calls=%fused_computation.1 | loop fusion | flops 3538944 | bytes 9437184 | tf_op jit(solution)/shard_map/add | solution.py:1029
  210.1 0.7 all-to-all-done.4
  210.7 0.7 collective-permute-start.32
  211.4 1.9 collective-permute-start.33
  213.3 0.7 collective-permute-done.31.d_other_ref
  214.0 1.1 copy-done.3
  215.0 5.9 %d_normed.1 = (bf16[4,4,32,768]{3,2,1,0:T(8,128)(2,1)}, bf16[16,64,576]{2,1,0:T(8,128)(2,1)}, f32[1,768]{1,0:T(1,128)}) custom-call(s32[8]{0:T(128)} %stack.46.place_ref, bf16[16,64,576]{2,1,0:T(8,128)(2,1)} %get-tuple-element.191.d_own_ref, bf16[16,64,576]{2,1,0:T(8,128)(2,1)} %copy-done.3, bf16[768,576]{1,0:T(8,128)(2,1)} %get-tuple-element.192.weight_ref, ...), custom_call_target="tpu_custom_call" | custom-call | flops 900000000 | bytes 1000000 | tf_op jit(solution)/shard_map/d_normed/pallas_call | solution.py:1109
  220.9 4.2 %all-to-all-start.5 = ((bf16[4,4,32,768]{3,2,1,0:T(8,128)(2,1)}), bf16[4,4,32,768]{3,2,1,0:T(8,128)(2,1)}, u32[]{:S(2)}, u32[]{:S(2)}) async-start(bf16[4,4,32,768]{3,2,1,0:T(8,128)(2,1)} %get-tuple-element.200), calls=%async_computation.5 | async-start | bytes 1572864 | tf_op jit(solution)/shard_map/all_to_all | solution.py:1136
  225.1 4.4 %weight_grads.1 = bf16[16,24,768]{2,1,0:T(8,128)(2,1)} custom-call(s32[8]{0:T(128)} %stack.46.place_ref, bf16[16,64,576]{2,1,0:T(8,128)(2,1)} %get-tuple-element.195.d_sum, bf16[16,64,768]{2,1,0:T(8,128)(2,1)} %get-tuple-element.193.normed_ref, f32[1,768]{1,0:T(1,128)} %get-tuple-element.196.gain_sum, f32[1,768]{1,0:T(1,128)} %get-tuple-element.197.gain_two_ref, ...), custom_call_target="tpu_custom_call" | custom-call | flops 7200000000 | bytes 8000000 | tf_op jit(solution)/shard_map/weight_grads/pallas_call | solution.py:1122
  229.6 6.8 %all-to-all-done.5.rows_ref = bf16[4,4,32,768]{3,2,1,0:T(8,128)(2,1)} async-done(((bf16[4,4,32,768]{3,2,1,0:T(8,128)(2,1)}), bf16[4,4,32,768]{3,2,1,0:T(8,128)(2,1)}, u32[]{:S(2)}, u32[]{:S(2)}) %all-to-all-start.5) | async-done | bytes 786464 | tf_op jit(solution)/shard_map/all_to_all | solution.py:1136
  236.3 5.7 %all-to-all-start.6 = ((bf16[16,24,768]{2,1,0:T(8,128)(2,1)}), bf16[16,24,768]{2,1,0:T(8,128)(2,1)}, u32[]{:S(2)}, u32[]{:S(2)}) async-start(bf16[16,24,768]{2,1,0:T(8,128)(2,1)} %weight_grads.1), calls=%async_computation.6 | async-start | bytes 1179648 | tf_op jit(solution)/shard_map/all_to_all | solution.py:749
  242.0 1.9 d_normed_total.1
  243.9 1.5 collective-permute-done.34.given_ref
  246.1 2.1 token_grad.1
  248.2 1.5 collective-permute-start.35
  249.7 1.9 collective-permute-start.36
  251.6 4.5 %convert_add_fusion = f32[768,1536]{1,0:T(8,128)} fusion(bf16[768,1536]{1,0:T(8,128)(2,1)} %collective-permute-done.37, bf16[768,1536]{1,0:T(8,128)(2,1)S(1)} %convolution_convert_fusion.1), kind=kLoop, calls=%fused_computation | loop fusion | flops 3538944 | bytes 9437184 | tf_op jit(solution)/shard_map/add | solution.py:1029
  256.2 2.5 all-to-all-done.6.final_ref
  258.7 1.9 sums.1
  260.6 2.0 collective-permute-start.38
  263.3 0.8 collective-permute-done.39.out_other_ref
  265.0 2.4 input_grad.1
  (159 shorter events, 10.5 us)
Async XLA Ops:
  0.6 25.4 %copy-start = (bf16[48,768]{1,0:T(8,128)(2,1)S(1)}, bf16[48,768]{1,0:T(8,128)(2,1)}, u32[]{:S(2)}) copy-start(bf16[48,768]{1,0:T(8,128)(2,1)} %param.18) | copy-start | bytes 221188
  1.5 5.5 %collective-permute-start = (s32[2,128]{1,0:T(2,128)S(1)}, s32[2,128]{1,0:T(2,128)S(1)}, u32[]{:S(2)}, u32[]{:S(2)}) collective-permute-start(s32[2,128]{1,0:T(2,128)S(1)} %pad_add_fusion.marks_ref), channel_id=1, source_target_pairs={{0,16},{16,0},{1,17},{17,1},{2,18},{18,2},{3,19},{19,3},{4,20},{20... | collective-permute-start | bytes 3080 | tf_op jit(solution)/shard_map/ppermute | solution.py:792
  2.9 6.8 %collective-permute-start.1 = (bf16[64,768]{1,0:T(8,128)(2,1)S(1)}, bf16[64,768]{1,0:T(8,128)(2,1)S(1)}, u32[]{:S(2)}, u32[]{:S(2)}) collective-permute-start(bf16[64,768]{1,0:T(8,128)(2,1)S(1)} %get-tuple-element.237), channel_id=1, source_target_pairs={{0,0},{1,1},{2,2},{3,3},{4,4},{5,5},{6,6},{7,7},{8,16},{9,17},{10,... | collective-permute-start | bytes 294920 | tf_op jit(solution)/shard_map/ppermute | solution.py:816
  3.5 6.1 %collective-permute-start.2 = (bf16[64,768]{1,0:T(8,128)(2,1)S(1)}, bf16[64,768]{1,0:T(8,128)(2,1)S(1)}, u32[]{:S(2)}, u32[]{:S(2)}) collective-permute-start(bf16[64,768]{1,0:T(8,128)(2,1)S(1)} %get-tuple-element.236), channel_id=1, source_target_pairs={{0,4},{1,5},{2,6},{3,7},{4,0},{5,1},{6,2},{7,3},{8,20},{9,21},{10,... | collective-permute-start | bytes 294920 | tf_op jit(solution)/shard_map/ppermute | solution.py:816
  7.5 15.9 %copy-start.6 = (bf16[2,64,768]{2,1,0:T(8,128)(2,1)S(1)}, bf16[2,64,768]{2,1,0:T(8,128)(2,1)}, u32[]{:S(2)}) copy-start(bf16[2,64,768]{2,1,0:T(8,128)(2,1)} %param.27) | copy-start | bytes 589828
  9.7 27.0 %all-to-all-start = ((bf16[16,24,768]{2,1,0:T(8,128)(2,1)}), bf16[16,24,768]{2,1,0:T(8,128)(2,1)S(1)}, u32[]{:S(2)}, u32[]{:S(2)}) async-start(bf16[16,24,768]{2,1,0:T(8,128)(2,1)} %pack.1), calls=%async_computation | async-start | bytes 1179648 | tf_op jit(solution)/shard_map/all_to_all | solution.py:749
  19.8 26.4 %copy-start.7 = (bf16[2,64,768]{2,1,0:T(8,128)(2,1)}, bf16[2,64,768]{2,1,0:T(8,128)(2,1)S(1)}, u32[]{:S(2)}) copy-start(bf16[2,64,768]{2,1,0:T(8,128)(2,1)S(1)} %maximum_select_fusion.refs_0_.x_ref) | copy-start | bytes 589828
  19.9 13.1 %collective-permute-start.3 = (bf16[2,64,768]{2,1,0:T(8,128)(2,1)S(1)}, bf16[2,64,768]{2,1,0:T(8,128)(2,1)S(1)}, u32[]{:S(2)}, u32[]{:S(2)}) collective-permute-start(bf16[2,64,768]{2,1,0:T(8,128)(2,1)S(1)} %maximum_select_fusion.refs_0_.x_ref), channel_id=1, source_target_pairs={{0,1},{1,0},{2,3},{3,2},{4,5},{5,4},{6,7},{7,6},{8,9},{9,8},{10,11... | collective-permute-start | bytes 589832 | tf_op jit(solution)/shard_map/ppermute | solution.py:802
  21.8 11.3 %collective-permute-start.4 = (bf16[2,64,768]{2,1,0:T(8,128)(2,1)S(1)}, bf16[2,64,768]{2,1,0:T(8,128)(2,1)S(1)}, u32[]{:S(2)}, u32[]{:S(2)}) collective-permute-start(bf16[2,64,768]{2,1,0:T(8,128)(2,1)S(1)} %maximum_select_fusion.refs_0_.x_ref), channel_id=1, source_target_pairs={{0,2},{1,3},{2,0},{3,1},{4,6},{5,7},{6,4},{7,5},{8,10},{9,11},{10,... | collective-permute-start | bytes 589832 | tf_op jit(solution)/shard_map/ppermute | solution.py:802
  23.3 13.4 %collective-permute-start.5 = (bf16[2,64,768]{2,1,0:T(8,128)(2,1)S(1)}, bf16[2,64,768]{2,1,0:T(8,128)(2,1)S(1)}, u32[]{:S(2)}, u32[]{:S(2)}) collective-permute-start(bf16[2,64,768]{2,1,0:T(8,128)(2,1)S(1)} %maximum_select_fusion.refs_0_.x_ref), channel_id=1, source_target_pairs={{0,3},{1,2},{2,1},{3,0},{4,7},{5,6},{6,5},{7,4},{8,11},{9,10},{10,... | collective-permute-start | bytes 589832 | tf_op jit(solution)/shard_map/ppermute | solution.py:802
  23.4 2.7 collective-permute-start.6
  24.1 6.1 %collective-permute-start.7 = (bf16[64,768]{1,0:T(8,128)(2,1)S(1)}, bf16[64,768]{1,0:T(8,128)(2,1)S(1)}, u32[]{:S(2)}, u32[]{:S(2)}) collective-permute-start(bf16[64,768]{1,0:T(8,128)(2,1)S(1)} %get-tuple-element.234), channel_id=1, source_target_pairs={{0,4},{1,5},{2,6},{3,7},{4,0},{5,1},{6,2},{7,3},{8,20},{9,21},{10,... | collective-permute-start | bytes 294920 | tf_op jit(solution)/shard_map/ppermute | solution.py:816
  26.1 36.8 %copy-start.30 = (bf16[64,768]{1,0:T(8,128)(2,1)}, bf16[64,768]{1,0:T(8,128)(2,1)S(1)}, u32[]{:S(2)}) copy-start(bf16[64,768]{1,0:T(8,128)(2,1)S(1)} %collective-permute-done.6.first_ref) | copy-start | bytes 294916
  33.0 13.3 %copy-start.20 = (bf16[2,64,768]{2,1,0:T(8,128)(2,1)}, bf16[2,64,768]{2,1,0:T(8,128)(2,1)S(1)}, u32[]{:S(2)}) copy-start(bf16[2,64,768]{2,1,0:T(8,128)(2,1)S(1)} %collective-permute-done.3.refs_1_) | copy-start | bytes 589828
  33.2 13.1 %copy-start.21 = (bf16[2,64,768]{2,1,0:T(8,128)(2,1)}, bf16[2,64,768]{2,1,0:T(8,128)(2,1)S(1)}, u32[]{:S(2)}) copy-start(bf16[2,64,768]{2,1,0:T(8,128)(2,1)S(1)} %collective-permute-done.4.refs_2_) | copy-start | bytes 589828
  36.7 9.6 %copy-start.22 = (bf16[2,64,768]{2,1,0:T(8,128)(2,1)}, bf16[2,64,768]{2,1,0:T(8,128)(2,1)S(1)}, u32[]{:S(2)}) copy-start(bf16[2,64,768]{2,1,0:T(8,128)(2,1)S(1)} %collective-permute-done.5.refs_3_) | copy-start | bytes 589828
  36.7 9.6 %copy-start.5 = (bf16[16,24,768]{2,1,0:T(8,128)(2,1)}, bf16[16,24,768]{2,1,0:T(8,128)(2,1)S(1)}, u32[]{:S(2)}) copy-start(bf16[16,24,768]{2,1,0:T(8,128)(2,1)S(1)} %all-to-all-done.own_ref) | copy-start | bytes 1769476
  37.6 3.2 %collective-permute-start.8 = (bf16[16,24,768]{2,1,0:T(8,128)(2,1)S(1)}, bf16[16,24,768]{2,1,0:T(8,128)(2,1)S(1)}, u32[]{:S(2)}, u32[]{:S(2)}) collective-permute-start(bf16[16,24,768]{2,1,0:T(8,128)(2,1)S(1)} %all-to-all-done.own_ref), channel_id=1, source_target_pairs={{0,16},{16,0},{1,17},{17,1},{2,18},{18,2},{3,19},{19,3},{4,20},{20... | collective-permute-start | bytes 1769480 | tf_op jit(solution)/shard_map/ppermute | solution.py:792
  39.2 7.0 %collective-permute-start.9 = (bf16[2,64,768]{2,1,0:T(8,128)(2,1)S(1)}, bf16[2,64,768]{2,1,0:T(8,128)(2,1)S(1)}, u32[]{:S(2)}, u32[]{:S(2)}) collective-permute-start(bf16[2,64,768]{2,1,0:T(8,128)(2,1)S(1)} %maximum_select_fusion.refs_0_.x_ref), channel_id=1, source_target_pairs={{0,16},{16,0},{1,17},{17,1},{2,18},{18,2},{3,19},{19,3},{4,20},{20... | collective-permute-start | bytes 589832 | tf_op jit(solution)/shard_map/ppermute | solution.py:792
  39.2 7.0 %collective-permute-start.10 = (bf16[2,64,768]{2,1,0:T(8,128)(2,1)S(1)}, bf16[2,64,768]{2,1,0:T(8,128)(2,1)S(1)}, u32[]{:S(2)}, u32[]{:S(2)}) collective-permute-start(bf16[2,64,768]{2,1,0:T(8,128)(2,1)S(1)} %collective-permute-done.3.refs_1_), channel_id=1, source_target_pairs={{0,16},{16,0},{1,17},{17,1},{2,18},{18,2},{3,19},{19,3},{4,20},{20... | collective-permute-start | bytes 589832 | tf_op jit(solution)/shard_map/ppermute | solution.py:792
  39.7 6.5 %collective-permute-start.11 = (bf16[2,64,768]{2,1,0:T(8,128)(2,1)S(1)}, bf16[2,64,768]{2,1,0:T(8,128)(2,1)S(1)}, u32[]{:S(2)}, u32[]{:S(2)}) collective-permute-start(bf16[2,64,768]{2,1,0:T(8,128)(2,1)S(1)} %collective-permute-done.4.refs_2_), channel_id=1, source_target_pairs={{0,16},{16,0},{1,17},{17,1},{2,18},{18,2},{3,19},{19,3},{4,20},{20... | collective-permute-start | bytes 589832 | tf_op jit(solution)/shard_map/ppermute | solution.py:792
  39.7 6.6 %collective-permute-start.12 = (bf16[2,64,768]{2,1,0:T(8,128)(2,1)S(1)}, bf16[2,64,768]{2,1,0:T(8,128)(2,1)S(1)}, u32[]{:S(2)}, u32[]{:S(2)}) collective-permute-start(bf16[2,64,768]{2,1,0:T(8,128)(2,1)S(1)} %collective-permute-done.5.refs_3_), channel_id=1, source_target_pairs={{0,16},{16,0},{1,17},{17,1},{2,18},{18,2},{3,19},{19,3},{4,20},{20... | collective-permute-start | bytes 589832 | tf_op jit(solution)/shard_map/ppermute | solution.py:792
  40.8 22.1 %all-to-all-start.1 = ((bf16[16,48,384]{2,1,0:T(8,128)(2,1)}), bf16[16,48,384]{2,1,0:T(8,128)(2,1)S(1)}, u32[]{:S(2)}, u32[]{:S(2)}) async-start(bf16[16,48,384]{2,1,0:T(8,128)(2,1)} %broadcast_in_dim.2), calls=%async_computation.1 | async-start | bytes 1179648 | tf_op jit(solution)/shard_map/all_to_all | solution.py:749
  62.9 12.3 %copy-start.4 = (bf16[16,48,384]{2,1,0:T(8,128)(2,1)}, bf16[16,48,384]{2,1,0:T(8,128)(2,1)S(1)}, u32[]{:S(2)}) copy-start(bf16[16,48,384]{2,1,0:T(8,128)(2,1)S(1)} %all-to-all-done.1) | copy-start | bytes 1769476
  62.9 12.3 %collective-permute-start.13 = (bf16[768,384]{1,0:T(8,128)(2,1)S(1)}, bf16[768,384]{1,0:T(8,128)(2,1)S(1)}, u32[]{:S(2)}, u32[]{:S(2)}) collective-permute-start(bf16[768,384]{1,0:T(8,128)(2,1)S(1)} %bitcast.33), channel_id=1, source_target_pairs={{0,16},{16,0},{1,17},{17,1},{2,18},{18,2},{3,19},{19,3},{4,20},{20... | collective-permute-start | bytes 1769480 | tf_op jit(solution)/shard_map/ppermute | solution.py:792
  63.0 3.9 %collective-permute-start.14 = (bf16[2,32,192]{2,1,0:T(8,128)(2,1)}, bf16[2,32,192]{2,1,0:T(8,128)(2,1)S(1)}, u32[]{:S(2)}, u32[]{:S(2)}) collective-permute-start(bf16[2,32,192]{2,1,0:T(8,128)(2,1)} %get-tuple-element.152), channel_id=1, source_target_pairs={{0,16},{1,17},{2,18},{3,19},{4,20},{5,21},{6,22},{7,23},{8,24},{9,... | collective-permute-start | bytes 73736 | tf_op jit(solution)/shard_map/ppermute | solution.py:802
  63.5 4.1 %collective-permute-start.15 = (bf16[2,32,192]{2,1,0:T(8,128)(2,1)}, bf16[2,32,192]{2,1,0:T(8,128)(2,1)S(1)}, u32[]{:S(2)}, u32[]{:S(2)}) collective-permute-start(bf16[2,32,192]{2,1,0:T(8,128)(2,1)} %get-tuple-element.153), channel_id=1, source_target_pairs={{0,1},{1,0},{2,3},{3,2},{4,5},{5,4},{6,7},{7,6},{8,9},{9,8},{10,11... | collective-permute-start | bytes 73736 | tf_op jit(solution)/shard_map/ppermute | solution.py:802
  65.4 5.4 %collective-permute-start.16 = (bf16[2,32,192]{2,1,0:T(8,128)(2,1)}, bf16[2,32,192]{2,1,0:T(8,128)(2,1)S(1)}, u32[]{:S(2)}, u32[]{:S(2)}) collective-permute-start(bf16[2,32,192]{2,1,0:T(8,128)(2,1)} %get-tuple-element.154), channel_id=1, source_target_pairs={{0,17},{1,16},{2,19},{3,18},{4,21},{5,20},{6,23},{7,22},{8,25},{9,... | collective-permute-start | bytes 73736 | tf_op jit(solution)/shard_map/ppermute | solution.py:802
  65.4 5.4 %collective-permute-start.17 = (bf16[2,32,192]{2,1,0:T(8,128)(2,1)}, bf16[2,32,192]{2,1,0:T(8,128)(2,1)S(1)}, u32[]{:S(2)}, u32[]{:S(2)}) collective-permute-start(bf16[2,32,192]{2,1,0:T(8,128)(2,1)} %get-tuple-element.155), channel_id=1, source_target_pairs={{0,2},{1,3},{2,0},{3,1},{4,6},{5,7},{6,4},{7,5},{8,10},{9,11},{10,... | collective-permute-start | bytes 73736 | tf_op jit(solution)/shard_map/ppermute | solution.py:802
  66.9 8.4 %copy-start.40 = (bf16[2,32,192]{2,1,0:T(8,128)(2,1)}, bf16[2,32,192]{2,1,0:T(8,128)(2,1)S(1)}, u32[]{:S(2)}) copy-start(bf16[2,32,192]{2,1,0:T(8,128)(2,1)S(1)} %collective-permute-done.14.refs_1_) | copy-start | bytes 73732
  66.9 3.9 %collective-permute-start.18 = (bf16[2,32,192]{2,1,0:T(8,128)(2,1)}, bf16[2,32,192]{2,1,0:T(8,128)(2,1)S(1)}, u32[]{:S(2)}, u32[]{:S(2)}) collective-permute-start(bf16[2,32,192]{2,1,0:T(8,128)(2,1)} %get-tuple-element.156), channel_id=1, source_target_pairs={{0,18},{1,19},{2,16},{3,17},{4,22},{5,23},{6,20},{7,21},{8,26},{9,... | collective-permute-start | bytes 73736 | tf_op jit(solution)/shard_map/ppermute | solution.py:802
  67.6 5.3 %collective-permute-start.19 = (bf16[2,32,192]{2,1,0:T(8,128)(2,1)}, bf16[2,32,192]{2,1,0:T(8,128)(2,1)S(1)}, u32[]{:S(2)}, u32[]{:S(2)}) collective-permute-start(bf16[2,32,192]{2,1,0:T(8,128)(2,1)} %get-tuple-element.157), channel_id=1, source_target_pairs={{0,3},{1,2},{2,1},{3,0},{4,7},{5,6},{6,5},{7,4},{8,11},{9,10},{10,... | collective-permute-start | bytes 73736 | tf_op jit(solution)/shard_map/ppermute | solution.py:802
  70.8 4.5 %collective-permute-start.20 = (bf16[2,32,192]{2,1,0:T(8,128)(2,1)}, bf16[2,32,192]{2,1,0:T(8,128)(2,1)S(1)}, u32[]{:S(2)}, u32[]{:S(2)}) collective-permute-start(bf16[2,32,192]{2,1,0:T(8,128)(2,1)} %get-tuple-element.158), channel_id=1, source_target_pairs={{0,19},{1,18},{2,17},{3,16},{4,23},{5,22},{6,21},{7,20},{8,27},{9,... | collective-permute-start | bytes 73736 | tf_op jit(solution)/shard_map/ppermute | solution.py:802
  132.3 37.8 %all-to-all-start.3 = ((bf16[16,64,768]{2,1,0:T(8,128)(2,1)}), bf16[16,64,768]{2,1,0:T(8,128)(2,1)}, u32[]{:S(2)}, u32[]{:S(2)}) async-start(bf16[16,64,768]{2,1,0:T(8,128)(2,1)} %get-tuple-element.160), calls=%async_computation.3 | async-start | bytes 3145728 | tf_op jit(solution)/shard_map/all_to_all | solution.py:749
  139.7 30.5 %copy-start.19 = (bf16[128,768]{1,0:T(8,128)(2,1)S(1)}, bf16[128,768]{1,0:T(8,128)(2,1)}, u32[]{:S(2)}) copy-start(bf16[128,768]{1,0:T(8,128)(2,1)} %get-tuple-element.178.attended_ref) | copy-start | bytes 589828
  170.2 35.3 %collective-permute-start.30 = (bf16[1536,768]{1,0:T(8,128)(2,1)}, bf16[1536,768]{1,0:T(8,128)(2,1)}, u32[]{:S(2)}, u32[]{:S(2)}) collective-permute-start(bf16[1536,768]{1,0:T(8,128)(2,1)} %convolution_convert_fusion), channel_id=1, source_target_pairs={{0,16},{16,0},{1,17},{17,1},{2,18},{18,2},{3,19},{19,3},{4,20},{20... | collective-permute-start | bytes 7077896 | tf_op jit(solution)/shard_map/ppermute | solution.py:792
  170.2 6.3 %collective-permute-start.28 = (bf16[128,768]{1,0:T(8,128)(2,1)S(1)}, bf16[128,768]{1,0:T(8,128)(2,1)S(1)}, u32[]{:S(2)}, u32[]{:S(2)}) collective-permute-start(bf16[128,768]{1,0:T(8,128)(2,1)S(1)} %copy-done.19), channel_id=1, source_target_pairs={{0,16},{16,0},{1,17},{17,1},{2,18},{18,2},{3,19},{19,3},{4,20},{20... | collective-permute-start | bytes 589832 | tf_op jit(solution)/shard_map/ppermute | solution.py:792
  175.3 8.6 %collective-permute-start.29 = (bf16[128,768]{1,0:T(8,128)(2,1)}, bf16[128,768]{1,0:T(8,128)(2,1)S(1)}, u32[]{:S(2)}, u32[]{:S(2)}) collective-permute-start(bf16[128,768]{1,0:T(8,128)(2,1)} %get-tuple-element.179.d_ref), channel_id=1, source_target_pairs={{0,16},{16,0},{1,17},{17,1},{2,18},{18,2},{3,19},{19,3},{4,20},{20... | collective-permute-start | bytes 589832 | tf_op jit(solution)/shard_map/ppermute | solution.py:792
  175.3 1.9 collective-permute-start.21
  175.8 4.4 %collective-permute-start.22 = (bf16[2,32,192]{2,1,0:T(8,128)(2,1)}, bf16[2,32,192]{2,1,0:T(8,128)(2,1)S(1)}, u32[]{:S(2)}, u32[]{:S(2)}) collective-permute-start(bf16[2,32,192]{2,1,0:T(8,128)(2,1)} %get-tuple-element.172), channel_id=1, source_target_pairs={{0,1},{1,0},{2,3},{3,2},{4,5},{5,4},{6,7},{7,6},{8,9},{9,8},{10,11... | collective-permute-start | bytes 73736 | tf_op jit(solution)/shard_map/ppermute | solution.py:802
  176.5 8.8 %copy-start.23 = (bf16[128,768]{1,0:T(8,128)(2,1)}, bf16[128,768]{1,0:T(8,128)(2,1)S(1)}, u32[]{:S(2)}) copy-start(bf16[128,768]{1,0:T(8,128)(2,1)S(1)} %collective-permute-done.28.other_ref) | copy-start | bytes 589828
  176.5 4.7 %collective-permute-start.23 = (bf16[2,32,192]{2,1,0:T(8,128)(2,1)}, bf16[2,32,192]{2,1,0:T(8,128)(2,1)S(1)}, u32[]{:S(2)}, u32[]{:S(2)}) collective-permute-start(bf16[2,32,192]{2,1,0:T(8,128)(2,1)} %get-tuple-element.173), channel_id=1, source_target_pairs={{0,17},{1,16},{2,19},{3,18},{4,21},{5,20},{6,23},{7,22},{8,25},{9,... | collective-permute-start | bytes 73736 | tf_op jit(solution)/shard_map/ppermute | solution.py:802
  177.3 10.9 %copy-start.9 = (bf16[2,32,192]{2,1,0:T(8,128)(2,1)}, bf16[2,32,192]{2,1,0:T(8,128)(2,1)S(1)}, u32[]{:S(2)}) copy-start(bf16[2,32,192]{2,1,0:T(8,128)(2,1)S(1)} %collective-permute-done.21.refs_1_) | copy-start | bytes 73732
  177.3 10.9 %collective-permute-start.24 = (bf16[2,32,192]{2,1,0:T(8,128)(2,1)}, bf16[2,32,192]{2,1,0:T(8,128)(2,1)S(1)}, u32[]{:S(2)}, u32[]{:S(2)}) collective-permute-start(bf16[2,32,192]{2,1,0:T(8,128)(2,1)} %get-tuple-element.174), channel_id=1, source_target_pairs={{0,2},{1,3},{2,0},{3,1},{4,6},{5,7},{6,4},{7,5},{8,10},{9,11},{10,... | collective-permute-start | bytes 73736 | tf_op jit(solution)/shard_map/ppermute | solution.py:802
  180.2 7.9 %copy-start.10 = (bf16[2,32,192]{2,1,0:T(8,128)(2,1)}, bf16[2,32,192]{2,1,0:T(8,128)(2,1)S(1)}, u32[]{:S(2)}) copy-start(bf16[2,32,192]{2,1,0:T(8,128)(2,1)S(1)} %collective-permute-done.22.refs_2_) | copy-start | bytes 73732
  180.2 8.0 %collective-permute-start.25 = (bf16[2,32,192]{2,1,0:T(8,128)(2,1)}, bf16[2,32,192]{2,1,0:T(8,128)(2,1)S(1)}, u32[]{:S(2)}, u32[]{:S(2)}) collective-permute-start(bf16[2,32,192]{2,1,0:T(8,128)(2,1)} %get-tuple-element.175), channel_id=1, source_target_pairs={{0,18},{1,19},{2,16},{3,17},{4,22},{5,23},{6,20},{7,21},{8,26},{9,... | collective-permute-start | bytes 73736 | tf_op jit(solution)/shard_map/ppermute | solution.py:802
  181.2 7.0 %collective-permute-start.26 = (bf16[2,32,192]{2,1,0:T(8,128)(2,1)}, bf16[2,32,192]{2,1,0:T(8,128)(2,1)S(1)}, u32[]{:S(2)}, u32[]{:S(2)}) collective-permute-start(bf16[2,32,192]{2,1,0:T(8,128)(2,1)} %get-tuple-element.176), channel_id=1, source_target_pairs={{0,3},{1,2},{2,1},{3,0},{4,7},{5,6},{6,5},{7,4},{8,11},{9,10},{10,... | collective-permute-start | bytes 73736 | tf_op jit(solution)/shard_map/ppermute | solution.py:802
  183.9 4.8 %collective-permute-start.27 = (bf16[2,32,192]{2,1,0:T(8,128)(2,1)}, bf16[2,32,192]{2,1,0:T(8,128)(2,1)S(1)}, u32[]{:S(2)}, u32[]{:S(2)}) collective-permute-start(bf16[2,32,192]{2,1,0:T(8,128)(2,1)} %get-tuple-element.177), channel_id=1, source_target_pairs={{0,19},{1,18},{2,17},{3,16},{4,23},{5,22},{6,21},{7,20},{8,27},{9,... | collective-permute-start | bytes 73736 | tf_op jit(solution)/shard_map/ppermute | solution.py:802
  188.7 22.1 %all-to-all-start.4 = ((bf16[16,24,768]{2,1,0:T(8,128)(2,1)}), bf16[16,24,768]{2,1,0:T(8,128)(2,1)S(1)}, u32[]{:S(2)}, u32[]{:S(2)}) async-start(bf16[16,24,768]{2,1,0:T(8,128)(2,1)} %out_grad.1), calls=%async_computation.4 | async-start | bytes 1179648 | tf_op jit(solution)/shard_map/all_to_all | solution.py:749
  194.1 11.4 %copy-start.2 = (bf16[1536,768]{1,0:T(8,128)(2,1)S(1)}, bf16[1536,768]{1,0:T(8,128)(2,1)}, u32[]{:S(2)}) copy-start(bf16[1536,768]{1,0:T(8,128)(2,1)} %convolution_convert_fusion) | copy-start | bytes 7077892
  194.2 57.5 %collective-permute-start.37 = (bf16[768,1536]{1,0:T(8,128)(2,1)S(1)}, bf16[768,1536]{1,0:T(8,128)(2,1)}, u32[]{:S(2)}, u32[]{:S(2)}) collective-permute-start(bf16[768,1536]{1,0:T(8,128)(2,1)S(1)} %convolution_convert_fusion.1), channel_id=1, source_target_pairs={{0,16},{16,0},{1,17},{17,1},{2,18},{18,2},{3,19},{19,3},{4,20},{20... | collective-permute-start | bytes 7077896 | tf_op jit(solution)/shard_map/ppermute | solution.py:792
  210.7 3.2 %collective-permute-start.31 = (bf16[16,64,576]{2,1,0:T(8,128)(2,1)}, bf16[16,64,576]{2,1,0:T(8,128)(2,1)S(1)}, u32[]{:S(2)}, u32[]{:S(2)}) collective-permute-start(bf16[16,64,576]{2,1,0:T(8,128)(2,1)} %get-tuple-element.191.d_own_ref), channel_id=1, source_target_pairs={{0,16},{16,0},{1,17},{17,1},{2,18},{18,2},{3,19},{19,3},{4,20},{20... | collective-permute-start | bytes 3538952 | tf_op jit(solution)/shard_map/ppermute | solution.py:792
  210.7 18.8 %collective-permute-start.32 = (bf16[64,768]{1,0:T(8,128)(2,1)S(1)}, bf16[64,768]{1,0:T(8,128)(2,1)S(1)}, u32[]{:S(2)}, u32[]{:S(2)}) collective-permute-start(bf16[64,768]{1,0:T(8,128)(2,1)S(1)} %copy-done.33), channel_id=1, source_target_pairs={{0,0},{1,1},{2,2},{3,3},{4,4},{5,5},{6,6},{7,7},{16,8},{17,9},{18,... | collective-permute-start | bytes 294920 | tf_op jit(solution)/shard_map/ppermute | solution.py:816
  211.4 18.1 %collective-permute-start.33 = (bf16[64,768]{1,0:T(8,128)(2,1)S(1)}, bf16[64,768]{1,0:T(8,128)(2,1)S(1)}, u32[]{:S(2)}, u32[]{:S(2)}) collective-permute-start(bf16[64,768]{1,0:T(8,128)(2,1)S(1)} %copy-done.32), channel_id=1, source_target_pairs={{4,0},{5,1},{6,2},{7,3},{0,4},{1,5},{2,6},{3,7},{20,8},{21,9},{22,... | collective-permute-start | bytes 294920 | tf_op jit(solution)/shard_map/ppermute | solution.py:816
  220.9 15.4 %all-to-all-start.5 = ((bf16[4,4,32,768]{3,2,1,0:T(8,128)(2,1)}), bf16[4,4,32,768]{3,2,1,0:T(8,128)(2,1)}, u32[]{:S(2)}, u32[]{:S(2)}) async-start(bf16[4,4,32,768]{3,2,1,0:T(8,128)(2,1)} %get-tuple-element.200), calls=%async_computation.5 | async-start | bytes 1572864 | tf_op jit(solution)/shard_map/all_to_all | solution.py:1136
  229.5 18.6 %copy-start.34 = (bf16[64,768]{1,0:T(8,128)(2,1)}, bf16[64,768]{1,0:T(8,128)(2,1)S(1)}, u32[]{:S(2)}) copy-start(bf16[64,768]{1,0:T(8,128)(2,1)S(1)} %collective-permute-done.32.out_first_ref) | copy-start | bytes 294916
  229.6 18.6 %copy-start.35 = (bf16[64,768]{1,0:T(8,128)(2,1)}, bf16[64,768]{1,0:T(8,128)(2,1)S(1)}, u32[]{:S(2)}) copy-start(bf16[64,768]{1,0:T(8,128)(2,1)S(1)} %collective-permute-done.33.out_second_ref) | copy-start | bytes 294916
  236.3 22.4 %all-to-all-start.6 = ((bf16[16,24,768]{2,1,0:T(8,128)(2,1)}), bf16[16,24,768]{2,1,0:T(8,128)(2,1)}, u32[]{:S(2)}, u32[]{:S(2)}) async-start(bf16[16,24,768]{2,1,0:T(8,128)(2,1)} %weight_grads.1), calls=%async_computation.6 | async-start | bytes 1179648 | tf_op jit(solution)/shard_map/all_to_all | solution.py:749
  243.9 1.5 collective-permute-start.34
  248.2 8.0 %collective-permute-start.35 = (bf16[64,768]{1,0:T(8,128)(2,1)}, bf16[64,768]{1,0:T(8,128)(2,1)S(1)}, u32[]{:S(2)}, u32[]{:S(2)}) collective-permute-start(bf16[64,768]{1,0:T(8,128)(2,1)} %get-tuple-element.208), channel_id=1, source_target_pairs={{0,0},{1,1},{2,2},{3,3},{4,4},{5,5},{6,6},{7,7},{16,8},{17,9},{18,... | collective-permute-start | bytes 294920 | tf_op jit(solution)/shard_map/ppermute | solution.py:816
  249.7 6.4 %collective-permute-start.36 = (bf16[64,768]{1,0:T(8,128)(2,1)}, bf16[64,768]{1,0:T(8,128)(2,1)S(1)}, u32[]{:S(2)}, u32[]{:S(2)}) collective-permute-start(bf16[64,768]{1,0:T(8,128)(2,1)} %get-tuple-element.209), channel_id=1, source_target_pairs={{4,0},{5,1},{6,2},{7,3},{0,4},{1,5},{2,6},{3,7},{20,8},{21,9},{22,... | collective-permute-start | bytes 294920 | tf_op jit(solution)/shard_map/ppermute | solution.py:816
  260.6 3.7 %collective-permute-start.38 = (bf16[3,24,768]{2,1,0:T(8,128)(2,1)}, bf16[3,24,768]{2,1,0:T(8,128)(2,1)S(1)}, u32[]{:S(2)}, u32[]{:S(2)}) collective-permute-start(bf16[3,24,768]{2,1,0:T(8,128)(2,1)} %get-tuple-element.217), channel_id=1, source_target_pairs={{0,16},{16,0},{1,17},{17,1},{2,18},{18,2},{3,19},{19,3},{4,20},{20... | collective-permute-start | bytes 331784 | tf_op jit(solution)/shard_map/ppermute | solution.py:792
  262.7 1.3 collective-permute-start.39
  262.8 1.6 collective-permute-start.40
  (34 other events, 111.5 us)
